TPU v7x, 32 devices: a whole 2x2x4 slice. The times are simulated.
32 devices in a mesh: dp: 16 (over z, y, x), fsdp: 2 (over core).
Axes of the slice: x: 2, y: 2, z: 4, core: 2. Of those that a mesh axis runs over, the one named last changes fastest.
Arguments:
- latents: bfloat16 [256, 128, 768], P(('dp', 'fsdp')), may hold values from -6 to 6
- inputs: bfloat16 [256, 296, 768], P(('dp', 'fsdp')), may hold values from -6 to 6
- frame_counts: int32 [256], P(('dp', 'fsdp')), may hold values from 4 to 16, as said below
- patch_mask: int32 [256, 256], P(('dp', 'fsdp')), may hold values 0 or 1
- text_mask: int32 [256, 40], P(('dp', 'fsdp')), may hold values 0 or 1
- drop_mask: int32 [256], P(('dp', 'fsdp')), may hold values 0 or 1
- cross_gains: bfloat16 [3, 768], P(None, ('dp', 'fsdp')), may hold values from 0.25 to 1.75
- cross_shifts: bfloat16 [3, 768], P(None, ('dp', 'fsdp')), may hold values from -1.75 to 1.75
- cross_qkv: bfloat16 [3, 768, 768], P(None, ('dp', 'fsdp')), may hold values from -0.21875 to 0.21875
- cross_out: bfloat16 [768, 768], P(('dp', 'fsdp')), may hold values from -0.75 to 0.75
- cross_up: bfloat16 [768, 3072], P(('dp', 'fsdp')), may hold values from -0.21875 to 0.21875
- cross_down: bfloat16 [3072, 768], P(('dp', 'fsdp')), may hold values from -0.109375 to 0.109375
- self_gains: bfloat16 [2, 768], P(None, ('dp', 'fsdp')), may hold values from 0.25 to 1.75
- self_shifts: bfloat16 [2, 768], P(None, ('dp', 'fsdp')), may hold values from -1.75 to 1.75
- self_qkv: bfloat16 [3, 768, 768], P(None, ('dp', 'fsdp')), may hold values from -0.21875 to 0.21875
- self_out: bfloat16 [768, 768], P(('dp', 'fsdp')), may hold values from -0.75 to 0.75
- self_up: bfloat16 [768, 3072], P(('dp', 'fsdp')), may hold values from -0.21875 to 0.21875
- self_down: bfloat16 [3072, 768], P(('dp', 'fsdp')), may hold values from -0.109375 to 0.109375
- cotangent: bfloat16 [256, 128, 768], P(('dp', 'fsdp')), may hold values from -6 to 6
Outputs:
- latents_out: bfloat16 [256, 128, 768], P(('dp', 'fsdp'))
- latents_grad: float32 [256, 128, 768], P(('dp', 'fsdp'))
- inputs_grad: float32 [256, 296, 768], P(('dp', 'fsdp'))
- cross_gains_grad: float32 [3, 768], P(None, ('dp', 'fsdp'))
- cross_shifts_grad: float32 [3, 768], P(None, ('dp', 'fsdp'))
- cross_qkv_grad: float32 [3, 768, 768], P(None, ('dp', 'fsdp'))
- cross_out_grad: float32 [768, 768], P(('dp', 'fsdp'))
- cross_up_grad: float32 [768, 3072], P(('dp', 'fsdp'))
- cross_down_grad: float32 [3072, 768], P(('dp', 'fsdp'))
- self_gains_grad: float32 [2, 768], P(None, ('dp', 'fsdp'))
- self_shifts_grad: float32 [2, 768], P(None, ('dp', 'fsdp'))
- self_qkv_grad: float32 [3, 768, 768], P(None, ('dp', 'fsdp'))
- self_out_grad: float32 [768, 768], P(('dp', 'fsdp'))
- self_up_grad: float32 [768, 3072], P(('dp', 'fsdp'))
- self_down_grad: float32 [3072, 768], P(('dp', 'fsdp'))
Inputs may be any that keep to these rules, and one draw needn't show every extreme that they name: `frame_counts`: some clip has exactly 16 frames and some exactly 4.
All inputs are finite; a program needn't handle non-finite values. No bound on the sum of `patch_mask` or of `text_mask` or of `drop_mask` on one device may be relied on, other than what follows from the above.
Results may differ from a plain program's by a relative error of at most 0.015.
Values may be sent and summed in bfloat16 or wider, within the bound.
No kernel may reach another device: no remote copies, remote signals or barrier semaphores. Data moves between devices by JAX's collectives and lax.ppermute only.
A program may use at most 320 MiB of HBM per device.

v0:
```python
import jax
import jax.numpy as jnp
from jax import lax
from jax.sharding import PartitionSpec as P

HEADS = 12
HEAD_DIM = 64
P_SIZE = 16
TEXT = 40
VIDEO = 256


def normalize(value, gain, shift):
    row_mean = jnp.mean(value, axis=-1, keepdims=True)
    centered = value - row_mean
    variance = jnp.mean(centered * centered, axis=-1, keepdims=True)
    return centered * lax.rsqrt(variance + 1e-05) * gain + shift


def key_valid(frame_counts, patch_mask, text_mask):
    places = jnp.arange(VIDEO, dtype=jnp.int32)
    video_ok = (places[None, :] // P_SIZE < frame_counts[:, None]) & (
        (patch_mask == 1) | (places[None, :] % P_SIZE == 0)
    )
    text_places = jnp.arange(TEXT, dtype=jnp.int32)
    text_ok = (text_mask == 1) | (text_places[None, :] == 0)
    return jnp.concatenate([video_ok, text_ok], axis=1)


def project(left, weight):
    return jnp.einsum("bld,de->ble", left, weight, preferred_element_type=jnp.float32)


def project_back(left, weight):
    return jnp.einsum("ble,de->bld", left, weight, preferred_element_type=jnp.float32)


def outer_sum(left, right):
    return jnp.einsum("bld,ble->de", left, right, preferred_element_type=jnp.float32)


def split_heads(value):
    return value.reshape(value.shape[0], value.shape[1], HEADS, HEAD_DIM)


def scores_of(queries, key_rows, usable):
    scores = jnp.einsum(
        "blhe,bshe->bhls",
        split_heads(queries),
        split_heads(key_rows),
        preferred_element_type=jnp.float32,
    ) * HEAD_DIM ** (-0.5)
    if usable is not None:
        scores = jnp.where(usable[:, None, None, :], scores, -1e30)
    return scores


def block_forward(latent, features, usable, keeping, weights):
    gain_rows, shift_rows, qkv, w_out, w_up, w_down = weights
    gain_rows = gain_rows.astype(jnp.float32)
    shift_rows = shift_rows.astype(jnp.float32)
    latent_low = normalize(latent, gain_rows[0], shift_rows[0]).astype(jnp.bfloat16)
    if features is None:
        feature_low = latent_low
        second = 1
    else:
        feature_low = normalize(features, gain_rows[1], shift_rows[1]).astype(jnp.bfloat16)
        second = 2
    queries = project(latent_low, qkv[0]).astype(jnp.bfloat16)
    key_rows = project(feature_low, qkv[1]).astype(jnp.bfloat16)
    value_rows = project(feature_low, qkv[2]).astype(jnp.bfloat16)
    scores = scores_of(queries, key_rows, usable)
    row_max = jnp.max(scores, axis=-1, keepdims=True)
    expo = jnp.exp(scores - row_max)
    denominator = jnp.sum(expo, axis=-1, keepdims=True)
    weights_soft = expo / denominator
    log_total = (row_max + jnp.log(denominator))[..., 0]
    merged = jnp.einsum(
        "bhls,bshe->blhe",
        weights_soft.astype(jnp.bfloat16),
        split_heads(value_rows),
        preferred_element_type=jnp.float32,
    )
    attended = merged.reshape(latent.shape).astype(jnp.bfloat16)
    branch = project(attended, w_out)
    residual = latent + branch
    hidden = normalize(residual, gain_rows[second], shift_rows[second]).astype(jnp.bfloat16)
    pre_act = project(hidden, w_up)
    activated = jax.nn.gelu(pre_act).astype(jnp.bfloat16)
    out_branch = project(activated, w_down)
    if keeping is None:
        result = latent + (branch + out_branch)
    else:
        result = latent + keeping[:, None, None] * (branch + out_branch)
    saved = (
        latent_low,
        feature_low,
        queries,
        key_rows,
        value_rows,
        log_total,
        attended,
        residual,
        hidden,
        pre_act,
        activated,
    )
    return (result, saved)


def block_backward(upstream, latent, features, usable, keeping, weights, saved):
    gain_rows, shift_rows, qkv, w_out, w_up, w_down = weights
    gain_rows = gain_rows.astype(jnp.float32)
    shift_rows = shift_rows.astype(jnp.float32)
    (
        latent_low,
        feature_low,
        queries,
        key_rows,
        value_rows,
        log_total,
        attended,
        residual,
        hidden,
        pre_act,
        activated,
    ) = saved
    second = 1 if features is None else 2
    direct = upstream if keeping is None else upstream * keeping[:, None, None]
    out_low = direct.astype(jnp.bfloat16)
    grad_down = outer_sum(activated, out_low)
    d_activated = project_back(out_low, w_down)
    gelu_value, gelu_back = jax.vjp(jax.nn.gelu, pre_act)
    d_pre = gelu_back(d_activated)[0].astype(jnp.bfloat16)
    grad_up = outer_sum(hidden, d_pre)
    d_hidden = project_back(d_pre, w_up)
    norm_value, mid_back = jax.vjp(normalize, residual, gain_rows[second], shift_rows[second])
    d_residual, gain_mid, shift_mid = mid_back(d_hidden)
    d_branch = (direct + d_residual).astype(jnp.bfloat16)
    grad_out = outer_sum(attended, d_branch)
    d_attended = split_heads(project_back(d_branch, w_out).astype(jnp.bfloat16))
    scores = scores_of(queries, key_rows, usable)
    weights_soft = jnp.exp(scores - log_total[..., None])
    d_values = jnp.einsum(
        "bhls,blhe->bshe",
        weights_soft.astype(jnp.bfloat16),
        d_attended,
        preferred_element_type=jnp.float32,
    )
    d_values = d_values.reshape(value_rows.shape).astype(jnp.bfloat16)
    d_soft = jnp.einsum(
        "blhe,bshe->bhls", d_attended, split_heads(value_rows), preferred_element_type=jnp.float32
    )
    d_scores = (
        weights_soft * (d_soft - jnp.sum(d_soft * weights_soft, axis=-1, keepdims=True))
    ).astype(jnp.bfloat16)
    score_scale = HEAD_DIM ** (-0.5)
    d_queries = (
        jnp.einsum(
            "bhls,bshe->blhe", d_scores, split_heads(key_rows), preferred_element_type=jnp.float32
        )
        * score_scale
    )
    d_queries = d_queries.reshape(queries.shape).astype(jnp.bfloat16)
    d_keys = (
        jnp.einsum(
            "bhls,blhe->bshe", d_scores, split_heads(queries), preferred_element_type=jnp.float32
        )
        * score_scale
    )
    d_keys = d_keys.reshape(key_rows.shape).astype(jnp.bfloat16)
    grad_qkv = jnp.stack(
        [
            outer_sum(latent_low, d_queries),
            outer_sum(feature_low, d_keys),
            outer_sum(feature_low, d_values),
        ]
    )
    d_latent_low = project_back(d_queries, qkv[0])
    d_feature_low = project_back(d_keys, qkv[1]) + project_back(d_values, qkv[2])
    if features is None:
        d_latent_low = d_latent_low + d_feature_low
    first_value, first_back = jax.vjp(normalize, latent, gain_rows[0], shift_rows[0])
    d_latent, gain_first, shift_first = first_back(d_latent_low)
    d_latent = d_latent + d_residual + upstream
    if features is None:
        d_features = None
        grad_gains = jnp.stack([gain_first, gain_mid])
        grad_shifts = jnp.stack([shift_first, shift_mid])
    else:
        input_value, input_back = jax.vjp(normalize, features, gain_rows[1], shift_rows[1])
        d_features, gain_input, shift_input = input_back(d_feature_low)
        grad_gains = jnp.stack([gain_first, gain_input, gain_mid])
        grad_shifts = jnp.stack([shift_first, shift_input, shift_mid])
    return (d_latent, d_features, (grad_gains, grad_shifts, grad_qkv, grad_out, grad_up, grad_down))


def local(
    latents,
    inputs,
    frame_counts,
    patch_mask,
    text_mask,
    drop_mask,
    cross_gains,
    cross_shifts,
    cross_qkv,
    cross_out,
    cross_up,
    cross_down,
    self_gains,
    self_shifts,
    self_qkv,
    self_out,
    self_up,
    self_down,
    cotangent,
):
    usable = key_valid(frame_counts, patch_mask, text_mask)
    keeping = (1 - drop_mask).astype(jnp.float32)
    latent_in = latents.astype(jnp.float32)
    features_in = inputs.astype(jnp.float32)
    cross_full = (
        lax.all_gather(cross_gains, ("dp", "fsdp"), axis=1, tiled=True),
        lax.all_gather(cross_shifts, ("dp", "fsdp"), axis=1, tiled=True),
        lax.all_gather(cross_qkv, ("dp", "fsdp"), axis=1, tiled=True),
        lax.all_gather(cross_out, ("dp", "fsdp"), axis=0, tiled=True),
        lax.all_gather(cross_up, ("dp", "fsdp"), axis=0, tiled=True),
        lax.all_gather(cross_down, ("dp", "fsdp"), axis=0, tiled=True),
    )
    middle, cross_saved = block_forward(latent_in, features_in, usable, keeping, cross_full)
    self_full = (
        lax.all_gather(self_gains, ("dp", "fsdp"), axis=1, tiled=True),
        lax.all_gather(self_shifts, ("dp", "fsdp"), axis=1, tiled=True),
        lax.all_gather(self_qkv, ("dp", "fsdp"), axis=1, tiled=True),
        lax.all_gather(self_out, ("dp", "fsdp"), axis=0, tiled=True),
        lax.all_gather(self_up, ("dp", "fsdp"), axis=0, tiled=True),
        lax.all_gather(self_down, ("dp", "fsdp"), axis=0, tiled=True),
    )
    result, self_saved = block_forward(middle, None, None, None, self_full)
    upstream = cotangent.astype(jnp.float32)
    self_back = (
        lax.all_gather(self_gains, ("dp", "fsdp"), axis=1, tiled=True),
        lax.all_gather(self_shifts, ("dp", "fsdp"), axis=1, tiled=True),
        lax.all_gather(self_qkv, ("dp", "fsdp"), axis=1, tiled=True),
        lax.all_gather(self_out, ("dp", "fsdp"), axis=0, tiled=True),
        lax.all_gather(self_up, ("dp", "fsdp"), axis=0, tiled=True),
        lax.all_gather(self_down, ("dp", "fsdp"), axis=0, tiled=True),
    )
    d_middle, unused_features, self_terms = block_backward(
        upstream, middle, None, None, None, self_back, self_saved
    )
    self_parts = (
        lax.psum_scatter(self_terms[0], ("dp", "fsdp"), scatter_dimension=1, tiled=True),
        lax.psum_scatter(self_terms[1], ("dp", "fsdp"), scatter_dimension=1, tiled=True),
        lax.psum_scatter(self_terms[2], ("dp", "fsdp"), scatter_dimension=1, tiled=True),
        lax.psum_scatter(self_terms[3], ("dp", "fsdp"), scatter_dimension=0, tiled=True),
        lax.psum_scatter(self_terms[4], ("dp", "fsdp"), scatter_dimension=0, tiled=True),
        lax.psum_scatter(self_terms[5], ("dp", "fsdp"), scatter_dimension=0, tiled=True),
    )
    cross_back = (
        lax.all_gather(cross_gains, ("dp", "fsdp"), axis=1, tiled=True),
        lax.all_gather(cross_shifts, ("dp", "fsdp"), axis=1, tiled=True),
        lax.all_gather(cross_qkv, ("dp", "fsdp"), axis=1, tiled=True),
        lax.all_gather(cross_out, ("dp", "fsdp"), axis=0, tiled=True),
        lax.all_gather(cross_up, ("dp", "fsdp"), axis=0, tiled=True),
        lax.all_gather(cross_down, ("dp", "fsdp"), axis=0, tiled=True),
    )
    d_latent, d_features, cross_terms = block_backward(
        d_middle, latent_in, features_in, usable, keeping, cross_back, cross_saved
    )
    cross_parts = (
        lax.psum_scatter(cross_terms[0], ("dp", "fsdp"), scatter_dimension=1, tiled=True),
        lax.psum_scatter(cross_terms[1], ("dp", "fsdp"), scatter_dimension=1, tiled=True),
        lax.psum_scatter(cross_terms[2], ("dp", "fsdp"), scatter_dimension=1, tiled=True),
        lax.psum_scatter(cross_terms[3], ("dp", "fsdp"), scatter_dimension=0, tiled=True),
        lax.psum_scatter(cross_terms[4], ("dp", "fsdp"), scatter_dimension=0, tiled=True),
        lax.psum_scatter(cross_terms[5], ("dp", "fsdp"), scatter_dimension=0, tiled=True),
    )
    return (
        result.astype(jnp.bfloat16),
        d_latent,
        d_features,
        cross_parts[0],
        cross_parts[1],
        cross_parts[2],
        cross_parts[3],
        cross_parts[4],
        cross_parts[5],
        self_parts[0],
        self_parts[1],
        self_parts[2],
        self_parts[3],
        self_parts[4],
        self_parts[5],
    )


def solution(mesh):
    in_specs = (
        P(("dp", "fsdp"), None, None),
        P(("dp", "fsdp"), None, None),
        P(("dp", "fsdp")),
        P(("dp", "fsdp"), None),
        P(("dp", "fsdp"), None),
        P(("dp", "fsdp")),
        P(None, ("dp", "fsdp")),
        P(None, ("dp", "fsdp")),
        P(None, ("dp", "fsdp"), None),
        P(("dp", "fsdp"), None),
        P(("dp", "fsdp"), None),
        P(("dp", "fsdp"), None),
        P(None, ("dp", "fsdp")),
        P(None, ("dp", "fsdp")),
        P(None, ("dp", "fsdp"), None),
        P(("dp", "fsdp"), None),
        P(("dp", "fsdp"), None),
        P(("dp", "fsdp"), None),
        P(("dp", "fsdp"), None, None),
    )
    out_specs = (
        P(("dp", "fsdp"), None, None),
        P(("dp", "fsdp"), None, None),
        P(("dp", "fsdp"), None, None),
        P(None, ("dp", "fsdp")),
        P(None, ("dp", "fsdp")),
        P(None, ("dp", "fsdp"), None),
        P(("dp", "fsdp"), None),
        P(("dp", "fsdp"), None),
        P(("dp", "fsdp"), None),
        P(None, ("dp", "fsdp")),
        P(None, ("dp", "fsdp")),
        P(None, ("dp", "fsdp"), None),
        P(("dp", "fsdp"), None),
        P(("dp", "fsdp"), None),
        P(("dp", "fsdp"), None),
    )
    return jax.shard_map(local, mesh=mesh, in_specs=in_specs, out_specs=out_specs, check_vma=False)
```

profile of v0, /device:TPU:0, one launch (start us, length us, event | category | flops | bytes accessed | tf_op | source)
XLA Modules:
  0.0 1648.3 jit_solution(1496844735077151264)
XLA Ops:
  12.7 43.6 %all-gather.1 = bf16[32,24,3]{1,2,0:T(4,128)(2,1)S(1)} all-gather(bf16[1,24,3]{1,2,0:T(4,128)(2,1)} %bitcast.274), channel_id=1, replica_groups=mesh['dp'=16,'fsdp'=2] {'dp','fsdp'}, dimensions={0}, use_global_device_ids=true | all-gather | bytes 4752 | tf_op jit(solution)/shard_map/all_gather | solution.py:225
  56.6 36.9 %all-gather = bf16[32,24,3]{1,2,0:T(4,128)(2,1)S(1)} all-gather(bf16[1,24,3]{1,2,0:T(4,128)(2,1)} %bitcast.275), channel_id=1, replica_groups=mesh['dp'=16,'fsdp'=2] {'dp','fsdp'}, dimensions={0}, use_global_device_ids=true | all-gather | bytes 4752 | tf_op jit(solution)/shard_map/all_gather | solution.py:224
  99.2 37.8 %all-gather.3 = bf16[32,24,2]{1,2,0:T(2,128)(2,1)S(1)} all-gather(bf16[1,24,2]{1,2,0:T(2,128)(2,1)S(1)} %bitcast.276), channel_id=1, replica_groups=mesh['dp'=16,'fsdp'=2] {'dp','fsdp'}, dimensions={0}, use_global_device_ids=true | all-gather | bytes 3168 | tf_op jit(solution)/shard_map/all_gather | solution.py:234
  137.3 36.5 %all-gather.2 = bf16[32,24,2]{1,2,0:T(2,128)(2,1)S(1)} all-gather(bf16[1,24,2]{1,2,0:T(2,128)(2,1)S(1)} %bitcast.277), channel_id=1, replica_groups=mesh['dp'=16,'fsdp'=2] {'dp','fsdp'}, dimensions={0}, use_global_device_ids=true | all-gather | bytes 3168 | tf_op jit(solution)/shard_map/all_gather | solution.py:233
  246.6 11.1 fusion.50
  260.4 13.2 fusion.119
  275.9 46.3 %all-gather.21.cloned.1.call-done = bf16[3,768,768]{2,1,0:T(8,128)(2,1)} async-done(((bf16[3,24,768]{2,1,0:T(8,128)(2,1)}), bf16[3,768,768]{2,1,0:T(8,128)(2,1)}) %all-gather.21.cloned.1.call-update) | async-done | bytes 3538960 | tf_op jit(solution)/shard_map/all_gather | solution.py:235
  351.8 26.1 %all-gather.23.cloned.1.call-done = bf16[768,768]{1,0:T(8,128)(2,1)} async-done(((bf16[24,768]{1,0:T(8,128)(2,1)}), bf16[768,768]{1,0:T(8,128)(2,1)}) %all-gather.23.cloned.1.call-update) | async-done | bytes 1179664 | tf_op jit(solution)/shard_map/all_gather | solution.py:236
  385.0 58.3 %all-gather.25.cloned.1.call-done = bf16[768,3072]{1,0:T(8,128)(2,1)} async-done(((bf16[24,3072]{1,0:T(8,128)(2,1)}), bf16[768,3072]{1,0:T(8,128)(2,1)}) %all-gather.25.cloned.1.call-update) | async-done | bytes 4718608 | tf_op jit(solution)/shard_map/all_gather | solution.py:237
  443.3 11.1 fusion.42
  454.4 54.3 %all-gather.27.cloned.1.call-done = bf16[3072,768]{1,0:T(8,128)(2,1)} async-done(((bf16[96,768]{1,0:T(8,128)(2,1)}), bf16[3072,768]{1,0:T(8,128)(2,1)}) %all-gather.27.cloned.1.call-update) | async-done | bytes 4718608 | tf_op jit(solution)/shard_map/all_gather | solution.py:238
  508.7 15.9 fusion.14
  582.1 15.3 fusion.7
  622.3 16.4 multiply_reduce_fusion
  711.9 12.8 convolution_bitcast_fusion.2
  738.7 12.3 convolution_bitcast_fusion
  778.3 40.5 %all-reduce.4 = (f32[3,768]{1,0:T(4,128)S(1)}, f32[3,768]{1,0:T(4,128)S(1)}, f32[2,768]{1,0:T(2,128)S(1)}, f32[2,768]{1,0:T(2,128)S(1)}) all-reduce(f32[3,768]{1,0:T(4,128)S(1)} %pad_maximum_fusion.2, f32[3,768]{1,0:T(4,128)S(1)} %pad_maximum_fusion.3, ...), channel_id=2, replica_groups=mesh['dp'=16,'fsdp'=2] {'dp','fsdp'}, use_global_device_ids=true, to_apply=%region_29.30.clone | all-reduce | flops 7680 | bytes 61440
  836.6 11.4 add_convert_fusion.1
  848.1 101.3 %reduce-scatter.13.cloned.1.call-done = f32[3,24,768]{2,1,0:T(8,128)} async-done(((f32[3,768,768]{2,1,0:T(8,128)}), f32[3,24,768]{2,1,0:T(8,128)}) %reduce-scatter.13.cloned.1.call-update) | async-done | bytes 221200 | tf_op jit(solution)/shard_map/reduce_scatter | solution.py:275
  949.4 125.4 %reduce-scatter.21.cloned.1.call-done = f32[3,24,768]{2,1,0:T(8,128)} async-done(((f32[3,768,768]{2,1,0:T(8,128)}), f32[3,24,768]{2,1,0:T(8,128)}) %reduce-scatter.21.cloned.1.call-update) | async-done | bytes 221200 | tf_op jit(solution)/shard_map/reduce_scatter | solution.py:256
  1074.8 141.5 %reduce-scatter.17.cloned.1.call-done = f32[24,3072]{1,0:T(8,128)} async-done(((f32[768,3072]{1,0:T(8,128)}), f32[24,3072]{1,0:T(8,128)}) %reduce-scatter.17.cloned.1.call-update) | async-done | bytes 294928 | tf_op jit(solution)/shard_map/reduce_scatter | solution.py:277
  1216.4 142.0 %reduce-scatter.19.cloned.1.call-done = f32[96,768]{1,0:T(8,128)} async-done(((f32[3072,768]{1,0:T(8,128)}), f32[96,768]{1,0:T(8,128)}) %reduce-scatter.19.cloned.1.call-update) | async-done | bytes 294928 | tf_op jit(solution)/shard_map/reduce_scatter | solution.py:278
  1358.3 141.0 %reduce-scatter.25.cloned.1.call-done = f32[24,3072]{1,0:T(8,128)} async-done(((f32[768,3072]{1,0:T(8,128)}), f32[24,3072]{1,0:T(8,128)}) %reduce-scatter.25.cloned.1.call-update) | async-done | bytes 294928 | tf_op jit(solution)/shard_map/reduce_scatter | solution.py:258
  1499.3 142.0 %reduce-scatter.27.cloned.1.call-done = f32[96,768]{1,0:T(8,128)} async-done(((f32[3072,768]{1,0:T(8,128)}), f32[96,768]{1,0:T(8,128)}) %reduce-scatter.27.cloned.1.call-update) | async-done | bytes 294928 | tf_op jit(solution)/shard_map/reduce_scatter | solution.py:259
  (394 shorter events, 339.3 us)
Async XLA Ops:
  7.2 167.2 %all-gather.13.cloned.1.call-start = ((), (), s32[]{:S(2)}) async-start(), calls=%async_computation.8 | async-start | bytes 3649536 | tf_op jit(solution)/shard_map/all_gather | solution.py:226
  7.9 232.3 %all-gather.15.cloned.1.call-start = ((), (), s32[]{:S(2)}) async-start(), calls=%async_computation.9 | async-start | bytes 1216512 | tf_op jit(solution)/shard_map/all_gather | solution.py:227
  8.7 238.0 %all-gather.17.cloned.1.call-start = ((), (), s32[]{:S(2)}) async-start(), calls=%async_computation.10 | async-start | bytes 4866048 | tf_op jit(solution)/shard_map/all_gather | solution.py:228
  9.4 251.0 %all-gather.19.cloned.1.call-start = ((), (), s32[]{:S(2)}) async-start(), calls=%async_computation.11 | async-start | bytes 4866048 | tf_op jit(solution)/shard_map/all_gather | solution.py:229
  10.0 312.2 %all-gather.21.cloned.1.call-start = ((), (), s32[]{:S(2)}) async-start(), calls=%async_computation.12 | async-start | bytes 3649536 | tf_op jit(solution)/shard_map/all_gather | solution.py:235
  10.6 367.3 %all-gather.23.cloned.1.call-start = ((), (), s32[]{:S(2)}) async-start(), calls=%async_computation.13 | async-start | bytes 1216512 | tf_op jit(solution)/shard_map/all_gather | solution.py:236
  11.1 432.2 %all-gather.25.cloned.1.call-start = ((), (), s32[]{:S(2)}) async-start(), calls=%async_computation.14 | async-start | bytes 4866048 | tf_op jit(solution)/shard_map/all_gather | solution.py:237
  11.9 496.8 %all-gather.27.cloned.1.call-start = ((), (), s32[]{:S(2)}) async-start(), calls=%async_computation.15 | async-start | bytes 4866048 | tf_op jit(solution)/shard_map/all_gather | solution.py:238
  12.6 835.4 %reduce-scatter.15.cloned.1.call-start = ((), (), s32[]{:S(2)}) async-start(), calls=%async_computation.17 | async-start | bytes 2433024 | tf_op jit(solution)/shard_map/reduce_scatter | solution.py:276
  96.9 98.8 %copy-start.63 = (f32[8,296]{1,0:T(8,128)}, f32[8,296]{1,0:T(8,128)S(1)}, u32[]{:S(2)}) copy-start(f32[8,296]{1,0:T(8,128)S(1)} %broadcast_multiply_fusion) | copy-start | bytes 28420
  98.2 97.5 %copy-start.65 = (f32[8,296]{1,0:T(8,128)}, f32[8,296]{1,0:T(8,128)S(1)}, u32[]{:S(2)}) copy-start(f32[8,296]{1,0:T(8,128)S(1)} %fusion.97) | copy-start | bytes 28420
  98.5 91.1 %copy-start.69 = (f32[8,128]{1,0:T(8,128)}, f32[8,128]{1,0:T(8,128)S(1)}, u32[]{:S(2)}) copy-start(f32[8,128]{1,0:T(8,128)S(1)} %broadcast_multiply_fusion.4) | copy-start | bytes 12292
  137.2 306.1 %copy-start.59 = (f32[768]{0:T(1024)}, f32[768]{0:T(1024)S(1)}, u32[]{:S(2)}) copy-start(f32[768]{0:T(1024)S(1)} %get-tuple-element.41) | copy-start | bytes 9220
  174.1 361.5 %copy-start.54 = (f32[768]{0:T(1024)}, f32[768]{0:T(1024)S(1)}, u32[]{:S(2)}) copy-start(f32[768]{0:T(1024)S(1)} %get-tuple-element.39) | copy-start | bytes 9220
  273.7 306.7 %copy-start.1 = (f32[8,128,768]{2,1,0:T(8,128)}, f32[8,128,768]{2,1,0:T(8,128)S(1)}, u32[]{:S(2)}) copy-start(f32[8,128,768]{2,1,0:T(8,128)S(1)} %get-tuple-element.59) | copy-start | bytes 9437188
  382.8 152.7 %copy-start.52 = (f32[8,128]{1,0:T(8,128)}, f32[8,128]{1,0:T(8,128)S(1)}, u32[]{:S(2)}) copy-start(f32[8,128]{1,0:T(8,128)S(1)} %broadcast_multiply_fusion.1) | copy-start | bytes 12292
  385.0 150.6 %copy-start.56 = (f32[8,128]{1,0:T(8,128)}, f32[8,128]{1,0:T(8,128)S(1)}, u32[]{:S(2)}) copy-start(f32[8,128]{1,0:T(8,128)S(1)} %fusion.101) | copy-start | bytes 12292
  622.2 225.8 %reduce-scatter.23.cloned.1.call-start = ((), (), s32[]{:S(2)}) async-start(), calls=%async_computation.21 | async-start | bytes 2433024 | tf_op jit(solution)/shard_map/reduce_scatter | solution.py:257
  667.5 281.9 %reduce-scatter.13.cloned.1.call-start = ((), (), s32[]{:S(2)}) async-start(), calls=%async_computation.16 | async-start | bytes 7299072 | tf_op jit(solution)/shard_map/reduce_scatter | solution.py:275
  688.8 386.0 %reduce-scatter.21.cloned.1.call-start = ((), (), s32[]{:S(2)}) async-start(), calls=%async_computation.20 | async-start | bytes 7299072 | tf_op jit(solution)/shard_map/reduce_scatter | solution.py:256
  698.8 517.6 %reduce-scatter.17.cloned.1.call-start = ((), (), s32[]{:S(2)}) async-start(), calls=%async_computation.18 | async-start | bytes 9732096 | tf_op jit(solution)/shard_map/reduce_scatter | solution.py:277
  710.1 648.3 %reduce-scatter.19.cloned.1.call-start = ((), (), s32[]{:S(2)}) async-start(), calls=%async_computation.19 | async-start | bytes 9732096 | tf_op jit(solution)/shard_map/reduce_scatter | solution.py:278
  724.8 774.5 %reduce-scatter.25.cloned.1.call-start = ((), (), s32[]{:S(2)}) async-start(), calls=%async_computation.22 | async-start | bytes 9732096 | tf_op jit(solution)/shard_map/reduce_scatter | solution.py:258
  737.3 904.0 %reduce-scatter.27.cloned.1.call-start = ((), (), s32[]{:S(2)}) async-start(), calls=%async_computation.23 | async-start | bytes 9732096 | tf_op jit(solution)/shard_map/reduce_scatter | solution.py:259
  (101 other events, 1199.2 us)
Sparse Core Ops, SparseCore 0:
  11.0 62.8 all-gather.12
  76.8 52.8 all-gather.14
  132.6 62.6 all-gather.16
  198.0 62.4 all-gather.18
  263.2 58.9 all-gather.20
  325.0 52.8 all-gather.22
  380.7 62.5 all-gather.24
  446.2 62.4 all-gather.26
  622.3 97.8 reduce-scatter.14
  726.8 97.9 reduce-scatter.22
  831.1 118.2 reduce-scatter.12
  956.5 118.3 reduce-scatter.20
  1081.3 135.0 reduce-scatter.16
  1223.7 134.5 reduce-scatter.18
  1364.7 134.6 reduce-scatter.24
  1506.6 134.5 reduce-scatter.26
where the time goes:
time: 1660 us; the launch traced here: 1650 us
  waiting for transfers between devices  986 us (59%)
  matrix products  329 us (20%)
  blocking collectives  195 us (12%)
  other arithmetic  70.1 us (4%)
  local copies, waits for them, and re-layouts  50 us (3%)
    reduce_scatter x1, waiting for transfers between devices, local(): lax.psum_scatter(cross_terms[5], ('dp', 'fsdp'), scatter_dimension=0, til...  142 us
    reduce_scatter x1, waiting for transfers between devices, local(): lax.psum_scatter(self_terms[5], ('dp', 'fsdp'), scatter_dimension=0, tile...  142 us
    reduce_scatter x1, waiting for transfers between devices, local(): lax.psum_scatter(cross_terms[4], ('dp', 'fsdp'), scatter_dimension=0, til...  142 us
    reduce_scatter x1, waiting for transfers between devices, local(): lax.psum_scatter(self_terms[4], ('dp', 'fsdp'), scatter_dimension=0, tile...  141 us
    reduce_scatter x1, waiting for transfers between devices, local(): lax.psum_scatter(self_terms[2], ('dp', 'fsdp'), scatter_dimension=1, tile...  125 us
    reduce_scatter x1, waiting for transfers between devices, local(): lax.psum_scatter(cross_terms[2], ('dp', 'fsdp'), scatter_dimension=1, til...  101 us
    dot_general x12, matrix products, project(): jnp.einsum('bld,de->ble', left, weight, preferred_element_type=jnp.float32)  92 us
    dot_general x12, matrix products, project_back(): jnp.einsum('ble,de->bld', left, weight, preferred_element_type=jnp.float32)  87.1 us
  transfers between devices with their start and end apart: 16, of which 11 were waited for; matrix products, arithmetic and copies ran while one was open for 20% of the time, Pallas kernels for 0%

commit v1 on v0

--- a/solution.py
+++ b/solution.py
@@ -1,3 +1,5 @@
+import functools
+
 import jax
 import jax.numpy as jnp
 from jax import lax
@@ -195,7 +197,198 @@
     return (d_latent, d_features, (grad_gains, grad_shifts, grad_qkv, grad_out, grad_up, grad_down))
 
 
+AX = ("dp", "fsdp")
+HALF = 384
+
+
+class Grid:
+    def __init__(self):
+        self.core = lax.axis_index("fsdp")
+        self.place = lax.rem(lax.axis_index("dp"), 4)
+        chips = range(16)
+        self.to_core = [(2 * i + c, 2 * i + 1 - c) for i in chips for c in range(2)]
+        self.to_x = [(2 * i + c, 2 * (i ^ 1) + c) for i in chips for c in range(2)]
+        self.to_y = [(2 * i + c, 2 * (i ^ 2) + c) for i in chips for c in range(2)]
+        self.columns = [[4 * z + i for z in range(4)] for i in range(4)]
+
+    def swap_core(self, value):
+        return lax.ppermute(value, AX, self.to_core)
+
+    def swap_x(self, value):
+        return lax.ppermute(value, AX, self.to_x)
+
+    def swap_y(self, value):
+        return lax.ppermute(value, AX, self.to_y)
+
+    def by_core(self, first, second):
+        return jnp.where(self.core == 0, first, second)
+
+    def halves(self, value):
+        left, right = (value[..., :HALF], value[..., HALF:])
+        return (self.by_core(left, right), self.by_core(right, left))
+
+    def gather(self, unit):
+        own = lax.all_gather(unit, "dp", axis=0, axis_index_groups=self.columns)
+        middle = unit.shape[0] // 2
+        from_x = self.swap_x(own)
+        from_y = self.swap_y(own)
+        first = self.swap_x(from_y[:, :middle])
+        second = self.swap_y(from_x[:, middle:])
+        mine = (own, from_x, from_y, jnp.concatenate([first, second], axis=1))
+        other = tuple((self.swap_core(piece) for piece in mine))
+        return (mine, other)
+
+    def assemble(self, mine, other):
+        whole = [
+            jnp.concatenate([self.by_core(a, b), self.by_core(b, a)], axis=-1)
+            for a, b in zip(mine, other)
+        ]
+        odd = lax.rem(self.place, 2) == 1
+        low = self.place >= 2
+        swapped = [jnp.where(odd, whole[i ^ 1], whole[i]) for i in range(4)]
+        placed = [jnp.where(low, swapped[i ^ 2], swapped[i]) for i in range(4)]
+        return jnp.stack(placed, axis=1)
+
+    def reduce(self, terms):
+        keep, send = self.halves(terms)
+        relative = [lax.dynamic_index_in_dim(keep, self.place ^ i, 1, False) for i in range(4)]
+        leaving = jnp.stack(
+            [lax.dynamic_index_in_dim(send, self.place ^ i, 1, False) for i in range(4)]
+        )
+        arrived = self.swap_core(leaving)
+        middle = terms.shape[2] // 2
+        sums = [relative[i] + arrived[i] for i in range(4)]
+        first = self.swap_x(sums[3][:, :middle])
+        second = self.swap_y(sums[3][:, middle:])
+        for_x = jnp.concatenate([sums[1][:, :middle], sums[1][:, middle:] + second], axis=1)
+        for_y = jnp.concatenate([sums[2][:, :middle] + first, sums[2][:, middle:]], axis=1)
+        own = sums[0] + self.swap_x(for_x) + self.swap_y(for_y)
+        return lax.psum_scatter(own, "dp", scatter_dimension=0, axis_index_groups=self.columns)
+
+
+def pack_rows(grid, mine, theirs, axis):
+    return jnp.concatenate([grid.by_core(mine, theirs), grid.by_core(theirs, mine)], axis=axis)
+
+
+def shard_of_block(qkv, w_out, w_up, w_down):
+    depth = w_out.shape[0]
+    attn = jnp.concatenate([qkv, w_out[None]], axis=0)
+    up = w_up.reshape(depth, 4, 768).transpose(1, 0, 2)
+    return jnp.concatenate([attn.reshape(-1, 768), up.reshape(-1, 768), w_down], axis=0)
+
+
+def units_of_block(grid, mine, theirs):
+    attn = pack_rows(grid, mine[:96].reshape(4, 24, HALF), theirs[:96].reshape(4, 24, HALF), 1)
+    up = pack_rows(grid, mine[96:192].reshape(4, 24, HALF), theirs[96:192].reshape(4, 24, HALF), 1)
+    down = pack_rows(grid, mine[192:], theirs[192:], 0)
+    return (attn.reshape(192, HALF), jnp.concatenate([up.reshape(192, HALF), down], axis=0))
+
+
+def square(part):
+    return part.reshape(768, 768)
+
+
+def attn_weights(full):
+    rows = [square(full[:, :, 48 * i : 48 * i + 48]) for i in range(4)]
+    return (jnp.stack(rows[:3]), rows[3])
+
+
+def mlp_weights(full):
+    up = jnp.concatenate([square(full[:, :, 48 * i : 48 * i + 48]) for i in range(4)], axis=1)
+    return (up, full[:, :, 192:].reshape(3072, 768))
+
+
+def attn_terms(qkv, w_out, extra):
+    parts = [qkv[i] for i in range(3)] + [w_out]
+    parts = [p.astype(jnp.bfloat16).reshape(4, 4, 48, 768) for p in parts]
+    extra = jnp.broadcast_to(extra.astype(jnp.bfloat16), (4, 4) + extra.shape)
+    return jnp.concatenate(parts + [extra], axis=2)
+
+
+def mlp_terms(w_up, w_down):
+    up = w_up.astype(jnp.bfloat16).reshape(4, 4, 48, 4, 768).transpose(0, 1, 3, 2, 4)
+    down = w_down.astype(jnp.bfloat16).reshape(4, 4, 192, 768)
+    return jnp.concatenate([up.reshape(4, 4, 192, 768), down], axis=2)
+
+
+def finish(grid, attn, mlp):
+    attn = attn.astype(jnp.float32)
+    mlp = mlp.astype(jnp.float32)
+    matrices = attn[:192].reshape(4, 2, 24, HALF)
+    up = mlp[:192].reshape(4, 2, 24, HALF)
+    down = mlp[192:].reshape(2, 96, HALF)
+    both = [
+        jnp.concatenate(
+            [matrices[:, i].reshape(96, HALF), up[:, i].reshape(96, HALF), down[i], attn[192:]]
+        )
+        for i in range(2)
+    ]
+    keep = grid.by_core(both[0], both[1])
+    arrived = grid.swap_core(grid.by_core(both[1], both[0]))
+    rows = jnp.concatenate([grid.by_core(keep, arrived), grid.by_core(arrived, keep)], axis=1)
+    matrices = rows[:96].reshape(4, 24, 768)
+    up = rows[96:192].reshape(4, 24, 768).transpose(1, 0, 2).reshape(24, 3072)
+    return (matrices[:3], matrices[3], up, rows[192:288], rows[288:])
+
+
+def gather_block_plain(gains, shifts, qkv, w_out, w_up, w_down):
+    return (
+        lax.all_gather(gains, AX, axis=1, tiled=True),
+        lax.all_gather(shifts, AX, axis=1, tiled=True),
+        lax.all_gather(qkv, AX, axis=1, tiled=True),
+        lax.all_gather(w_out, AX, axis=0, tiled=True),
+        lax.all_gather(w_up, AX, axis=0, tiled=True),
+        lax.all_gather(w_down, AX, axis=0, tiled=True),
+    )
+
+
+def reduce_block_plain(terms):
+    gains, shifts, qkv, w_out, w_up, w_down = terms
+    return (
+        lax.psum_scatter(gains, AX, scatter_dimension=1, tiled=True),
+        lax.psum_scatter(shifts, AX, scatter_dimension=1, tiled=True),
+        lax.psum_scatter(qkv, AX, scatter_dimension=1, tiled=True),
+        lax.psum_scatter(w_out, AX, scatter_dimension=0, tiled=True),
+        lax.psum_scatter(w_up, AX, scatter_dimension=0, tiled=True),
+        lax.psum_scatter(w_down, AX, scatter_dimension=0, tiled=True),
+    )
+
+
+def gather_all(grid, cross, own_block):
+    low = jnp.concatenate([cross[0], cross[1], own_block[0], own_block[1]], axis=0)
+    low = jnp.pad(low, ((0, 6), (0, HALF - 24)))
+    shards = [shard_of_block(*cross[2:]), shard_of_block(*own_block[2:])]
+    keep, send = grid.halves(jnp.concatenate(shards, axis=0))
+    arrived = grid.swap_core(jnp.concatenate([send, low], axis=0))
+    cross_attn, cross_mlp = units_of_block(grid, keep[:288], arrived[:288])
+    self_attn, self_mlp = units_of_block(grid, keep[288:], arrived[288:576])
+    vectors = pack_rows(grid, low[:, :24], arrived[576:, :24], 1)
+    vectors = jnp.pad(vectors, ((0, 0), (0, HALF - 48)))
+    cross_attn = jnp.concatenate([cross_attn, vectors], axis=0)
+    full = grid.assemble(*grid.gather(cross_attn))
+    vectors = full[:, :, 192:, :48].transpose(2, 0, 1, 3).reshape(16, 768)
+    cross_full = (vectors[0:3], vectors[3:6]) + attn_weights(full)
+    cross_full += mlp_weights(grid.assemble(*grid.gather(cross_mlp)))
+    self_full = (vectors[6:8], vectors[8:10])
+    self_full += attn_weights(grid.assemble(*grid.gather(self_attn)))
+    self_full += mlp_weights(grid.assemble(*grid.gather(self_mlp)))
+    return (cross_full, self_full)
+
+
+def reduce_block(grid, terms):
+    gains, shifts, qkv, w_out, w_up, w_down = terms
+    vectors = jnp.concatenate([gains, shifts], axis=0)
+    count = gains.shape[0]
+    extra = jnp.pad(vectors, ((0, 16 - 2 * count), (0, 0)))
+    mlp = grid.reduce(mlp_terms(w_up, w_down))
+    attn = grid.reduce(attn_terms(qkv, w_out, extra))
+    qkv, w_out, w_up, w_down, vectors = finish(grid, attn, mlp)
+    mine = lax.dynamic_slice_in_dim(vectors, 24 * (2 * lax.axis_index("dp") + grid.core), 24, 1)
+    return (mine[:count], mine[count : 2 * count], qkv, w_out, w_up, w_down)
+
+
 def local(
+    planned,
     latents,
     inputs,
     frame_counts,
@@ -220,83 +413,34 @@
     keeping = (1 - drop_mask).astype(jnp.float32)
     latent_in = latents.astype(jnp.float32)
     features_in = inputs.astype(jnp.float32)
-    cross_full = (
-        lax.all_gather(cross_gains, ("dp", "fsdp"), axis=1, tiled=True),
-        lax.all_gather(cross_shifts, ("dp", "fsdp"), axis=1, tiled=True),
-        lax.all_gather(cross_qkv, ("dp", "fsdp"), axis=1, tiled=True),
-        lax.all_gather(cross_out, ("dp", "fsdp"), axis=0, tiled=True),
-        lax.all_gather(cross_up, ("dp", "fsdp"), axis=0, tiled=True),
-        lax.all_gather(cross_down, ("dp", "fsdp"), axis=0, tiled=True),
-    )
+    cross = (cross_gains, cross_shifts, cross_qkv, cross_out, cross_up, cross_down)
+    own_block = (self_gains, self_shifts, self_qkv, self_out, self_up, self_down)
+    if planned:
+        grid = Grid()
+        cross_full, self_full = gather_all(grid, cross, own_block)
+    else:
+        cross_full = gather_block_plain(*cross)
+        self_full = gather_block_plain(*own_block)
     middle, cross_saved = block_forward(latent_in, features_in, usable, keeping, cross_full)
-    self_full = (
-        lax.all_gather(self_gains, ("dp", "fsdp"), axis=1, tiled=True),
-        lax.all_gather(self_shifts, ("dp", "fsdp"), axis=1, tiled=True),
-        lax.all_gather(self_qkv, ("dp", "fsdp"), axis=1, tiled=True),
-        lax.all_gather(self_out, ("dp", "fsdp"), axis=0, tiled=True),
-        lax.all_gather(self_up, ("dp", "fsdp"), axis=0, tiled=True),
-        lax.all_gather(self_down, ("dp", "fsdp"), axis=0, tiled=True),
-    )
     result, self_saved = block_forward(middle, None, None, None, self_full)
     upstream = cotangent.astype(jnp.float32)
-    self_back = (
-        lax.all_gather(self_gains, ("dp", "fsdp"), axis=1, tiled=True),
-        lax.all_gather(self_shifts, ("dp", "fsdp"), axis=1, tiled=True),
-        lax.all_gather(self_qkv, ("dp", "fsdp"), axis=1, tiled=True),
-        lax.all_gather(self_out, ("dp", "fsdp"), axis=0, tiled=True),
-        lax.all_gather(self_up, ("dp", "fsdp"), axis=0, tiled=True),
-        lax.all_gather(self_down, ("dp", "fsdp"), axis=0, tiled=True),
-    )
     d_middle, unused_features, self_terms = block_backward(
-        upstream, middle, None, None, None, self_back, self_saved
-    )
-    self_parts = (
-        lax.psum_scatter(self_terms[0], ("dp", "fsdp"), scatter_dimension=1, tiled=True),
-        lax.psum_scatter(self_terms[1], ("dp", "fsdp"), scatter_dimension=1, tiled=True),
-        lax.psum_scatter(self_terms[2], ("dp", "fsdp"), scatter_dimension=1, tiled=True),
-        lax.psum_scatter(self_terms[3], ("dp", "fsdp"), scatter_dimension=0, tiled=True),
-        lax.psum_scatter(self_terms[4], ("dp", "fsdp"), scatter_dimension=0, tiled=True),
-        lax.psum_scatter(self_terms[5], ("dp", "fsdp"), scatter_dimension=0, tiled=True),
-    )
-    cross_back = (
-        lax.all_gather(cross_gains, ("dp", "fsdp"), axis=1, tiled=True),
-        lax.all_gather(cross_shifts, ("dp", "fsdp"), axis=1, tiled=True),
-        lax.all_gather(cross_qkv, ("dp", "fsdp"), axis=1, tiled=True),
-        lax.all_gather(cross_out, ("dp", "fsdp"), axis=0, tiled=True),
-        lax.all_gather(cross_up, ("dp", "fsdp"), axis=0, tiled=True),
-        lax.all_gather(cross_down, ("dp", "fsdp"), axis=0, tiled=True),
+        upstream, middle, None, None, None, self_full, self_saved
     )
     d_latent, d_features, cross_terms = block_backward(
-        d_middle, latent_in, features_in, usable, keeping, cross_back, cross_saved
-    )
-    cross_parts = (
-        lax.psum_scatter(cross_terms[0], ("dp", "fsdp"), scatter_dimension=1, tiled=True),
-        lax.psum_scatter(cross_terms[1], ("dp", "fsdp"), scatter_dimension=1, tiled=True),
-        lax.psum_scatter(cross_terms[2], ("dp", "fsdp"), scatter_dimension=1, tiled=True),
-        lax.psum_scatter(cross_terms[3], ("dp", "fsdp"), scatter_dimension=0, tiled=True),
-        lax.psum_scatter(cross_terms[4], ("dp", "fsdp"), scatter_dimension=0, tiled=True),
-        lax.psum_scatter(cross_terms[5], ("dp", "fsdp"), scatter_dimension=0, tiled=True),
-    )
-    return (
-        result.astype(jnp.bfloat16),
-        d_latent,
-        d_features,
-        cross_parts[0],
-        cross_parts[1],
-        cross_parts[2],
-        cross_parts[3],
-        cross_parts[4],
-        cross_parts[5],
-        self_parts[0],
-        self_parts[1],
-        self_parts[2],
-        self_parts[3],
-        self_parts[4],
-        self_parts[5],
-    )
+        d_middle, latent_in, features_in, usable, keeping, cross_full, cross_saved
+    )
+    if planned:
+        self_parts = reduce_block(grid, self_terms)
+        cross_parts = reduce_block(grid, cross_terms)
+    else:
+        self_parts = reduce_block_plain(self_terms)
+        cross_parts = reduce_block_plain(cross_terms)
+    return (result.astype(jnp.bfloat16), d_latent, d_features) + cross_parts + self_parts
 
 
 def solution(mesh):
+    planned = mesh.shape["dp"] == 16 and mesh.shape["fsdp"] == 2
     in_specs = (
         P(("dp", "fsdp"), None, None),
         P(("dp", "fsdp"), None, None),
@@ -335,4 +479,5 @@
         P(("dp", "fsdp"), None),
         P(("dp", "fsdp"), None),
     )
-    return jax.shard_map(local, mesh=mesh, in_specs=in_specs, out_specs=out_specs, check_vma=False)
+    return jax.shard_map(
+        functools.partial(local, planned), mesh=mesh, in_specs=in_specs, out_specs=out_specs, check_vma=False)

time: 1660 us -> 823 us (0.50)
  waiting for transfers between devices: 986 us -> 161 us
  blocking collectives: 195 us -> 43.5 us
  other arithmetic: 70.1 us -> 155 us
  local copies, waits for them, and re-layouts: 50 us -> 110 us
  starting transfers between devices: 1.42 us -> 39.9 us
  matrix products: 329 us -> 291 us
    reduce_scatter x8 -> x4, waiting for transfers between devices: 793 us -> 22.3 us  [reduce(): lax.psum_scatter(own, 'dp', scatter_dimension=0, axis_index_groups=self.c...]
    all_gather x8 -> x2, waiting for transfers between devices: 188 us -> 0.02 us  [gather(): own = lax.all_gather(unit, 'dp', axis=0, axis_index_groups=self.columns)]
    ppermute x0 -> x55, waiting for transfers between devices: none -> 139 us  [the longest x16 90.3 us: swap_x(): return lax.ppermute(value, AX, self.to_x)]
    all_gather x4 -> x2, blocking collectives: 155 us -> 43.5 us  [gather(): own = lax.all_gather(unit, 'dp', axis=0, axis_index_groups=self.columns)]
    unnamed x1 -> x0, blocking collectives: 40.5 us -> none
    ppermute x0 -> x55, starting transfers between devices: none -> 38.9 us  [the longest x16 21.1 us: swap_x(): return lax.ppermute(value, AX, self.to_x)]
    reshape x0 -> x7, local copies, waits for them, and re-layouts: none -> 28.7 us  [the longest x3 25.4 us: mlp_terms(): w_up.astype(jnp.bfloat16).reshape(4, 4, 48, 4, 768).transpose(0, 1, 3, 2, 4)]
    concatenate x0 -> x39, other arithmetic: none -> 27.7 us  [the longest x16 14.1 us: assemble(): jnp.concatenate([self.by_core(a, b), self.by_core(b, a)], axis=-1)]
  transfers between devices with their start and end apart: 16 -> 61, of which waited for: 11 -> 22; matrix products, arithmetic and copies ran while one was open for 20% -> 27% of each run, Pallas kernels for 0% -> 0%
where the time goes in v1:
time: 823 us; the launch traced here: 817 us
  matrix products  291 us (35%)
  waiting for transfers between devices  161 us (20%)
  other arithmetic  155 us (19%)
  local copies, waits for them, and re-layouts  110 us (13%)
  blocking collectives  43.5 us (5%)
  starting transfers between devices  39.9 us (5%)
  between operations  17 us (2%)
    ppermute x16, waiting for transfers between devices, swap_x(): return lax.ppermute(value, AX, self.to_x)  90.3 us
    dot_general x12, matrix products, project(): jnp.einsum('bld,de->ble', left, weight, preferred_element_type=jnp.float32)  81.7 us
    dot_general x12, matrix products, project_back(): jnp.einsum('ble,de->bld', left, weight, preferred_element_type=jnp.float32)  71.1 us
    dot_general x12, matrix products, outer_sum(): jnp.einsum('bld,ble->de', left, right, preferred_element_type=jnp.float32)  69.1 us
    ppermute x16, waiting for transfers between devices, swap_y(): return lax.ppermute(value, AX, self.to_y)  47.1 us
    all_gather x2, blocking collectives, gather(): own = lax.all_gather(unit, 'dp', axis=0, axis_index_groups=self.columns)  43.5 us
    unnamed x291, local copies, waits for them, and re-layouts  26.9 us
    reshape x3, local copies, waits for them, and re-layouts, mlp_terms(): w_up.astype(jnp.bfloat16).reshape(4, 4, 48, 4, 768).transpose(0, 1, 3, 2, 4)  25.4 us
  transfers between devices with their start and end apart: 61, of which 22 were waited for; matrix products, arithmetic and copies ran while one was open for 27% of the time, Pallas kernels for 0%

profile of v1, /device:TPU:0, one launch (start us, length us, event | category | flops | bytes accessed | tf_op | source)
XLA Modules:
  0.0 816.7 jit_solution(13277702009009992834)
XLA Ops:
  18.5 22.4 %all_gather.25 = bf16[4,192,384]{2,1,0:T(8,128)(2,1)S(1)} all-gather(bf16[1,192,384]{2,1,0:T(8,128)(2,1)S(1)} %bitcast.748), channel_id=1, replica_groups={{0,8,16,24},{2,10,18,26},{4,12,20,28},{6,14,22,30},{1,9,17,25},{3,11,19..., dimensions={0}, use_global_device_ids=true | all-gather | bytes 737280 | tf_op jit(solution)/shard_map/all_gather | solution.py:231
  44.7 21.1 %all-gather = bf16[832,384]{1,0:T(8,128)(2,1)S(1)} all-gather(bf16[208,384]{1,0:T(8,128)(2,1)S(1)} %pad_maximum_fusion.57), channel_id=2, replica_groups={{0,8,16,24},{2,10,18,26},{4,12,20,28},{6,14,22,30},{1,9,17,25},{3,11,19..., dimensions={0}, use_global_device_ids=true | all-gather | bytes 798720 | tf_op jit(solution)/shard_map/all_gather | solution.py:231
  152.5 9.8 %fusion.163 = (f32[8,12,128]{2,1,0:T(8,128)S(1)}, f32[8,12,128,296]{2,3,1,0:T(8,128)}) fusion(bf16[8,128,12,64]{1,3,2,0:T(8,128)(2,1)S(1)} %bitcast.633, bf16[8,296,12,64]{1,3,2,0:T(8,128)(2,1)} %bitcast.610, pred[8,296]{1,0:T(8,128)(4,1)S(1)} %pad_add_fusion), kind=kOutput, calls=%fused_computation.525 | convolution fusion | flops 476467200 | bytes 19810624 | tf_op jit(solution)/shard_map/blhe,bshe->bhls/dot_general | solution.py:49
  171.5 9.8 %fusion.67 = bf16[8,12,64,128]{3,2,1,0:T(8,128)(2,1)S(1)} fusion(bf16[8,296,12,64]{1,3,2,0:T(8,128)(2,1)} %bitcast.614, f32[8,12,128,296]{2,3,1,0:T(8,128)} %get-tuple-element.219, f32[8,12,128]{2,1,0:T(8,128)S(1)} %fusion, f32[8,12,128]{2,1,0:T(8,128)S(1)} %get-tuple-element.218), kind=kOutput, calls=%fused_computation.182 | convolution fusion | flops 477265920 | bytes 19857408 | tf_op jit(solution)/shard_map/bhls,bshe->blhe/dot_general | solution.py:80
  189.2 10.8 %collective-permute-done.9 = bf16[4,384,384]{2,1,0:T(8,128)(2,1)S(1)} collective-permute-done((bf16[4,384,384]{2,1,0:T(8,128)(2,1)}, bf16[4,384,384]{2,1,0:T(8,128)(2,1)S(1)}, u32[]{:S(2)}, u32[]{:S(2)}) %collective-permute-start.9) | collective-permute-done | bytes 1179680 | tf_op jit(solution)/shard_map/ppermute | solution.py:221
  214.4 9.9 %collective-permute-done.25 = bf16[4,384,384]{2,1,0:T(8,128)(2,1)S(1)} collective-permute-done((bf16[4,384,384]{2,1,0:T(8,128)(2,1)}, bf16[4,384,384]{2,1,0:T(8,128)(2,1)S(1)}, u32[]{:S(2)}, u32[]{:S(2)}) %collective-permute-start.25) | collective-permute-done | bytes 1179680 | tf_op jit(solution)/shard_map/ppermute | solution.py:221
  224.9 10.9 %collective-permute-done.27 = bf16[4,384,384]{2,1,0:T(8,128)(2,1)} collective-permute-done((bf16[4,384,384]{2,1,0:T(8,128)(2,1)}, bf16[4,384,384]{2,1,0:T(8,128)(2,1)}, u32[]{:S(2)}, u32[]{:S(2)}) %collective-permute-start.27) | collective-permute-done | bytes 1179680 | tf_op jit(solution)/shard_map/ppermute | solution.py:218
  250.0 9.8 %collective-permute-done.26 = bf16[4,192,384]{2,1,0:T(8,128)(2,1)S(1)} collective-permute-done((bf16[4,192,384]{2,1,0:T(8,128)(2,1)S(1)}, bf16[4,192,384]{2,1,0:T(8,128)(2,1)S(1)}, u32[]{:S(2)}, u32[]{:S(2)}) %collective-permute-start.26) | collective-permute-done | bytes 589856 | tf_op jit(solution)/shard_map/ppermute | solution.py:218
  294.4 10.9 %fusion.164 = (f32[8,128]{1,0:T(8,128)S(1)}, f32[8,128,768]{2,1,0:T(8,128)S(1)}) fusion(f32[8,128,768]{2,1,0:T(8,128)S(1)} %copy-done.38, bf16[3072,768,1]{1,0,2:T(8,128)(2,1)S(1)} %bitcast.647, f32[8,128,3072]{2,1,0:T(8,128)} %fusion.62, f32[8]{0:T(128)S(1)} %copy-done.110, bf16[8,128,768]{2,1,0:T(8,128)(2,1)S(1)} %copy-done.8), kind=kOutput, calls=%fused_computation.526 | convolution fusion | flops 4864080896 | bytes 25169952 | tf_op jit(solution)/shard_map/bld,de->ble/dot_general | solution.py:33
  339.5 9.8 %fusion.60 = f32[8,128,3072]{2,1,0:T(8,128)} fusion(bf16[768,768]{1,0:T(8,128)(2,1)S(1)} %bitcast.713, bf16[768,768]{1,0:T(8,128)(2,1)S(1)} %bitcast.715, bf16[768,768]{1,0:T(8,128)(2,1)S(1)} %bitcast.717, bf16[768,768]{1,0:T(8,128)(2,1)S(1)} %bitcast.711, f32[8,128,768]{2,1,0:T(8,128)S(1)} %get-tuple-element.47, f32[768]{0:T(1024)S(1)} %add.387, ...), kind=kOutput, calls=%fused_computation.177 | convolution fusion | flops 4854644736 | bytes 20461568 | tf_op jit(solution)/shard_map/bld,de->ble/dot_general | solution.py:33
  349.3 12.1 %bitcast_convert_fusion = bf16[3072,768]{1,0:T(8,128)(2,1)} fusion(bf16[8,128,768]{2,1,0:T(8,128)(2,1)S(1)} %copy-done.28, f32[8,128,3072]{2,1,0:T(8,128)} %fusion.60), kind=kOutput, calls=%fused_computation.38 | convolution fusion | flops 4862509056 | bytes 18874368 | tf_op jit(solution)/shard_map/bld,ble->de/dot_general | solution.py:41
  361.4 15.3 %fusion.14 = bf16[8,128,3072]{2,1,0:T(8,128)(2,1)} fusion(f32[8,128,3072]{2,1,0:T(8,128)} %fusion.60, bf16[3072,768,1]{1,0,2:T(8,128)(2,1)S(1)} %bitcast.646, bf16[8,128,768]{2,1,0:T(8,128)(2,1)S(1)} %copy-done.28), kind=kOutput, calls=%fused_computation.24 | convolution fusion | flops 4894752768 | bytes 25165824 | tf_op jit(solution)/shard_map/ble,de->bld/dot_general | solution.py:37
  385.7 9.9 %bitcast_convert_fusion.1 = bf16[768,3072]{1,0:T(8,128)(2,1)} fusion(bf16[8,128,3072]{2,1,0:T(8,128)(2,1)} %fusion.14, f32[8,128,768]{2,1,0:T(8,128)S(1)} %get-tuple-element.47, f32[768]{0:T(1024)S(1)} %add.387, f32[768]{0:T(1024)S(1)} %mul.485, f32[8,128]{1,0:T(8,128)S(1)} %fusion.128, f32[8,128]{1,0:T(8,128)S(1)} %broadcast_multiply_fusion.1), kind=kOutput, calls=%fused_computation.39 | convolution fusion | flops 4838129664 | bytes 14170112 | tf_op jit(solution)/shard_map/bld,ble->de/dot_general | solution.py:41
  439.3 14.8 %fusion.7 = bf16[8,128,3072]{2,1,0:T(8,128)(2,1)S(1)} fusion(f32[8,128,3072]{2,1,0:T(8,128)} %fusion.62, bf16[3072,768,1]{1,0,2:T(8,128)(2,1)S(1)} %bitcast.650, f32[8,128,768]{2,1,0:T(8,128)S(1)} %convert_add_fusion.2, f32[8]{0:T(128)S(1)} %copy-done.110), kind=kOutput, calls=%fused_computation.17 | convolution fusion | flops 4896325632 | bytes 26738720 | tf_op jit(solution)/shard_map/ble,de->bld/dot_general | solution.py:37
  454.2 12.6 %bitcast_convert_fusion.2 = bf16[3072,768]{1,0:T(8,128)(2,1)} fusion(f32[8,128,768]{2,1,0:T(8,128)S(1)} %convert_add_fusion.2, f32[8]{0:T(128)S(1)} %copy-done.110, f32[8,128,3072]{2,1,0:T(8,128)} %fusion.62), kind=kOutput, calls=%fused_computation.40 | convolution fusion | flops 4864081920 | bytes 20447264 | tf_op jit(solution)/shard_map/bld,ble->de/dot_general | solution.py:41
  489.9 10.7 %fusion.55 = bf16[8,12,64,296]{3,2,1,0:T(8,128)(2,1)} fusion(bf16[8,128,12,64]{1,3,2,0:T(8,128)(2,1)} %bitcast.627, f32[8,12,128,296]{2,3,1,0:T(8,128)} %get-tuple-element.219, f32[8,12,128]{2,1,0:T(8,128)S(1)} %copy-done.70), kind=kOutput, calls=%fused_computation.133 | convolution fusion | flops 474660864 | bytes 19808256 | tf_op jit(solution)/shard_map/bhls,blhe->bshe/dot_general | solution.py:146
  500.6 15.0 %multiply_reduce_fusion = (f32[8,12,128]{2,1,0:T(8,128)S(1)}, f32[8,12,128,296]{2,3,1,0:T(8,128)}) fusion(f32[8,12,128,296]{2,3,1,0:T(8,128)} %get-tuple-element.219, f32[8,12,128]{2,1,0:T(8,128)S(1)} %copy-done.70, bf16[8,128,12,64]{1,3,2,0:T(8,128)(2,1)} %bitcast.628, bf16[8,296,12,64]{1,3,2,0:T(8,128)(2,1)S(1)} %bitcast.617), kind=kOutput, calls=%fused_computation.5 | convolution fusion | flops 476467200 | bytes 34406400 | tf_op jit(solution)/shard_map/blhe,bshe->bhls/dot_general | solution.py:153
  515.6 10.5 %multiply_convert_fusion = bf16[8,12,128,296]{2,3,1,0:T(8,128)(2,1)S(1)} fusion(f32[8,12,128,296]{2,3,1,0:T(8,128)} %get-tuple-element.233, f32[8,12,128,296]{2,3,1,0:T(8,128)} %get-tuple-element.219, f32[8,12,128]{2,1,0:T(8,128)S(1)} %get-tuple-element.232, f32[8,12,128]{2,1,0:T(8,128)S(1)} %copy-done.70), kind=kLoop, calls=%fused_computation.4 | loop fusion | flops 14548992 | bytes 36470784 | tf_op jit(solution)/shard_map/convert_element_type | solution.py:158
  549.2 10.1 %reshape.1805 = bf16[4,4,48,4,768]{4,3,2,1,0:T(4,128)(2,1)} reshape(bf16[768,3072]{1,0:T(8,128)(2,1)} %bitcast_convert_fusion.1) | data formatting | bytes 9437184 | tf_op jit(solution)/shard_map/reshape | solution.py:309
  564.8 9.8 %reshape.1794 = bf16[4,4,48,4,768]{4,3,2,1,0:T(4,128)(2,1)} reshape(bf16[768,3072]{1,0:T(8,128)(2,1)} %bitcast_convert_fusion.3) | data formatting | bytes 9437184 | tf_op jit(solution)/shard_map/reshape | solution.py:309
  685.9 10.4 %collective-permute-done.52 = bf16[4,192,384]{2,1,0:T(8,128)(2,1)S(1)} collective-permute-done((bf16[4,192,384]{2,1,0:T(8,128)(2,1)S(1)}, bf16[4,192,384]{2,1,0:T(8,128)(2,1)S(1)}, u32[]{:S(2)}, u32[]{:S(2)}) %collective-permute-start.52) | collective-permute-done | bytes 589856 | tf_op jit(solution)/shard_map/ppermute | solution.py:218
  720.1 11.8 %collective-permute-done.53 = bf16[4,384,384]{2,1,0:T(8,128)(2,1)} collective-permute-done((bf16[4,384,384]{2,1,0:T(8,128)(2,1)}, bf16[4,384,384]{2,1,0:T(8,128)(2,1)}, u32[]{:S(2)}, u32[]{:S(2)}) %collective-permute-start.53) | collective-permute-done | bytes 1179680 | tf_op jit(solution)/shard_map/ppermute | solution.py:221
  742.0 13.2 %add_convert_fusion.1 = bf16[8,128,768]{2,1,0:T(8,128)(2,1)} fusion(f32[8,128,768]{2,1,0:T(8,128)S(1)} %copy-done.3, f32[8,128,768]{2,1,0:T(8,128)} %get-tuple-element.225, bf16[3072,768,1]{1,0,2:T(8,128)(2,1)} %bitcast.643, f32[8,128,3072]{2,1,0:T(8,128)} %fusion.60), kind=kOutput, calls=%fused_computation.123 | convolution fusion | flops 4862509056 | bytes 25165824 | tf_op jit(solution)/shard_map/bld,de->ble/dot_general | solution.py:33
  778.1 22.2 %reduce-scatter.7.cloned.1.call-done = bf16[1,384,384]{2,1,0:T(8,128)(2,1)} async-done(((bf16[4,384,384]{2,1,0:T(8,128)(2,1)}), bf16[1,384,384]{2,1,0:T(8,128)(2,1)}) %reduce-scatter.7.cloned.1.call-update) | async-done | bytes 294928 | tf_op jit(solution)/shard_map/reduce_scatter | solution.py:266
  (687 shorter events, 496.1 us)
Async XLA Ops:
  7.2 163.7 %all-gather.6.cloned.1.call-start = ((), (), s32[]{:S(2)}) async-start(), calls=%async_computation.8 | async-start | bytes 1474560 | tf_op jit(solution)/shard_map/all_gather | solution.py:231
  18.4 168.7 %all-gather.8.cloned.1.call-start = ((), (), s32[]{:S(2)}) async-start(), calls=%async_computation.9 | async-start | bytes 1474560 | tf_op jit(solution)/shard_map/all_gather | solution.py:231
  40.9 34.9 %collective-permute-start.24 = (bf16[4,192,384]{2,1,0:T(8,128)(2,1)S(1)}, bf16[4,192,384]{2,1,0:T(8,128)(2,1)}, u32[]{:S(2)}, u32[]{:S(2)}) collective-permute-start(bf16[4,192,384]{2,1,0:T(8,128)(2,1)S(1)} %all_gather.25), channel_id=1, source_target_pairs={{0,1},{1,0},{2,3},{3,2},{4,5},{5,4},{6,7},{7,6},{8,9},{9,8},{10,11... | collective-permute-start | bytes 1769480 | tf_op jit(solution)/shard_map/ppermute | solution.py:215
  42.6 31.7 %collective-permute-start.17 = (bf16[4,192,384]{2,1,0:T(8,128)(2,1)S(1)}, bf16[4,192,384]{2,1,0:T(8,128)(2,1)}, u32[]{:S(2)}, u32[]{:S(2)}) collective-permute-start(bf16[4,192,384]{2,1,0:T(8,128)(2,1)S(1)} %all_gather.25), channel_id=1, source_target_pairs={{0,4},{1,5},{2,6},{3,7},{4,0},{5,1},{6,2},{7,3},{8,12},{9,13},{10,... | collective-permute-start | bytes 1769480 | tf_op jit(solution)/shard_map/ppermute | solution.py:221
  72.6 699.4 %reduce-scatter.9.cloned.1.call-start = ((), (), s32[]{:S(2)}) async-start(), calls=%async_computation.6 | async-start | bytes 798720 | tf_op jit(solution)/shard_map/reduce_scatter | solution.py:266
  187.1 51.4 %collective-permute-start.16 = (bf16[4,384,384]{2,1,0:T(8,128)(2,1)}, bf16[4,384,384]{2,1,0:T(8,128)(2,1)}, u32[]{:S(2)}, u32[]{:S(2)}) collective-permute-start(bf16[4,384,384]{2,1,0:T(8,128)(2,1)} %bitcast.44), channel_id=1, source_target_pairs={{0,1},{1,0},{2,3},{3,2},{4,5},{5,4},{6,7},{7,6},{8,9},{9,8},{10,11... | collective-permute-start | bytes 3538952 | tf_op jit(solution)/shard_map/ppermute | solution.py:215
  187.1 48.7 %collective-permute-start.27 = (bf16[4,384,384]{2,1,0:T(8,128)(2,1)}, bf16[4,384,384]{2,1,0:T(8,128)(2,1)}, u32[]{:S(2)}, u32[]{:S(2)}) collective-permute-start(bf16[4,384,384]{2,1,0:T(8,128)(2,1)} %bitcast.719), channel_id=1, source_target_pairs={{0,2},{1,3},{2,0},{3,1},{4,6},{5,7},{6,4},{7,5},{8,10},{9,11},{10,... | collective-permute-start | bytes 3538952 | tf_op jit(solution)/shard_map/ppermute | solution.py:218
  187.7 36.6 %collective-permute-start.25 = (bf16[4,384,384]{2,1,0:T(8,128)(2,1)}, bf16[4,384,384]{2,1,0:T(8,128)(2,1)S(1)}, u32[]{:S(2)}, u32[]{:S(2)}) collective-permute-start(bf16[4,384,384]{2,1,0:T(8,128)(2,1)} %bitcast.720), channel_id=1, source_target_pairs={{0,4},{1,5},{2,6},{3,7},{4,0},{5,1},{6,2},{7,3},{8,12},{9,13},{10,... | collective-permute-start | bytes 3538952 | tf_op jit(solution)/shard_map/ppermute | solution.py:221
  200.0 40.5 %collective-permute-start.32 = (bf16[4,384,384]{2,1,0:T(8,128)(2,1)}, bf16[4,384,384]{2,1,0:T(8,128)(2,1)}, u32[]{:S(2)}, u32[]{:S(2)}) collective-permute-start(bf16[4,384,384]{2,1,0:T(8,128)(2,1)} %bitcast.721), channel_id=1, source_target_pairs={{0,1},{1,0},{2,3},{3,2},{4,5},{5,4},{6,7},{7,6},{8,9},{9,8},{10,11... | collective-permute-start | bytes 3538952 | tf_op jit(solution)/shard_map/ppermute | solution.py:215
  210.5 37.9 %collective-permute-start.10 = (bf16[4,192,384]{2,1,0:T(8,128)(2,1)}, bf16[4,192,384]{2,1,0:T(8,128)(2,1)}, u32[]{:S(2)}, u32[]{:S(2)}) collective-permute-start(bf16[4,192,384]{2,1,0:T(8,128)(2,1)} %slice.659), channel_id=1, source_target_pairs={{0,2},{1,3},{2,0},{3,1},{4,6},{5,7},{6,4},{7,5},{8,10},{9,11},{10,... | collective-permute-start | bytes 1769480 | tf_op jit(solution)/shard_map/ppermute | solution.py:218
  224.3 36.6 %collective-permute-start.12 = (bf16[4,192,384]{2,1,0:T(8,128)(2,1)S(1)}, bf16[4,192,384]{2,1,0:T(8,128)(2,1)S(1)}, u32[]{:S(2)}, u32[]{:S(2)}) collective-permute-start(bf16[4,192,384]{2,1,0:T(8,128)(2,1)S(1)} %slice.660), channel_id=1, source_target_pairs={{0,4},{1,5},{2,6},{3,7},{4,0},{5,1},{6,2},{7,3},{8,12},{9,13},{10,... | collective-permute-start | bytes 1769480 | tf_op jit(solution)/shard_map/ppermute | solution.py:221
  591.7 42.1 %collective-permute-start.44 = (bf16[4,4,208,384]{3,2,1,0:T(8,128)(2,1)}, bf16[4,4,208,384]{3,2,1,0:T(8,128)(2,1)}, u32[]{:S(2)}, u32[]{:S(2)}) collective-permute-start(bf16[4,4,208,384]{3,2,1,0:T(8,128)(2,1)} %pad_maximum_fusion.12), channel_id=1, source_target_pairs={{0,1},{1,0},{2,3},{3,2},{4,5},{5,4},{6,7},{7,6},{8,9},{9,8},{10,11... | collective-permute-start | bytes 7667720 | tf_op jit(solution)/shard_map/ppermute | solution.py:215
  601.7 72.1 %collective-permute-start.49 = (bf16[4,4,384,384]{3,2,1,0:T(8,128)(2,1)}, bf16[4,4,384,384]{3,2,1,0:T(8,128)(2,1)}, u32[]{:S(2)}, u32[]{:S(2)}) collective-permute-start(bf16[4,4,384,384]{3,2,1,0:T(8,128)(2,1)} %pad_maximum_fusion.10), channel_id=1, source_target_pairs={{0,1},{1,0},{2,3},{3,2},{4,5},{5,4},{6,7},{7,6},{8,9},{9,8},{10,11... | collective-permute-start | bytes 14155784 | tf_op jit(solution)/shard_map/ppermute | solution.py:215
  633.7 45.4 %collective-permute-start.38 = (bf16[4,4,384,384]{3,2,1,0:T(8,128)(2,1)}, bf16[4,4,384,384]{3,2,1,0:T(8,128)(2,1)}, u32[]{:S(2)}, u32[]{:S(2)}) collective-permute-start(bf16[4,4,384,384]{3,2,1,0:T(8,128)(2,1)} %pad_maximum_fusion.9), channel_id=1, source_target_pairs={{0,1},{1,0},{2,3},{3,2},{4,5},{5,4},{6,7},{7,6},{8,9},{9,8},{10,11... | collective-permute-start | bytes 14155784 | tf_op jit(solution)/shard_map/ppermute | solution.py:215
  657.8 43.0 %collective-permute-start.37 = (bf16[4,208,384]{2,1,0:T(8,128)(2,1)}, bf16[4,208,384]{2,1,0:T(8,128)(2,1)}, u32[]{:S(2)}, u32[]{:S(2)}) collective-permute-start(bf16[4,208,384]{2,1,0:T(8,128)(2,1)} %pad_maximum_fusion.45), channel_id=1, source_target_pairs={{0,4},{1,5},{2,6},{3,7},{4,0},{5,1},{6,2},{7,3},{8,12},{9,13},{10,... | collective-permute-start | bytes 1916936 | tf_op jit(solution)/shard_map/ppermute | solution.py:221
  666.6 34.8 %collective-permute-start.35 = (bf16[4,208,384]{2,1,0:T(8,128)(2,1)}, bf16[4,208,384]{2,1,0:T(8,128)(2,1)}, u32[]{:S(2)}, u32[]{:S(2)}) collective-permute-start(bf16[4,208,384]{2,1,0:T(8,128)(2,1)} %pad_maximum_fusion.44), channel_id=1, source_target_pairs={{0,2},{1,3},{2,0},{3,1},{4,6},{5,7},{6,4},{7,5},{8,10},{9,11},{10,... | collective-permute-start | bytes 1916936 | tf_op jit(solution)/shard_map/ppermute | solution.py:218
  673.7 100.2 %reduce-scatter.5.cloned.1.call-start = ((), (), s32[]{:S(2)}) async-start(), calls=%async_computation.4 | async-start | bytes 798720 | tf_op jit(solution)/shard_map/reduce_scatter | solution.py:266
  684.0 32.3 %collective-permute-start.39 = (bf16[4,192,384]{2,1,0:T(8,128)(2,1)}, bf16[4,192,384]{2,1,0:T(8,128)(2,1)}, u32[]{:S(2)}, u32[]{:S(2)}) collective-permute-start(bf16[4,192,384]{2,1,0:T(8,128)(2,1)} %get-tuple-element.154), channel_id=1, source_target_pairs={{0,4},{1,5},{2,6},{3,7},{4,0},{5,1},{6,2},{7,3},{8,12},{9,13},{10,... | collective-permute-start | bytes 1769480 | tf_op jit(solution)/shard_map/ppermute | solution.py:221
  699.0 32.8 %collective-permute-start.53 = (bf16[4,384,384]{2,1,0:T(8,128)(2,1)}, bf16[4,384,384]{2,1,0:T(8,128)(2,1)}, u32[]{:S(2)}, u32[]{:S(2)}) collective-permute-start(bf16[4,384,384]{2,1,0:T(8,128)(2,1)} %pad_maximum_fusion.39), channel_id=1, source_target_pairs={{0,4},{1,5},{2,6},{3,7},{4,0},{5,1},{6,2},{7,3},{8,12},{9,13},{10,... | collective-permute-start | bytes 3538952 | tf_op jit(solution)/shard_map/ppermute | solution.py:221
  700.9 37.4 %collective-permute-start.51 = (bf16[4,384,384]{2,1,0:T(8,128)(2,1)}, bf16[4,384,384]{2,1,0:T(8,128)(2,1)}, u32[]{:S(2)}, u32[]{:S(2)}) collective-permute-start(bf16[4,384,384]{2,1,0:T(8,128)(2,1)} %pad_maximum_fusion.38), channel_id=1, source_target_pairs={{0,2},{1,3},{2,0},{3,1},{4,6},{5,7},{6,4},{7,5},{8,10},{9,11},{10,... | collective-permute-start | bytes 3538952 | tf_op jit(solution)/shard_map/ppermute | solution.py:218
  703.9 72.1 %reduce-scatter.11.cloned.1.call-start = ((), (), s32[]{:S(2)}) async-start(), calls=%async_computation.7 | async-start | bytes 1474560 | tf_op jit(solution)/shard_map/reduce_scatter | solution.py:266
  715.8 41.9 %collective-permute-start.42 = (bf16[4,384,384]{2,1,0:T(8,128)(2,1)}, bf16[4,384,384]{2,1,0:T(8,128)(2,1)}, u32[]{:S(2)}, u32[]{:S(2)}) collective-permute-start(bf16[4,384,384]{2,1,0:T(8,128)(2,1)} %pad_maximum_fusion.37), channel_id=1, source_target_pairs={{0,4},{1,5},{2,6},{3,7},{4,0},{5,1},{6,2},{7,3},{8,12},{9,13},{10,... | collective-permute-start | bytes 3538952 | tf_op jit(solution)/shard_map/ppermute | solution.py:221
  718.6 42.5 %collective-permute-start.40 = (bf16[4,384,384]{2,1,0:T(8,128)(2,1)}, bf16[4,384,384]{2,1,0:T(8,128)(2,1)}, u32[]{:S(2)}, u32[]{:S(2)}) collective-permute-start(bf16[4,384,384]{2,1,0:T(8,128)(2,1)} %pad_maximum_fusion.36), channel_id=1, source_target_pairs={{0,2},{1,3},{2,0},{3,1},{4,6},{5,7},{6,4},{7,5},{8,10},{9,11},{10,... | collective-permute-start | bytes 3538952 | tf_op jit(solution)/shard_map/ppermute | solution.py:218
  741.8 58.5 %reduce-scatter.7.cloned.1.call-start = ((), (), s32[]{:S(2)}) async-start(), calls=%async_computation.5 | async-start | bytes 1474560 | tf_op jit(solution)/shard_map/reduce_scatter | solution.py:266
  (174 other events, 2245.2 us)
Sparse Core Ops, SparseCore 0:
  18.5 42.4 all-gather.5
  72.8 28.6 all-gather.7
  673.8 21.1 reduce-scatter.8
  704.0 21.6 reduce-scatter.4
  742.0 28.2 reduce-scatter.10
  772.4 27.8 reduce-scatter.6

commit v2 on v0

v2 whole, which is shorter than its diff:
```python
import functools

import jax
import jax.numpy as jnp
from jax import lax
from jax.experimental import pallas as pl
from jax.experimental.pallas import tpu as pltpu
from jax.sharding import PartitionSpec as P

D = 768
FF = 3072
HALF = 384
LAT = 128
TOK = 296
PAD = 304
PAIRS = 6
P_SIZE = 16
VIDEO = 256
ITEMS = 2
ROWS = ITEMS * LAT
AX = ("dp", "fsdp")
F32 = jnp.float32
BF16 = jnp.bfloat16
NN = (((1,), (0,)), ((), ()))
NT = (((1,), (1,)), ((), ()))
TN = (((0,), (0,)), ((), ()))
ANY = pl.BlockSpec(memory_space=pl.ANY)
SMALL = pl.BlockSpec(memory_space=pltpu.SMEM)
VMEM_BYTES = 58 * 2**20
EXTRA = 16
SHARE = 0.1
ATTN_SPLIT = 96
MLP_SPLIT = 192


def dot(left, right, dims=NN):
    return lax.dot_general(left, right, dims, preferred_element_type=F32)


def norm_parts(value):
    mean = jnp.mean(value, axis=-1, keepdims=True)
    centered = value - mean
    variance = jnp.mean(centered * centered, axis=-1, keepdims=True)
    scale = lax.rsqrt(variance + 1e-05)
    return (centered * scale, scale)


def norm_back(hat, scale, gain, upstream):
    inner = upstream * gain
    first = jnp.mean(inner, axis=-1, keepdims=True)
    second = jnp.mean(inner * hat, axis=-1, keepdims=True)
    d_gain = jnp.sum(upstream * hat, axis=0, keepdims=True)
    d_shift = jnp.sum(upstream, axis=0, keepdims=True)
    return (scale * (inner - first - hat * second), d_gain, d_shift)


def gelu_both(u):
    c = 0.7978845608028654
    square = u * u
    t = jnp.tanh(u * (c + (c * 0.044715) * square))
    w = 0.5 + 0.5 * t
    slope = w + (0.5 * u) * (1.0 - t * t) * (c + (3.0 * c * 0.044715) * square)
    return (u * w, slope)


def weight_copies(info, pieces, split, targets, sems):
    place, core = (info[0], info[1])
    groups = []
    number = 0
    for start, rows, ref, base in targets:
        group = []
        for side in range(2):
            half = core if side == 0 else 1 - core
            column = pl.multiple_of(base + half * HALF, 128)
            for relative in range(4):
                if relative < 3:
                    source = pieces[5 * side + relative].at[:, pl.ds(start, rows)]
                elif start < split:
                    source = pieces[5 * side + 3].at[:, pl.ds(start, rows)]
                else:
                    source = pieces[5 * side + 4].at[:, pl.ds(start - split, rows)]
                target = ref.at[:, place ^ relative, :, pl.ds(column, HALF)]
                group.append(pltpu.make_async_copy(source, target, sems.at[number]))
                number += 1
        groups.append(group)
    return groups


def attn_copies(info, pieces, weights, sems):
    targets = [(48 * i, 48, weights[i], 0) for i in range(4)]
    return weight_copies(info, pieces, ATTN_SPLIT, targets, sems)


def mlp_copies(info, pieces, w_up, w_down, sems):
    targets = [(48 * i, 48, w_up, D * i) for i in range(4)] + [(192, 192, w_down, 0)]
    return weight_copies(info, pieces, MLP_SPLIT, targets, sems)


def start_all(groups):
    for group in groups:
        for copy in group:
            copy.start()


def wait_all(groups):
    for group in groups:
        for copy in group:
            copy.wait()


def matrix(ref):
    return ref[...].reshape(D, D)


ATTN_SCRATCH = [pltpu.VMEM((4, 4, 48, D), BF16)] * 4 + [pltpu.SemaphoreType.DMA((32,))]
MLP_SCRATCH = [
    pltpu.VMEM((4, 4, 48, FF), BF16),
    pltpu.VMEM((4, 4, 192, D), BF16),
    pltpu.SemaphoreType.DMA((40,)),
]


def grad_copies(info, sources, outs, sems):
    place, core = (info[0], info[1])
    copies = []
    for side in range(2):
        half = core if side == 0 else 1 - core
        column = pl.ds(pl.multiple_of(half * HALF, 128), HALF)
        for relative in range(4):
            source = sources(place ^ relative, column)
            copies.append(
                pltpu.make_async_copy(source, outs[side](relative), sems.at[4 * side + relative])
            )
    return copies


def stack_heads(value, low):
    zero = jnp.zeros_like(value)
    return jnp.concatenate([jnp.where(low, value, zero), jnp.where(low, zero, value)], axis=0)


def head_lanes():
    return lax.broadcasted_iota(jnp.int32, (LAT, 128), 1) < 64


def attend(item, q_ref, k_ref, v_ref, bias, o_ref, p_ref, group):
    low = head_lanes()
    for begin in range(0, PAIRS, group):
        scores = []
        for h in range(begin, begin + group):
            lanes = slice(128 * h, 128 * h + 128)
            queries = stack_heads(q_ref[item, :, lanes] * BF16(0.125), low)
            scores.append(dot(k_ref[item, :, lanes], queries, NT))
        soft = []
        for s in scores:
            if bias is not None:
                s = s + bias
            expo = jnp.exp(s - jnp.max(s, axis=0, keepdims=True))
            soft.append((expo * (1.0 / jnp.sum(expo, axis=0, keepdims=True))).astype(BF16))
        for h, p in zip(range(begin, begin + group), soft):
            lanes = slice(128 * h, 128 * h + 128)
            p_ref[item, h] = p
            o = dot(p, v_ref[item, :, lanes], TN)
            o_ref[item, :, lanes] = jnp.where(low, o[:LAT], o[LAT:]).astype(BF16)


def attend_back(item, q_ref, k_ref, v_ref, p_ref, do_ref, dq_ref, dk_ref, dv_ref, group):
    low = head_lanes()
    for begin in range(0, PAIRS, group):
        first = []
        for h in range(begin, begin + group):
            lanes = slice(128 * h, 128 * h + 128)
            queries = stack_heads(q_ref[item, :, lanes] * BF16(0.125), low)
            d_out = stack_heads(do_ref[item, :, lanes], low)
            p = p_ref[item, h]
            d_soft = dot(v_ref[item, :, lanes], d_out, NT)
            dv_ref[item, :, lanes] = dot(p, d_out).astype(BF16)
            first.append((queries, p, d_soft))
        for h, (queries, p, d_soft) in zip(range(begin, begin + group), first):
            lanes = slice(128 * h, 128 * h + 128)
            p = p.astype(F32)
            total = jnp.sum(d_soft * p, axis=0, keepdims=True)
            d_scores = (p * (d_soft - total)).astype(BF16)
            dk_ref[item, :, lanes] = dot(d_scores, queries).astype(BF16)
            dq = dot(d_scores, k_ref[item, :, lanes], TN)
            dq_ref[item, :, lanes] = (jnp.where(low, dq[:LAT], dq[LAT:]) * 0.125).astype(BF16)


def call(
    kernel, name, grid, in_specs, out_specs, out_shape, scratch, flops, moved, args, aliases=None
):
    return pl.pallas_call(
        kernel,
        grid=(grid,),
        in_specs=in_specs,
        out_specs=out_specs,
        out_shape=out_shape,
        scratch_shapes=scratch,
        name=name,
        input_output_aliases=aliases or {},
        compiler_params=pltpu.CompilerParams(vmem_limit_bytes=VMEM_BYTES),
        cost_estimate=pl.CostEstimate(
            flops=int(flops * SHARE), bytes_accessed=int(moved * SHARE), transcendentals=0
        ),
    )(*args)


def items_spec(*shape):
    return pl.BlockSpec((ITEMS,) + shape, lambda i: (i,) + (0,) * len(shape))


def rows_spec(width):
    return pl.BlockSpec((ROWS, width), lambda i: (i, 0))


def whole_spec(*shape):
    return pl.BlockSpec(shape, lambda i: (0,) * len(shape))


def shaped(shape, dtype):
    return jax.ShapeDtypeStruct(shape, dtype)


def cross_attn_kernel(info, lat, inp, bias, vec, *refs):
    pieces, (r, q, k, v, o, p), scratch = (refs[:10], refs[10:16], refs[16:])
    wq, wk, wv, wo, sems = scratch
    first = pl.program_id(0) == 0
    groups = attn_copies(info, pieces, (wq, wk, wv, wo), sems)

    @pl.when(first)
    def _():
        start_all(groups)

    z = lat[...].reshape(ROWS, D).astype(F32)
    hat, scale = norm_parts(z)
    zl = (hat * vec[0:1] + vec[3:4]).astype(BF16)
    xl = []
    for i in range(ITEMS):
        x = jnp.concatenate([inp[i].astype(F32), jnp.zeros((PAD - TOK, D), F32)], axis=0)
        hat, scale = norm_parts(x)
        xl.append((hat * vec[1:2] + vec[4:5]).astype(BF16))

    @pl.when(first)
    def _():
        wait_all(groups)

    q[...] = dot(zl, matrix(wq)).astype(BF16).reshape(ITEMS, LAT, D)
    for i in range(ITEMS):
        k[i] = dot(xl[i], matrix(wk)).astype(BF16)
        v[i] = dot(xl[i], matrix(wv)).astype(BF16)
        attend(i, q, k, v, jnp.broadcast_to(bias[i], (PAD, 256)), o, p, PAIRS)
    r[...] = z + dot(o[...].reshape(ROWS, D), matrix(wo))


def cross_attn_forward(info, lat, inp, bias, vec, pieces):
    n = lat.shape[0]
    steps = n // ITEMS
    return call(
        cross_attn_kernel,
        "cross_attn_forward",
        steps,
        [SMALL, items_spec(LAT, D), items_spec(TOK, D), items_spec(PAD, 1), whole_spec(16, D)]
        + [ANY] * 10,
        [pl.BlockSpec((ROWS, D), lambda i: (i, 0)), items_spec(LAT, D)]
        + [items_spec(PAD, D)] * 2
        + [items_spec(LAT, D), items_spec(PAIRS, PAD, 256)],
        [
            shaped((n * LAT, D), F32),
            shaped((n, LAT, D), BF16),
            shaped((n, PAD, D), BF16),
            shaped((n, PAD, D), BF16),
            shaped((n, LAT, D), BF16),
            shaped((n, PAIRS, PAD, 256), BF16),
        ],
        ATTN_SCRATCH,
        n * (4 * LAT * D * D + 4 * PAD * D * D + 24 * LAT * PAD * 256),
        n * (LAT * D * 10 + PAD * D * 6 + PAIRS * PAD * 512) + 8 * D * D,
        (info, lat, inp, bias, vec, *pieces),
    )


def self_attn_kernel(info, mid, vec, *refs):
    pieces, (r, q, k, v, o, p), scratch = (refs[:10], refs[10:16], refs[16:])
    wq, wk, wv, wo, sems = scratch
    first = pl.program_id(0) == 0
    groups = attn_copies(info, pieces, (wq, wk, wv, wo), sems)

    @pl.when(first)
    def _():
        start_all(groups)

    z = mid[...]
    hat, scale = norm_parts(z)
    zl = (hat * vec[6:7] + vec[8:9]).astype(BF16)

    @pl.when(first)
    def _():
        wait_all(groups)

    q[...] = dot(zl, matrix(wq)).astype(BF16).reshape(ITEMS, LAT, D)
    k[...] = dot(zl, matrix(wk)).astype(BF16).reshape(ITEMS, LAT, D)
    v[...] = dot(zl, matrix(wv)).astype(BF16).reshape(ITEMS, LAT, D)
    for i in range(ITEMS):
        attend(i, q, k, v, None, o, p, 2)
    r[...] = z + dot(o[...].reshape(ROWS, D), matrix(wo))


def self_attn_forward(info, mid, vec, pieces):
    n = mid.shape[0] // LAT
    steps = n // ITEMS
    rows = pl.BlockSpec((ROWS, D), lambda i: (i, 0))
    return call(
        self_attn_kernel,
        "self_attn_forward",
        steps,
        [SMALL, rows, whole_spec(16, D)] + [ANY] * 10,
        [rows] + [items_spec(LAT, D)] * 4 + [items_spec(PAIRS, LAT, 256)],
        [shaped((n * LAT, D), F32)]
        + [shaped((n, LAT, D), BF16)] * 4
        + [shaped((n, PAIRS, LAT, 256), BF16)],
        ATTN_SCRATCH,
        n * (8 * LAT * D * D + 24 * LAT * LAT * 256),
        n * (LAT * D * 16 + PAIRS * LAT * 512) + 8 * D * D,
        (info, mid, vec, *pieces),
    )


def cross_mlp_kernel(info, res, lat, keep, vec, *refs):
    pieces, (mid, e, slope), scratch = (refs[:10], refs[10:13], refs[13:])
    w_up, w_down, sems = scratch
    first = pl.program_id(0) == 0
    groups = mlp_copies(info, pieces, w_up, w_down, sems)

    @pl.when(first)
    def _():
        start_all(groups)

    r = res[...]
    z = lat[...].astype(F32)
    hat, scale = norm_parts(r)
    h = (hat * vec[2:3] + vec[5:6]).astype(BF16)

    @pl.when(first)
    def _():
        wait_all(groups)

    y = jnp.zeros((ROWS, D), F32)
    for j in range(4):
        lanes = slice(D * j, D * j + D)
        value, grad = gelu_both(dot(h, w_up[:, :, :, lanes].reshape(D, D)))
        value = value.astype(BF16)
        e[:, lanes] = value
        slope[:, lanes] = grad.astype(BF16)
        y += dot(value, w_down[j].reshape(D, D))
    mid[...] = z + keep[...] * ((r - z) + y)


def cross_mlp_forward(info, res, lat, keep, vec, pieces):
    m = res.shape[0]
    steps = m // ROWS
    spec = rows_spec
    return call(
        cross_mlp_kernel,
        "cross_mlp_forward",
        steps,
        [SMALL, spec(D), spec(D), spec(1), whole_spec(16, D)] + [ANY] * 10,
        [spec(D), spec(FF), spec(FF)],
        [shaped((m, D), F32), shaped((m, FF), BF16), shaped((m, FF), BF16)],
        MLP_SCRATCH,
        4 * m * D * FF,
        m * (D * 10 + FF * 4) + 4 * D * FF,
        (info, res, lat, keep, vec, *pieces),
    )


def mlp_grads_kernel(info, h, du, e, dy, keep, send, stage, sems):
    step = pl.program_id(0)

    @pl.when(step < 4)
    def _():
        stage[step] = dot(h[...], du[...], TN).astype(BF16)
        view = stage.at[step].reshape(4, 4, 48, D)
        rows = pl.ds(pl.multiple_of(step * 48, 16), 48)
        copies = grad_copies(
            info,
            lambda place, column: view.at[:, place, :, column],
            (lambda i: keep.at[i, :, rows], lambda i: send.at[i, :, rows]),
            sems.at[step],
        )
        for copy in copies:
            copy.start()

    def down_copies(tile, z):
        view = stage.at[tile].reshape(4, 192, D)
        return grad_copies(
            info,
            lambda place, column: view.at[place, :, column],
            (lambda i: keep.at[i, z, pl.ds(192, 192)], lambda i: send.at[i, z, pl.ds(192, 192)]),
            sems.at[tile],
        )

    @pl.when(step >= 4)
    def _():
        stage[step] = dot(e[...], dy[...], TN).astype(BF16)
        for copy in down_copies(step, step - 4):
            copy.start()

    @pl.when(step == 7)
    def _():
        for tile in range(8):
            for copy in down_copies(tile, 0):
                copy.wait()


def mlp_grads(name, info, h, du, e, dy):
    m = h.shape[0]
    return call(
        mlp_grads_kernel,
        name,
        8,
        [
            SMALL,
            whole_spec(m, D),
            pl.BlockSpec((m, D), lambda i: (0, jnp.minimum(i, 3))),
            pl.BlockSpec((m, D), lambda i: (0, jnp.maximum(i - 4, 0))),
            whole_spec(m, D),
        ],
        [ANY, ANY],
        [shaped((4, 4, 384, HALF), BF16)] * 2,
        [pltpu.VMEM((8, D, D), BF16), pltpu.SemaphoreType.DMA((8, 8))],
        4 * m * D * FF,
        m * (4 * D + 4 * FF) + 4 * D * FF,
        (info, h, du, e, dy),
    )


def self_mlp_kernel(info, res, cot, vec, *refs):
    pieces, outs, (w_up, w_down, sems) = (refs[:10], refs[10:17], refs[17:])
    out, total, da, d_vec, h_all, du_all, e_all = outs
    step = pl.program_id(0)
    first = step == 0
    groups = mlp_copies(info, pieces, w_up, w_down, sems)

    @pl.when(first)
    def _():
        start_all(groups)
        d_vec[...] = jnp.zeros_like(d_vec)

    r = res[...]
    dy = cot[...]
    hat, scale = norm_parts(r)
    gain = vec[7:8]
    h = (hat * gain + vec[9:10]).astype(BF16)
    h_all[...] = h

    @pl.when(first)
    def _():
        wait_all(groups)

    y = jnp.zeros((ROWS, D), F32)
    dh = jnp.zeros((ROWS, D), F32)
    for j in range(4):
        lanes = slice(D * j, D * j + D)
        up = w_up[:, :, :, lanes].reshape(D, D)
        down = w_down[j].reshape(D, D)
        value, slope = gelu_both(dot(h, up))
        value = value.astype(BF16)
        e_all[:, lanes] = value
        y += dot(value, down)
        du = (dot(dy, down, NT) * slope).astype(BF16)
        du_all[:, lanes] = du
        dh += dot(du, up, NT)
    out[...] = (r + y).astype(BF16)
    dr, d_gain, d_shift = norm_back(hat, scale, gain, dh)
    t = dy.astype(F32) + dr
    total[...] = t
    da[...] = t.astype(BF16)
    d_vec[0:1] += d_gain
    d_vec[1:2] += d_shift


def self_mlp(info, res, cot, vec, pieces):
    m = res.shape[0]
    steps = m // ROWS
    spec = rows_spec
    return call(
        self_mlp_kernel,
        "self_mlp",
        steps,
        [SMALL, spec(D), spec(D), whole_spec(16, D)] + [ANY] * 10,
        [spec(D), spec(D), spec(D), whole_spec(8, D), spec(D), spec(FF), spec(FF)],
        [
            shaped((m, D), BF16),
            shaped((m, D), F32),
            shaped((m, D), BF16),
            shaped((8, D), F32),
            shaped((m, D), BF16),
            shaped((m, FF), BF16),
            shaped((m, FF), BF16),
        ],
        MLP_SCRATCH,
        8 * m * D * FF,
        m * (D * 16 + 4 * FF) + 4 * D * FF,
        (info, res, cot, vec, *pieces),
    )


def cross_mlp_back_kernel(info, up_grad, keep_rows, res, slope, vec, *refs):
    pieces, outs, (w_up, w_down, sems) = (refs[:10], refs[10:16], refs[16:])
    total, da, d_vec, h_all, du_all, dy_all = outs
    first = pl.program_id(0) == 0
    groups = mlp_copies(info, pieces, w_up, w_down, sems)

    @pl.when(first)
    def _():
        start_all(groups)
        d_vec[...] = jnp.zeros_like(d_vec)

    g = up_grad[...]
    direct = keep_rows[...] * g
    dy = direct.astype(BF16)
    dy_all[...] = dy
    hat, scale = norm_parts(res[...])
    gain = vec[2:3]
    h_all[...] = (hat * gain + vec[5:6]).astype(BF16)

    @pl.when(first)
    def _():
        wait_all(groups)

    dh = jnp.zeros((ROWS, D), F32)
    for j in range(4):
        lanes = slice(D * j, D * j + D)
        d_act = dot(dy, w_down[j].reshape(D, D), NT)
        du = (d_act * slope[:, lanes].astype(F32)).astype(BF16)
        du_all[:, lanes] = du
        dh += dot(du, w_up[:, :, :, lanes].reshape(D, D), NT)
    dr, d_gain, d_shift = norm_back(hat, scale, gain, dh)
    total[...] = g + dr
    da[...] = (direct + dr).astype(BF16)
    d_vec[0:1] += d_gain
    d_vec[1:2] += d_shift


def cross_mlp_back(info, up_grad, keep_rows, res, slope, vec, pieces):
    m = res.shape[0]
    steps = m // ROWS
    spec = rows_spec
    return call(
        cross_mlp_back_kernel,
        "cross_mlp_back",
        steps,
        [SMALL, spec(D), spec(1), spec(D), spec(FF), whole_spec(16, D)] + [ANY] * 10,
        [spec(D), spec(D), whole_spec(8, D), spec(D), spec(FF), spec(D)],
        [
            shaped((m, D), F32),
            shaped((m, D), BF16),
            shaped((8, D), F32),
            shaped((m, D), BF16),
            shaped((m, FF), BF16),
            shaped((m, D), BF16),
        ],
        MLP_SCRATCH,
        4 * m * D * FF,
        m * (D * 18 + 4 * FF) + 4 * D * FF,
        (info, up_grad, keep_rows, res, slope, vec, *pieces),
    )


def attn_grads_kernel(pairs, counts, info, *refs):
    few = len(counts)
    stage, last, in_sems, sems = refs[-4:]
    held = refs[-4 - few : -4]
    keep, send = refs[-6 - few : -4 - few]
    arrays, vectors = (refs[:few], refs[few : -6 - few])
    step = pl.program_id(0)
    loads = [pltpu.make_async_copy(a, b, in_sems.at[i]) for i, (a, b) in enumerate(zip(arrays, held))]

    @pl.when(step == 0)
    def _():
        for load in loads:
            load.start()

    def copies_of(tile):
        view = stage.at[tile].reshape(4, 4, 48, D)
        rows = pl.ds(48 * tile, 48)
        return grad_copies(
            info,
            lambda place, column: view.at[:, place, :, column],
            (lambda i: keep.at[i, :, rows], lambda i: send.at[i, :, rows]),
            sems.at[tile],
        )

    def last_copies():
        rows = pl.ds(192, EXTRA)
        return grad_copies(
            info,
            lambda place, column: last.at[:, :, column],
            (lambda i: keep.at[i, :, rows], lambda i: send.at[i, :, rows]),
            sems.at[4],
        )

    waited = set()
    for tile, pair in enumerate(pairs):
        fresh = [i for i in pair if i not in waited]
        waited.update(fresh)

        @pl.when(step == tile)
        def _():
            for i in fresh:
                loads[i].wait()
            left, right = (held[i][...].reshape(-1, D) for i in pair)
            stage[tile] = dot(left, right, TN).astype(BF16)
            for copy in copies_of(tile):
                copy.start()
            if tile == 0 and vectors:
                attn_vec, mlp_vec, self_vec, own_vec = vectors
                rows = [attn_vec[0:2], mlp_vec[0:1], attn_vec[2:4], mlp_vec[1:2]]
                rows += [self_vec[0:1], own_vec[0:1], self_vec[1:2], own_vec[1:2]]
                rows.append(jnp.zeros((EXTRA - 10, D), F32))
                rows = jnp.concatenate(rows, axis=0).astype(BF16)
                last[...] = jnp.broadcast_to(rows[None], (4, EXTRA, D))
                for copy in last_copies():
                    copy.start()
            if tile == 3:
                if vectors:
                    for copy in last_copies():
                        copy.wait()
                for i in range(4):
                    for copy in copies_of(i):
                        copy.wait()


def attn_grads(name, info, arrays, pairs, vectors=()):
    rows = 192 + (EXTRA if vectors else 0)
    counts = [a.size // D for a in arrays]
    flops = sum(2 * counts[i] * D * D for i, _ in pairs)
    return call(
        functools.partial(attn_grads_kernel, pairs, counts),
        name,
        4,
        [SMALL] + [ANY] * len(arrays) + [whole_spec(8, D)] * len(vectors),
        [ANY, ANY],
        [shaped((4, 4, rows, HALF), BF16)] * 2,
        [pltpu.VMEM(a.shape, BF16) for a in arrays]
        + [
            pltpu.VMEM((4, D, D), BF16),
            pltpu.VMEM((4, EXTRA, D), BF16),
            pltpu.SemaphoreType.DMA((len(arrays),)),
            pltpu.SemaphoreType.DMA((5, 8)),
        ],
        flops,
        sum(counts) * D * 2 + 8 * D * D,
        (info, *arrays, *vectors),
    )


def self_attn_back_kernel(info, total, da, q, k, v, p, mid, vec, *refs):
    pieces, (d_mid, d_vec, zl, dq, dk, dv), scratch = (refs[:10], refs[10:16], refs[16:])
    wq, wk, wv, wo, sems, do_rows = scratch
    first = pl.program_id(0) == 0
    groups = attn_copies(info, pieces, (wq, wk, wv, wo), sems)

    @pl.when(first)
    def _():
        start_all(groups)
        d_vec[...] = jnp.zeros_like(d_vec)

    hat, scale = norm_parts(mid[...])
    gain = vec[6:7]
    zl[...] = (hat * gain + vec[8:9]).astype(BF16).reshape(ITEMS, LAT, D)

    @pl.when(first)
    def _():
        wait_all(groups)

    do_rows[...] = dot(da[...], matrix(wo), NT).astype(BF16).reshape(ITEMS, LAT, D)
    for i in range(ITEMS):
        attend_back(i, q, k, v, p, do_rows, dq, dk, dv, 3)
    dz = dot(dq[...].reshape(ROWS, D), matrix(wq), NT)
    dz += dot(dk[...].reshape(ROWS, D), matrix(wk), NT)
    dz += dot(dv[...].reshape(ROWS, D), matrix(wv), NT)
    dz, d_gain, d_shift = norm_back(hat, scale, gain, dz)
    d_mid[...] = total[...] + dz
    d_vec[0:1] += d_gain
    d_vec[1:2] += d_shift


def self_attn_back(info, total, da, q, k, v, p, mid, vec, pieces):
    m = total.shape[0]
    n = m // LAT
    steps = m // ROWS
    spec = rows_spec
    return call(
        self_attn_back_kernel,
        "self_attn_back",
        steps,
        [SMALL, spec(D), spec(D)]
        + [items_spec(LAT, D)] * 3
        + [items_spec(PAIRS, LAT, 256), spec(D), whole_spec(16, D)]
        + [ANY] * 10,
        [spec(D), whole_spec(8, D)] + [items_spec(LAT, D)] * 4,
        [shaped((m, D), F32), shaped((8, D), F32)] + [shaped((n, LAT, D), BF16)] * 4,
        ATTN_SCRATCH + [pltpu.VMEM((ITEMS, LAT, D), BF16)],
        n * (8 * LAT * D * D + 48 * LAT * LAT * 256),
        m * D * 32 + 8 * D * D,
        (info, total, da, q, k, v, p, mid, vec, *pieces),
    )


def cross_attn_back_kernel(later, info, total, da, q, k, v, p, lat, inp, vec, *refs):
    pieces, refs = (refs[:10], refs[10:])
    if later:
        before, refs = (refs[0], refs[8:])
    (d_vec, d_lat, d_inp, zl, dq, xl, dk, dv), scratch = (refs[:8], refs[8:])
    wq, wk, wv, wo, sems, do_rows = scratch
    first = pl.program_id(0) == 0
    groups = attn_copies(info, pieces, (wq, wk, wv, wo), sems)

    @pl.when(first)
    def _():
        start_all(groups)
        d_vec[...] = before[...] if later else jnp.zeros_like(d_vec)

    hat, scale = norm_parts(lat[...].astype(F32))
    gain = vec[0:1]
    zl[...] = (hat * gain + vec[3:4]).astype(BF16).reshape(ITEMS, LAT, D)

    @pl.when(first)
    def _():
        wait_all(groups)

    do_rows[...] = dot(da[...], matrix(wo), NT).astype(BF16).reshape(ITEMS, LAT, D)
    for i in range(ITEMS):
        attend_back(i, q, k, v, p, do_rows, dq, dk, dv, 3)
        x = jnp.concatenate([inp[i].astype(F32), jnp.zeros((PAD - TOK, D), F32)], axis=0)
        x_hat, x_scale = norm_parts(x)
        x_gain = vec[1:2]
        xl[i] = (x_hat * x_gain + vec[4:5]).astype(BF16)
        dx = dot(dk[i], matrix(wk), NT) + dot(dv[i], matrix(wv), NT)
        dx, d_gain, d_shift = norm_back(x_hat, x_scale, x_gain, dx)
        d_inp[i] = dx[:TOK]
        d_vec[1:2] += d_gain
        d_vec[3:4] += d_shift
    dz = dot(dq[...].reshape(ROWS, D), matrix(wq), NT)
    dz, d_gain, d_shift = norm_back(hat, scale, gain, dz)
    d_lat[...] = total[...] + dz
    d_vec[0:1] += d_gain
    d_vec[2:3] += d_shift


def cross_attn_back(part, parts, before, info, total, da, q, k, v, p, lat, inp, vec, pieces):
    m = total.shape[0]
    n = m // LAT
    steps = n // ITEMS // parts
    begin = part * steps

    def item(*shape):
        return pl.BlockSpec((ITEMS,) + shape, lambda i: (begin + i,) + (0,) * len(shape))

    rows = pl.BlockSpec((ROWS, D), lambda i: (begin + i, 0))
    in_specs = [SMALL, rows, rows, item(LAT, D), item(PAD, D), item(PAD, D)]
    in_specs += [item(PAIRS, PAD, 256), rows, item(TOK, D), whole_spec(16, D)] + [ANY] * 10
    aliases = {}
    if before:
        aliases = {len(in_specs) + i: i for i in range(1, 8)}
        in_specs += [whole_spec(8, D)] + [ANY] * 7
    return call(
        functools.partial(cross_attn_back_kernel, bool(before)),
        f"cross_attn_back_{part}",
        steps,
        in_specs,
        [whole_spec(8, D), rows, item(TOK, D)] + [item(LAT, D)] * 2 + [item(PAD, D)] * 3,
        [shaped((8, D), F32), shaped((m, D), F32), shaped((n, TOK, D), F32)]
        + [shaped((n, LAT, D), BF16)] * 2
        + [shaped((n, PAD, D), BF16)] * 3,
        ATTN_SCRATCH + [pltpu.VMEM((ITEMS, LAT, D), BF16)],
        (n * (4 * LAT * D * D + 4 * PAD * D * D + 48 * LAT * PAD * 256)) // parts,
        (m * D * 20 + n * PAD * (D * 16 + PAIRS * 512)) // parts + 8 * D * D,
        (info, total, da, q, k, v, p, lat, inp, vec, *pieces, *(before or ())),
        aliases,
    )


def key_valid(frame_counts, patch_mask, text_mask):
    places = jnp.arange(VIDEO, dtype=jnp.int32)
    video_ok = (places[None, :] // P_SIZE < frame_counts[:, None]) & (
        (patch_mask == 1) | (places[None, :] % P_SIZE == 0)
    )
    text_places = jnp.arange(text_mask.shape[1], dtype=jnp.int32)
    text_ok = (text_mask == 1) | (text_places[None, :] == 0)
    return jnp.concatenate([video_ok, text_ok], axis=1)


class Grid:
    def __init__(self):
        self.core = lax.axis_index("fsdp")
        self.place = lax.rem(lax.axis_index("dp"), 4)
        chips = range(16)
        self.to_core = [(2 * i + c, 2 * i + 1 - c) for i in chips for c in range(2)]
        self.to_x = [(2 * i + c, 2 * (i ^ 1) + c) for i in chips for c in range(2)]
        self.to_y = [(2 * i + c, 2 * (i ^ 2) + c) for i in chips for c in range(2)]
        self.columns = [[4 * z + i for z in range(4)] for i in range(4)]

    def swap_core(self, value):
        return lax.ppermute(value, AX, self.to_core)

    def swap_x(self, value):
        return lax.ppermute(value, AX, self.to_x)

    def swap_y(self, value):
        return lax.ppermute(value, AX, self.to_y)

    def by_core(self, first, second):
        return jnp.where(self.core == 0, first, second)

    def info(self):
        return jnp.stack([self.place, self.core]).astype(jnp.int32)

    def gather_z(self, unit):
        return lax.all_gather(unit, "dp", axis=0, axis_index_groups=self.columns)

    def near(self, own):
        return (self.swap_x(own), self.swap_y(own))

    def far(self, near, split):
        return (self.swap_x(near[1][:, :split]), self.swap_y(near[0][:, split:]))

    def both_cores(self, own, near, far):
        mine = (own,) + near + far
        return mine + tuple((self.swap_core(piece) for piece in mine))


    def diagonal(self, keep, arrived, split):
        return (keep[3, :, :split] + arrived[3, :, :split], keep[3, :, split:] + arrived[3, :, split:])

    def send_diagonal(self, sums):
        return (self.swap_x(sums[0]), self.swap_y(sums[1]))

    def sides(self, keep, arrived, first, second):
        for_x = jnp.concatenate([jnp.zeros_like(first), second], axis=1)
        for_y = jnp.concatenate([first, jnp.zeros_like(second)], axis=1)
        return (keep[1] + arrived[1] + for_x, keep[2] + arrived[2] + for_y)

    def send_sides(self, sums):
        return (self.swap_x(sums[0]), self.swap_y(sums[1]))

    def own_column(self, keep, arrived, sides):
        return keep[0] + arrived[0] + sides[0] + sides[1]

    def scatter_z(self, own):
        return lax.psum_scatter(own, "dp", scatter_dimension=0, axis_index_groups=self.columns)

    def to_rows(self, parts):
        parts = [part.astype(F32).reshape(part.shape[0], 2, -1, HALF) for part in parts]
        keep, send = [
            jnp.concatenate([part[:, i].reshape(-1, HALF) for part in parts]) for i in range(2)
        ]
        keep, send = (self.by_core(keep, send), self.by_core(send, keep))
        arrived = self.swap_core(send)
        return jnp.concatenate([self.by_core(keep, arrived), self.by_core(arrived, keep)], axis=1)


def pack_rows(grid, mine, theirs, axis):
    return jnp.concatenate([grid.by_core(mine, theirs), grid.by_core(theirs, mine)], axis=axis)


def shard_of_block(qkv, w_out, w_up, w_down):
    depth = w_out.shape[0]
    attn = jnp.concatenate([qkv, w_out[None]], axis=0)
    up = w_up.reshape(depth, 4, D).transpose(1, 0, 2)
    return jnp.concatenate([attn.reshape(-1, D), up.reshape(-1, D), w_down], axis=0)


def units_of_block(grid, mine, theirs):
    attn = pack_rows(grid, mine[:96].reshape(4, 24, HALF), theirs[:96].reshape(4, 24, HALF), 1)
    up = pack_rows(grid, mine[96:192].reshape(4, 24, HALF), theirs[96:192].reshape(4, 24, HALF), 1)
    down = pack_rows(grid, mine[192:], theirs[192:], 0)
    return (attn.reshape(192, HALF), jnp.concatenate([up.reshape(192, HALF), down], axis=0))


def gather_planned(grid, cross, own_block):
    low = jnp.concatenate([cross[0], cross[1], own_block[0], own_block[1]], axis=0)
    low = jnp.pad(low, ((0, EXTRA - 10), (0, HALF - 24)))
    shard = jnp.concatenate([shard_of_block(*cross[2:]), shard_of_block(*own_block[2:])], axis=0)
    left, right = (shard[:, :HALF], shard[:, HALF:])
    keep, send = (grid.by_core(left, right), grid.by_core(right, left))
    arrived = grid.swap_core(jnp.concatenate([send, low], axis=0))
    cross_attn, cross_mlp = units_of_block(grid, keep[:288], arrived[:288])
    self_attn, self_mlp = units_of_block(grid, keep[288:], arrived[288:576])
    vectors = pack_rows(grid, low[:, :24], arrived[576:, :24], 1)
    vectors = jnp.pad(vectors, ((0, 0), (0, HALF - 48)))
    cross_attn = jnp.concatenate([cross_attn, vectors], axis=0)
    own = grid.gather_z(jnp.concatenate([self_attn, self_mlp], axis=0))
    return (grid.gather_z(cross_attn), grid.gather_z(cross_mlp), own[:, :192], own[:, 192:])


def gathered_vectors(grid, pieces):
    rows = [piece[:, 192:, :48] for piece in pieces[:3]]
    rows.append(pieces[4][:, 192 - ATTN_SPLIT :, :48])
    odd = lax.rem(grid.place, 2) == 1
    rows = [jnp.where(odd, rows[i ^ 1], rows[i]) for i in range(4)]
    rows = [jnp.where(grid.place >= 2, rows[i ^ 2], rows[i]) for i in range(4)]
    return jnp.stack(rows, axis=1).transpose(2, 0, 1, 3).reshape(EXTRA, D).astype(F32)


def finish_attn(grid, total):
    parts = [total[:192].reshape(4, 48, HALF)]
    if total.shape[0] > 192:
        parts.append(jnp.broadcast_to(total[192:], (2, EXTRA, HALF)).reshape(1, 2 * EXTRA, HALF))
    rows = grid.to_rows(parts)
    matrices = rows[:96].reshape(4, 24, D)
    return (matrices[:3], matrices[3], rows[96:])


def finish_mlp(grid, total):
    rows = grid.to_rows([total[:192].reshape(4, 48, HALF), total[192:].reshape(1, 192, HALF)])
    return (rows[:96].reshape(4, 24, D).transpose(1, 0, 2).reshape(24, FF), rows[96:])


def unit_pieces(unit, split):
    pieces = ()
    for half in (slice(0, HALF), slice(HALF, D)):
        pieces += tuple((unit[:, i, :, half] for i in range(3)))
        pieces += (unit[:, 3, :split, half], unit[:, 3, split:, half])
    return pieces


def gather_plain(cross, own_block):
    gather = functools.partial(lax.all_gather, axis_name=AX, tiled=True)
    vectors = jnp.concatenate([cross[0], cross[1], own_block[0], own_block[1]], axis=0)
    vectors = jnp.pad(gather(vectors, axis=1), ((0, EXTRA - 10), (0, 0))).astype(F32)
    units = []
    for block in (cross, own_block):
        qkv, w_out, w_up, w_down = block[2:]
        matrices = list(gather(qkv, axis=1)) + [gather(w_out, axis=0)]
        attn = jnp.concatenate([w.reshape(4, 4, 48, D) for w in matrices], axis=2)
        up = gather(w_up, axis=0).reshape(4, 4, 48, 4, D).transpose(0, 1, 3, 2, 4)
        down = gather(w_down, axis=0).reshape(4, 4, 192, D)
        units.append(unit_pieces(attn, ATTN_SPLIT))
        mlp = jnp.concatenate([up.reshape(4, 4, 192, D), down], axis=2)
        units.append(unit_pieces(mlp, MLP_SPLIT))
    return (vectors,) + tuple(units)


def whole_terms(terms):
    return jnp.concatenate(terms, axis=-1).transpose(1, 0, 2, 3).astype(F32)


def reduce_plain_attn(terms):
    scatter = functools.partial(lax.psum_scatter, axis_name=AX, tiled=True)
    unit = whole_terms(terms)
    matrices = [unit[:, :, 48 * i : 48 * i + 48].reshape(D, D) for i in range(4)]
    qkv = scatter(jnp.stack(matrices[:3]), scatter_dimension=1)
    vectors = scatter(unit[0, 0, 192:], scatter_dimension=1) if unit.shape[2] > 192 else None
    return (qkv, scatter(matrices[3], scatter_dimension=0), vectors)


def reduce_plain_mlp(terms):
    scatter = functools.partial(lax.psum_scatter, axis_name=AX, tiled=True)
    unit = whole_terms(terms)
    up = unit[:, :, :192].reshape(4, 4, 4, 48, D).transpose(0, 1, 3, 2, 4).reshape(D, FF)
    down = unit[:, :, 192:].reshape(FF, D)
    return (scatter(up, scatter_dimension=0), scatter(down, scatter_dimension=0))


def after(value, *events):
    return jax.tree.map(lambda x: lax.optimization_barrier((x, events))[0], value)


def planned_steps(args, cross, own_block):
    lat_rows, cot_rows, latents, inputs, bias, keeping = args
    grid = Grid()
    info = grid.info()
    ca_own, cm_own, sa_own, sm_own = gather_planned(grid, cross, own_block)

    ca_near = grid.near(ca_own)
    ca_far = grid.far(ca_near, ATTN_SPLIT)
    ca = grid.both_cores(ca_own, ca_near, ca_far)
    vec = gathered_vectors(grid, ca)
    cm_own = after(cm_own, ca_far)
    cm_near = grid.near(cm_own)
    res, q, k, v, o, p = cross_attn_forward(info, latents, inputs, bias, vec, ca)
    cm_near = after(cm_near, res)
    cm_far = grid.far(cm_near, MLP_SPLIT)
    cm = grid.both_cores(cm_own, cm_near, cm_far)
    sa_own = after(sa_own, cm_far)
    sa_near = grid.near(sa_own)
    mid, e, slope = cross_mlp_forward(info, res, lat_rows, keeping, vec, cm)
    sa_near = after(sa_near, mid)
    sa_far = grid.far(sa_near, ATTN_SPLIT)
    sm_near = grid.near(after(sm_own, sa_far))
    sa = grid.both_cores(sa_own, sa_near, sa_far)
    own_res, sq, sk, sv, so, sp = self_attn_forward(info, mid, vec, sa)
    sm_far = grid.far(after(sm_near, own_res), MLP_SPLIT)
    sm = grid.both_cores(sm_own, sm_near, sm_far)
    result, total, da, own_vec, h, du, own_e = self_mlp(info, own_res, cot_rows, vec, sm)
    a_keep, a_send = mlp_grads("self_mlp_grads", info, h, du, own_e, cot_rows)
    total, da = after((total, da), a_send)
    a_in = grid.swap_core(a_send)
    d_mid, self_vec, zl, dq, dk, dv = self_attn_back(info, total, da, sq, sk, sv, sp, mid, vec, sa)
    self_arrays = (zl, dq, dk, dv, so, da.reshape(so.shape))

    a_in = after(a_in, d_mid)
    a_diag = grid.diagonal(a_keep, a_in, MLP_SPLIT)
    d_mid = after(d_mid, a_diag)
    a_far = grid.send_diagonal(a_diag)
    total, da, mlp_vec, h, du, dy = cross_mlp_back(info, d_mid, keeping, res, slope, vec, cm)

    a_sides = grid.sides(a_keep, a_in, *after(a_far, total))
    h = after(h, a_sides)
    a_near = grid.send_sides(a_sides)
    c_keep, c_send = mlp_grads("cross_mlp_grads", info, h, du, e, dy)
    self_arrays = after(self_arrays, c_send)
    c_in = grid.swap_core(c_send)
    pairs = ((0, 1), (0, 2), (0, 3), (4, 5))
    b_keep, b_send = attn_grads("self_attn_grads", info, self_arrays, pairs)

    c_in = after(c_in, b_send)
    c_diag = grid.diagonal(c_keep, c_in, MLP_SPLIT)
    a_sum = grid.own_column(a_keep, a_in, after(a_near, b_send))
    total = after(total, c_diag, a_sum)
    a_sum = grid.scatter_z(a_sum)
    c_far = grid.send_diagonal(c_diag)
    b_in = grid.swap_core(after(b_send, c_diag))
    back = (da, q, k, v, p, lat_rows, inputs, vec, ca)
    half = cross_attn_back(0, 2, None, info, total, *back)

    b_in, c_far = after((b_in, c_far), half[0])
    c_sides = grid.sides(c_keep, c_in, *c_far)
    c_near = grid.send_sides(c_sides)
    b_diag = grid.diagonal(b_keep, b_in, ATTN_SPLIT)
    b_far = grid.send_diagonal(b_diag)
    total = after(total, c_sides, b_diag)
    cross_vec, d_lat, d_inp, zl, dq, xl, dk, dv = cross_attn_back(1, 2, half, info, total, *back)

    b_far, c_near = after((b_far, c_near), cross_vec)
    b_sides = grid.sides(b_keep, b_in, *b_far)
    c_sum = grid.own_column(c_keep, c_in, c_near)
    zl = after(zl, b_sides, c_sum)
    b_near = grid.send_sides(b_sides)
    c_sum = grid.scatter_z(c_sum)
    pairs = ((0, 1), (2, 3), (2, 4), (5, 6))
    arrays = (zl, dq, xl, dk, dv, o, da.reshape(o.shape))
    vectors = (cross_vec, mlp_vec, self_vec, own_vec)
    d_keep, d_send = attn_grads("cross_attn_grads", info, arrays, pairs, vectors)

    d_send = after(d_send, b_near, a_sum)
    d_in = grid.swap_core(d_send)
    d_diag = grid.diagonal(d_keep, d_in, ATTN_SPLIT)
    d_far = grid.send_diagonal(d_diag)
    b_sum = grid.scatter_z(grid.own_column(b_keep, b_in, after(b_near, d_diag)))
    d_far = after(d_far, b_near)
    d_near = grid.send_sides(grid.sides(d_keep, d_in, *d_far))
    d_near = after(d_near, b_sum)
    d_sum = grid.scatter_z(grid.own_column(d_keep, d_in, d_near))

    s_up, s_down = finish_mlp(grid, a_sum)
    s_qkv, s_out, _ = finish_attn(grid, b_sum)
    c_up, c_down = finish_mlp(grid, c_sum)
    c_qkv, c_out, vectors = finish_attn(grid, d_sum)
    at = 24 * (2 * lax.axis_index("dp") + grid.core)
    vectors = lax.dynamic_slice_in_dim(vectors, at, 24, 1)
    cross_grads = (vectors[0:3], vectors[3:6], c_qkv, c_out, c_up, c_down)
    self_grads = (vectors[6:8], vectors[8:10], s_qkv, s_out, s_up, s_down)
    return ((result, d_lat, d_inp), cross_grads + self_grads)


def plain_steps(args, cross, own_block):
    lat_rows, cot_rows, latents, inputs, bias, keeping = args
    info = jnp.zeros((2,), jnp.int32)
    vec, ca, cm, sa, sm = gather_plain(cross, own_block)
    res, q, k, v, o, p = cross_attn_forward(info, latents, inputs, bias, vec, ca)
    mid, e, slope = cross_mlp_forward(info, res, lat_rows, keeping, vec, cm)
    own_res, sq, sk, sv, so, sp = self_attn_forward(info, mid, vec, sa)
    result, total, da, own_vec, h, du, own_e = self_mlp(info, own_res, cot_rows, vec, sm)
    a_terms = mlp_grads("self_mlp_grads", info, h, du, own_e, cot_rows)
    d_mid, self_vec, zl, dq, dk, dv = self_attn_back(info, total, da, sq, sk, sv, sp, mid, vec, sa)
    pairs = ((0, 1), (0, 2), (0, 3), (4, 5))
    arrays = (zl, dq, dk, dv, so, da.reshape(so.shape))
    b_terms = attn_grads("self_attn_grads", info, arrays, pairs)
    total, da, mlp_vec, h, du, dy = cross_mlp_back(info, d_mid, keeping, res, slope, vec, cm)
    c_terms = mlp_grads("cross_mlp_grads", info, h, du, e, dy)
    cross_vec, d_lat, d_inp, zl, dq, xl, dk, dv = cross_attn_back(
        0, 1, None, info, total, da, q, k, v, p, lat_rows, inputs, vec, ca
    )
    pairs = ((0, 1), (2, 3), (2, 4), (5, 6))
    arrays = (zl, dq, xl, dk, dv, o, da.reshape(o.shape))
    vectors = (cross_vec, mlp_vec, self_vec, own_vec)
    d_terms = attn_grads("cross_attn_grads", info, arrays, pairs, vectors)
    s_up, s_down = reduce_plain_mlp(a_terms)
    s_qkv, s_out, _ = reduce_plain_attn(b_terms)
    c_up, c_down = reduce_plain_mlp(c_terms)
    c_qkv, c_out, vectors = reduce_plain_attn(d_terms)
    cross_grads = (vectors[0:3], vectors[3:6], c_qkv, c_out, c_up, c_down)
    self_grads = (vectors[6:8], vectors[8:10], s_qkv, s_out, s_up, s_down)
    return ((result, d_lat, d_inp), cross_grads + self_grads)


def local(
    planned,
    latents,
    inputs,
    frame_counts,
    patch_mask,
    text_mask,
    drop_mask,
    cross_gains,
    cross_shifts,
    cross_qkv,
    cross_out,
    cross_up,
    cross_down,
    self_gains,
    self_shifts,
    self_qkv,
    self_out,
    self_up,
    self_down,
    cotangent,
):
    n = latents.shape[0]
    usable = key_valid(frame_counts, patch_mask, text_mask)
    usable = jnp.pad(usable, ((0, 0), (0, PAD - TOK)))
    bias = jnp.where(usable, 0.0, -1e30).astype(F32)[:, :, None]
    keeping = jnp.repeat((1 - drop_mask).astype(F32), LAT)[:, None]
    lat_rows = latents.reshape(n * LAT, D)
    cot_rows = cotangent.reshape(n * LAT, D)
    cross = (cross_gains, cross_shifts, cross_qkv, cross_out, cross_up, cross_down)
    own_block = (self_gains, self_shifts, self_qkv, self_out, self_up, self_down)
    args = (lat_rows, cot_rows, latents, inputs, bias, keeping)
    if planned:
        results, grads = planned_steps(args, cross, own_block)
    else:
        results, grads = plain_steps(args, cross, own_block)
    result, d_lat, d_inp = results
    return (result.reshape(n, LAT, D), d_lat.reshape(n, LAT, D), d_inp) + grads


def solution(mesh):
    planned = mesh.shape["dp"] == 16 and mesh.shape["fsdp"] == 2
    in_specs = (
        P(("dp", "fsdp"), None, None),
        P(("dp", "fsdp"), None, None),
        P(("dp", "fsdp")),
        P(("dp", "fsdp"), None),
        P(("dp", "fsdp"), None),
        P(("dp", "fsdp")),
        P(None, ("dp", "fsdp")),
        P(None, ("dp", "fsdp")),
        P(None, ("dp", "fsdp"), None),
        P(("dp", "fsdp"), None),
        P(("dp", "fsdp"), None),
        P(("dp", "fsdp"), None),
        P(None, ("dp", "fsdp")),
        P(None, ("dp", "fsdp")),
        P(None, ("dp", "fsdp"), None),
        P(("dp", "fsdp"), None),
        P(("dp", "fsdp"), None),
        P(("dp", "fsdp"), None),
        P(("dp", "fsdp"), None, None),
    )
    out_specs = (
        P(("dp", "fsdp"), None, None),
        P(("dp", "fsdp"), None, None),
        P(("dp", "fsdp"), None, None),
        P(None, ("dp", "fsdp")),
        P(None, ("dp", "fsdp")),
        P(None, ("dp", "fsdp"), None),
        P(("dp", "fsdp"), None),
        P(("dp", "fsdp"), None),
        P(("dp", "fsdp"), None),
        P(None, ("dp", "fsdp")),
        P(None, ("dp", "fsdp")),
        P(None, ("dp", "fsdp"), None),
        P(("dp", "fsdp"), None),
        P(("dp", "fsdp"), None),
        P(("dp", "fsdp"), None),
    )
    return jax.shard_map(
        functools.partial(local, planned), mesh=mesh, in_specs=in_specs, out_specs=out_specs, check_vma=False)
```

time: 1660 us -> 539 us (0.32)
  waiting for transfers between devices: 986 us -> 141 us
  matrix products: 329 us -> 0 us
  Pallas kernels: 0 us -> 246 us
  blocking collectives: 195 us -> 24 us
  starting transfers between devices: 1.42 us -> 39.9 us
  local copies, waits for them, and re-layouts: 50 us -> 22.6 us
  other arithmetic: 70.1 us -> 45.8 us
    reduce_scatter x8 -> x4, waiting for transfers between devices: 793 us -> 31.4 us  [scatter_z(): lax.psum_scatter(own, 'dp', scatter_dimension=0, axis_index_groups=self.c...]
    dot_general x48 -> x0, matrix products: 329 us -> none  [the longest x12 92 us: project(): jnp.einsum('bld,de->ble', left, weight, preferred_element_type=jnp.float32)]
    pallas_call x0 -> x12, Pallas kernels: none -> 246 us  [call(): pl.pallas_call(kernel, grid=(grid,), in_specs=in_specs, out_specs=out_spe...]
    all_gather x8 -> x2, waiting for transfers between devices: 188 us -> 0.02 us  [gather_z(): return lax.all_gather(unit, 'dp', axis=0, axis_index_groups=self.columns)]
    all_gather x4 -> x1, blocking collectives: 155 us -> 24 us  [gather_z(): return lax.all_gather(unit, 'dp', axis=0, axis_index_groups=self.columns)]
    ppermute x0 -> x61, waiting for transfers between devices: none -> 110 us  [the longest x16 53 us: swap_x(): return lax.ppermute(value, AX, self.to_x)]
    unnamed x1 -> x0, blocking collectives: 40.5 us -> none
    ppermute x0 -> x61, starting transfers between devices: none -> 39.6 us  [the longest x16 18.9 us: swap_y(): return lax.ppermute(value, AX, self.to_y)]
  transfers between devices with their start and end apart: 16 -> 67, of which waited for: 11 -> 29; matrix products, arithmetic and copies ran while one was open for 20% -> 8% of each run, Pallas kernels for 0% -> 33%
where the time goes in v2:
time: 539 us; the launch traced here: 535 us
  Pallas kernels  246 us (46%)
  waiting for transfers between devices  141 us (26%)
  other arithmetic  45.8 us (8%)
  starting transfers between devices  39.9 us (7%)
  blocking collectives  24 us (4%)
  local copies, waits for them, and re-layouts  22.6 us (4%)
  between operations  15.4 us (3%)
    pallas_call x12, Pallas kernels, call(): pl.pallas_call(kernel, grid=(grid,), in_specs=in_specs, out_specs=out_spe...  246 us
    ppermute x16, waiting for transfers between devices, swap_x(): return lax.ppermute(value, AX, self.to_x)  53 us
    ppermute x16, waiting for transfers between devices, swap_y(): return lax.ppermute(value, AX, self.to_y)  44.7 us
    reduce_scatter x4, waiting for transfers between devices, scatter_z(): lax.psum_scatter(own, 'dp', scatter_dimension=0, axis_index_groups=self.c...  31.4 us
    all_gather x1, blocking collectives, gather_z(): return lax.all_gather(unit, 'dp', axis=0, axis_index_groups=self.columns)  24 us
    ppermute x16, starting transfers between devices, swap_y(): return lax.ppermute(value, AX, self.to_y)  18.9 us
    ppermute x16, starting transfers between devices, swap_x(): return lax.ppermute(value, AX, self.to_x)  15.3 us
    add x4, other arithmetic, sides(): return (keep[1] + arrived[1] + for_x, keep[2] + arrived[2] + for_y)  13.1 us
  transfers between devices with their start and end apart: 67, of which 29 were waited for; matrix products, arithmetic and copies ran while one was open for 8% of the time, Pallas kernels for 33%

profile of v2, /device:TPU:0, one launch (start us, length us, event | category | flops | bytes accessed | tf_op | source)
XLA Modules:
  0.0 535.3 jit_solution(3259526984802826915)
XLA Ops:
  14.9 24.0 %all-gather = bf16[832,384]{1,0:T(8,128)(2,1)S(1)} all-gather(bf16[208,384]{1,0:T(8,128)(2,1)S(1)} %pad_maximum_fusion.11), channel_id=2, replica_groups={{0,8,16,24},{2,10,18,26},{4,12,20,28},{6,14,22,30},{1,9,17,25},{3,11,19..., dimensions={0}, use_global_device_ids=true | all-gather | bytes 798720 | tf_op jit(solution)/shard_map/all_gather | solution.py:821
  42.0 9.3 %collective-permute-done.1.refs_1_ = bf16[4,208,384]{2,1,0:T(8,128)(2,1)S(1)} collective-permute-done((bf16[4,208,384]{2,1,0:T(8,128)(2,1)S(1)}, bf16[4,208,384]{2,1,0:T(8,128)(2,1)S(1)}, u32[]{:S(2)}, u32[]{:S(2)}) %collective-permute-start.1) | collective-permute-done | bytes 639008 | tf_op jit(solution)/shard_map/ppermute | solution.py:809
  56.3 6.3 %collective-permute-done.4.refs_3_ = bf16[4,96,384]{2,1,0:T(8,128)(2,1)S(1)} collective-permute-done((bf16[4,96,384]{2,1,0:T(8,128)(2,1)S(1)}, bf16[4,96,384]{2,1,0:T(8,128)(2,1)S(1)}, u32[]{:S(2)}, u32[]{:S(2)}) %collective-permute-start.4) | collective-permute-done | bytes 294944 | tf_op jit(solution)/shard_map/ppermute | solution.py:809
  69.9 25.6 %cross_attn_forward.1 = (f32[1024,768]{1,0:T(8,128)}, bf16[8,128,768]{2,1,0:T(8,128)(2,1)}, bf16[8,304,768]{2,1,0:T(8,128)(2,1)}, bf16[8,304,768]{2,1,0:T(8,128)...) custom-call(s32[2]{0:T(128)} %pad_add_fusion.1.info, bf16[8,128,768]{2,1,0:T(8,128)(2,1)} %lat.1, ...), custom_call_target="tpu_custom_call" | custom-call | flops 1006632960 | bytes 3126067 | tf_op jit(solution)/shard_map/cross_attn_forward/pallas_call | solution.py:192
  99.2 12.4 %collective-permute-done.12.refs_3_ = bf16[4,192,384]{2,1,0:T(8,128)(2,1)} collective-permute-done((bf16[4,192,384]{2,1,0:T(8,128)(2,1)S(1)}, bf16[4,192,384]{2,1,0:T(8,128)(2,1)}, u32[]{:S(2)}, u32[]{:S(2)}) %collective-permute-start.12) | collective-permute-done | bytes 589856 | tf_op jit(solution)/shard_map/ppermute | solution.py:809
  117.4 22.3 %cross_mlp_forward.1 = (f32[1024,768]{1,0:T(8,128)}, bf16[1024,3072]{1,0:T(8,128)(2,1)}, bf16[1024,3072]{1,0:T(8,128)(2,1)}) custom-call(s32[2]{0:T(128)} %pad_add_fusion.1.info, f32[1024,768]{1,0:T(8,128)} %get-tuple-element.116.res, bf16[1024,768]{1,0:T(8,128)(2,1)} %bitcast.156, f32[1024,1]{1,0:T(8,128)} %copy.49.keep.keep_rows, f32[16,768]{1,0:T(8,128)} %reshape.289.vec, ...), custom_call_target="tpu_custom_call" | custom-call | flops 966367616 | bytes 2988441 | tf_op jit(solution)/shard_map/cross_mlp_forward/pallas_call | solution.py:192
  144.4 6.2 %collective-permute-done.21.refs_3_ = bf16[4,96,384]{2,1,0:T(8,128)(2,1)S(1)} collective-permute-done((bf16[4,96,384]{2,1,0:T(8,128)(2,1)S(1)}, bf16[4,96,384]{2,1,0:T(8,128)(2,1)S(1)}, u32[]{:S(2)}, u32[]{:S(2)}) %collective-permute-start.21) | collective-permute-done | bytes 294944 | tf_op jit(solution)/shard_map/ppermute | solution.py:809
  159.8 19.2 %self_attn_forward.1 = (f32[1024,768]{1,0:T(8,128)}, bf16[8,128,768]{2,1,0:T(8,128)(2,1)}, bf16[8,128,768]{2,1,0:T(8,128)(2,1)}, bf16[8,128,768]{2,1,0:T(8,128)(...) custom-call(s32[2]{0:T(128)} %pad_add_fusion.1.info, f32[1024,768]{1,0:T(8,128)} %get-tuple-element.120.mid, ...), custom_call_target="tpu_custom_call" | custom-call | flops 563714432 | bytes 2044723 | tf_op jit(solution)/shard_map/self_attn_forward/pallas_call | solution.py:192
  182.0 12.9 %collective-permute-done.31.refs_4_ = bf16[4,192,384]{2,1,0:T(8,128)(2,1)S(1)} collective-permute-done((bf16[4,192,384]{2,1,0:T(8,128)(2,1)S(1)}, bf16[4,192,384]{2,1,0:T(8,128)(2,1)S(1)}, u32[]{:S(2)}, u32[]{:S(2)}) %collective-permute-start.31) | collective-permute-done | bytes 589856 | tf_op jit(solution)/shard_map/ppermute | solution.py:812
  199.2 31.4 %self_mlp.1 = (bf16[1024,768]{1,0:T(8,128)(2,1)}, f32[1024,768]{1,0:T(8,128)}, bf16[1024,768]{1,0:T(8,128)(2,1)}, f32[8,768]{1,0:T(8,128)}, bf16[1024,768]{1,0:T...) custom-call(s32[2]{0:T(128)} %pad_add_fusion.1.info, f32[1024,768]{1,0:T(8,128)} %get-tuple-element.124.res, ...), custom_call_target="tpu_custom_call" | custom-call | flops 1932735232 | bytes 3460300 | tf_op jit(solution)/shard_map/self_mlp/pallas_call | solution.py:192
  230.6 17.8 %self_mlp_grads.1 = (bf16[4,4,384,384]{3,2,1,0:T(8,128)(2,1)}, bf16[4,4,384,384]{3,2,1,0:T(8,128)(2,1)}) custom-call(s32[2]{0:T(128)} %pad_add_fusion.1.info, bf16[1024,768]{1,0:T(8,128)(2,1)} %get-tuple-element.130.h, bf16[1024,3072]{1,0:T(8,128)(2,1)} %get-tuple-element.131.du, bf16[1024,3072]{1,0:T(8,128)(2,1)} %get-tuple-element.132.e, ...), custom_call_target="tpu_custom_call" | custom-call | flops 966367616 | bytes 2516582 | tf_op jit(solution)/shard_map/self_mlp_grads/pallas_call | solution.py:192
  248.6 21.0 %self_attn_back.1 = (f32[1024,768]{1,0:T(8,128)}, f32[8,768]{1,0:T(8,128)}, bf16[8,128,768]{2,1,0:T(8,128)(2,1)}, bf16[8,128,768]{2,1,0:T(8,128)(2,1)}, bf16[8,1...) custom-call(s32[2]{0:T(128)} %pad_add_fusion.1.info, f32[1024,768]{1,0:T(8,128)} %get-tuple-element.134.total, ...), custom_call_target="tpu_custom_call" | custom-call | flops 644245120 | bytes 2988441 | tf_op jit(solution)/shard_map/self_attn_back/pallas_call | solution.py:192
  273.7 21.7 %cross_mlp_back.1 = (f32[1024,768]{1,0:T(8,128)}, bf16[1024,768]{1,0:T(8,128)(2,1)}, f32[8,768]{1,0:T(8,128)}, bf16[1024,768]{1,0:T(8,128)(2,1)}, bf16[1024,3072]{1,0:T(8,128)(2,1)}, /*index=5*/bf16[1024,768]{1,0:T(8,128)(2,1)}) custom-call(s32[2]{0:T(128)} %pad_add_fusion.1.info, f32[1024,768]{1,0:T(8,128)} %get-tuple-element.144.up_grad, ...), custom_call_target="tpu_custom_call" | custom-call | flops 966367616 | bytes 3617587 | tf_op jit(solution)/shard_map/cross_mlp_back/pallas_call | solution.py:192
  300.0 17.6 %cross_mlp_grads.1 = (bf16[4,4,384,384]{3,2,1,0:T(8,128)(2,1)}, bf16[4,4,384,384]{3,2,1,0:T(8,128)(2,1)}) custom-call(s32[2]{0:T(128)} %pad_add_fusion.1.info, bf16[1024,768]{1,0:T(8,128)(2,1)} %get-tuple-element.150.h, bf16[1024,3072]{1,0:T(8,128)(2,1)} %get-tuple-element.151.du, bf16[1024,3072]{1,0:T(8,128)(2,1)} %get-tuple-element.152.e, ...), custom_call_target="tpu_custom_call" | custom-call | flops 966367616 | bytes 2516582 | tf_op jit(solution)/shard_map/cross_mlp_grads/pallas_call | solution.py:192
  317.7 10.0 %self_attn_grads.1 = (bf16[4,4,192,384]{3,2,1,0:T(8,128)(2,1)}, bf16[4,4,192,384]{3,2,1,0:T(8,128)(2,1)}) custom-call(s32[2]{0:T(128)} %pad_add_fusion.1.info, bf16[8,128,768]{2,1,0:T(8,128)(2,1)} %get-tuple-element.157.refs_0_, bf16[8,128,768]{2,1,0:T(8,128)(2,1)} %get-tuple-element.159.refs_1_, bf16[8,128,768]{2,1,0:T(8,128)(2,1)} %get-tuple-element.161.refs_2_, ...), custom_call_target="tpu_custom_call" | custom-call | flops 483183808 | bytes 1415577 | tf_op jit(solution)/shard_map/self_attn_grads/pallas_call | solution.py:192
  336.9 24.8 %collective-permute-done.42 = bf16[4,384,384]{2,1,0:T(8,128)(2,1)S(1)} collective-permute-done((bf16[4,384,384]{2,1,0:T(8,128)(2,1)S(1)}, bf16[4,384,384]{2,1,0:T(8,128)(2,1)S(1)}, u32[]{:S(2)}, u32[]{:S(2)}) %collective-permute-start.42) | collective-permute-done | bytes 1179680 | tf_op jit(solution)/shard_map/ppermute | solution.py:812
  365.8 22.8 %cross_attn_back_0.1 = (f32[8,768]{1,0:T(8,128)}, f32[1024,768]{1,0:T(8,128)}, f32[8,296,768]{2,1,0:T(8,128)}, bf16[8,128,768]{2,1,0:T(8,128)(2,1)}, bf16[8,128,...) custom-call(s32[2]{0:T(128)} %pad_add_fusion.1.info, ...), custom_call_target="tpu_custom_call" | custom-call | flops 598946624 | bytes 3126067 | tf_op jit(solution)/shard_map/cross_attn_back_0/pallas_call | solution.py:192
  397.8 22.0 %cross_attn_back_1.1 = (f32[8,768]{1,0:T(8,128)}, f32[1024,768]{1,0:T(8,128)}, f32[8,296,768]{2,1,0:T(8,128)}, bf16[8,128,768]{2,1,0:T(8,128)(2,1)}, bf16[8,128,...) custom-call(s32[2]{0:T(128)} %pad_add_fusion.1.info, ...), custom_call_target="tpu_custom_call", output_to_operand_aliasing={{1}: (21, {}), {2}: (22, {}), {3}: (23, {}), {4}: (24, {}),... | custom-call | flops 598946624 | bytes 3126067 | tf_op jit(solution)/shard_map/cross_attn_back_1/pallas_call | solution.py:192
  419.8 4.9 collective-permute-done.47
  432.9 14.7 %cross_attn_grads.1 = (bf16[4,4,208,384]{3,2,1,0:T(8,128)(2,1)}, bf16[4,4,208,384]{3,2,1,0:T(8,128)(2,1)}) custom-call(s32[2]{0:T(128)} %pad_add_fusion.1.info, bf16[8,128,768]{2,1,0:T(8,128)(2,1)} %get-tuple-element.199.refs_0_, bf16[8,128,768]{2,1,0:T(8,128)(2,1)} %get-tuple-element.200.refs_1_, bf16[8,304,768]{2,1,0:T(8,128)(2,1)} %get-tuple-element.201.refs_2_, ...), custom_call_target="tpu_custom_call" | custom-call | flops 815372672 | bytes 2221670 | tf_op jit(solution)/shard_map/cross_attn_grads/pallas_call | solution.py:192
  449.0 3.9 collective-permute-done.52
  477.9 8.2 %collective-permute-done.54 = bf16[4,208,384]{2,1,0:T(8,128)(2,1)} collective-permute-done((bf16[4,208,384]{2,1,0:T(8,128)(2,1)}, bf16[4,208,384]{2,1,0:T(8,128)(2,1)}, u32[]{:S(2)}, u32[]{:S(2)}) %collective-permute-start.54) | collective-permute-done | bytes 639008 | tf_op jit(solution)/shard_map/ppermute | solution.py:809
  486.0 12.9 %reduce-scatter.5.cloned.1.call-done = bf16[1,192,384]{2,1,0:T(8,128)(2,1)} async-done(((bf16[4,192,384]{2,1,0:T(8,128)(2,1)}), bf16[1,192,384]{2,1,0:T(8,128)(2,1)}) %reduce-scatter.5.cloned.1.call-update) | async-done | bytes 147472 | tf_op jit(solution)/shard_map/reduce_scatter | solution.py:852
  506.7 15.6 %reduce-scatter.7.cloned.1.call-done = bf16[1,208,384]{2,1,0:T(8,128)(2,1)} async-done(((bf16[4,208,384]{2,1,0:T(8,128)(2,1)}), bf16[1,208,384]{2,1,0:T(8,128)(2,1)}) %reduce-scatter.7.cloned.1.call-update) | async-done | bytes 159760 | tf_op jit(solution)/shard_map/reduce_scatter | solution.py:852
  (311 shorter events, 132.4 us)
Async XLA Ops:
  7.2 55.3 %all-gather.6.cloned.1.call-start = ((), (), s32[]{:S(2)}) async-start(), calls=%async_computation.8 | async-start | bytes 1474560 | tf_op jit(solution)/shard_map/all_gather | solution.py:821
  14.7 98.7 %all-gather.8.cloned.1.call-start = ((), (), s32[]{:S(2)}) async-start(), calls=%async_computation.9 | async-start | bytes 2211840 | tf_op jit(solution)/shard_map/all_gather | solution.py:821
  54.5 393.3 %reduce-scatter.11.cloned.1.call-start = ((), (), s32[]{:S(2)}) async-start(), calls=%async_computation.7 | async-start | bytes 1474560 | tf_op jit(solution)/shard_map/reduce_scatter | solution.py:852
  63.2 32.8 %collective-permute-start.11 = (bf16[4,384,384]{2,1,0:T(8,128)(2,1)}, bf16[4,384,384]{2,1,0:T(8,128)(2,1)S(1)}, u32[]{:S(2)}, u32[]{:S(2)}) collective-permute-start(bf16[4,384,384]{2,1,0:T(8,128)(2,1)} %bitcast.25.refs_0_), channel_id=1, source_target_pairs={{0,4},{1,5},{2,6},{3,7},{4,0},{5,1},{6,2},{7,3},{8,12},{9,13},{10,... | collective-permute-start | bytes 3538952 | tf_op jit(solution)/shard_map/ppermute | solution.py:812
  65.6 31.4 %collective-permute-start.10 = (bf16[4,384,384]{2,1,0:T(8,128)(2,1)}, bf16[4,384,384]{2,1,0:T(8,128)(2,1)}, u32[]{:S(2)}, u32[]{:S(2)}) collective-permute-start(bf16[4,384,384]{2,1,0:T(8,128)(2,1)} %bitcast.25.refs_0_), channel_id=1, source_target_pairs={{0,2},{1,3},{2,0},{3,1},{4,6},{5,7},{6,4},{7,5},{8,10},{9,11},{10,... | collective-permute-start | bytes 3538952 | tf_op jit(solution)/shard_map/ppermute | solution.py:809
  114.6 25.1 %collective-permute-start.20 = (bf16[4,192,384]{2,1,0:T(8,128)(2,1)S(1)}, bf16[4,192,384]{2,1,0:T(8,128)(2,1)}, u32[]{:S(2)}, u32[]{:S(2)}) collective-permute-start(bf16[4,192,384]{2,1,0:T(8,128)(2,1)S(1)} %slice.463.refs_0_), channel_id=1, source_target_pairs={{0,4},{1,5},{2,6},{3,7},{4,0},{5,1},{6,2},{7,3},{8,12},{9,13},{10,... | collective-permute-start | bytes 1769480 | tf_op jit(solution)/shard_map/ppermute | solution.py:812
  115.1 24.6 %collective-permute-start.19 = (bf16[4,192,384]{2,1,0:T(8,128)(2,1)S(1)}, bf16[4,192,384]{2,1,0:T(8,128)(2,1)}, u32[]{:S(2)}, u32[]{:S(2)}) collective-permute-start(bf16[4,192,384]{2,1,0:T(8,128)(2,1)S(1)} %slice.463.refs_0_), channel_id=1, source_target_pairs={{0,2},{1,3},{2,0},{3,1},{4,6},{5,7},{6,4},{7,5},{8,10},{9,11},{10,... | collective-permute-start | bytes 1769480 | tf_op jit(solution)/shard_map/ppermute | solution.py:809
  151.2 27.8 %collective-permute-start.28 = (bf16[4,384,384]{2,1,0:T(8,128)(2,1)S(1)}, bf16[4,384,384]{2,1,0:T(8,128)(2,1)S(1)}, u32[]{:S(2)}, u32[]{:S(2)}) collective-permute-start(bf16[4,384,384]{2,1,0:T(8,128)(2,1)S(1)} %slice.464.refs_0_), channel_id=1, source_target_pairs={{0,2},{1,3},{2,0},{3,1},{4,6},{5,7},{6,4},{7,5},{8,10},{9,11},{10,... | collective-permute-start | bytes 3538952 | tf_op jit(solution)/shard_map/ppermute | solution.py:809
  152.4 26.7 %collective-permute-start.29 = (bf16[4,384,384]{2,1,0:T(8,128)(2,1)S(1)}, bf16[4,384,384]{2,1,0:T(8,128)(2,1)S(1)}, u32[]{:S(2)}, u32[]{:S(2)}) collective-permute-start(bf16[4,384,384]{2,1,0:T(8,128)(2,1)S(1)} %slice.464.refs_0_), channel_id=1, source_target_pairs={{0,4},{1,5},{2,6},{3,7},{4,0},{5,1},{6,2},{7,3},{8,12},{9,13},{10,... | collective-permute-start | bytes 3538952 | tf_op jit(solution)/shard_map/ppermute | solution.py:812
  158.0 38.3 %collective-permute-start.32 = (bf16[4,384,384]{2,1,0:T(8,128)(2,1)S(1)}, bf16[4,384,384]{2,1,0:T(8,128)(2,1)}, u32[]{:S(2)}, u32[]{:S(2)}) collective-permute-start(bf16[4,384,384]{2,1,0:T(8,128)(2,1)S(1)} %slice.464.refs_0_), channel_id=1, source_target_pairs={{0,1},{1,0},{2,3},{3,2},{4,5},{5,4},{6,7},{7,6},{8,9},{9,8},{10,11... | collective-permute-start | bytes 3538952 | tf_op jit(solution)/shard_map/ppermute | solution.py:806
  332.3 62.1 %collective-permute-start.45 = (bf16[4,4,192,384]{3,2,1,0:T(8,128)(2,1)}, bf16[4,4,192,384]{3,2,1,0:T(8,128)(2,1)}, u32[]{:S(2)}, u32[]{:S(2)}) collective-permute-start(bf16[4,4,192,384]{3,2,1,0:T(8,128)(2,1)} %get-tuple-element.181), channel_id=1, source_target_pairs={{0,1},{1,0},{2,3},{3,2},{4,5},{5,4},{6,7},{7,6},{8,9},{9,8},{10,11... | collective-permute-start | bytes 7077896 | tf_op jit(solution)/shard_map/ppermute | solution.py:806
  332.8 28.8 %collective-permute-start.42 = (bf16[4,384,384]{2,1,0:T(8,128)(2,1)S(1)}, bf16[4,384,384]{2,1,0:T(8,128)(2,1)S(1)}, u32[]{:S(2)}, u32[]{:S(2)}) collective-permute-start(bf16[4,384,384]{2,1,0:T(8,128)(2,1)S(1)} %copy-done.21), channel_id=1, source_target_pairs={{0,4},{1,5},{2,6},{3,7},{4,0},{5,1},{6,2},{7,3},{8,12},{9,13},{10,... | collective-permute-start | bytes 3538952 | tf_op jit(solution)/shard_map/ppermute | solution.py:812
  333.9 28.9 %collective-permute-start.41 = (bf16[4,384,384]{2,1,0:T(8,128)(2,1)S(1)}, bf16[4,384,384]{2,1,0:T(8,128)(2,1)S(1)}, u32[]{:S(2)}, u32[]{:S(2)}) collective-permute-start(bf16[4,384,384]{2,1,0:T(8,128)(2,1)S(1)} %get-tuple-element.222), channel_id=1, source_target_pairs={{0,2},{1,3},{2,0},{3,1},{4,6},{5,7},{6,4},{7,5},{8,10},{9,11},{10,... | collective-permute-start | bytes 3538952 | tf_op jit(solution)/shard_map/ppermute | solution.py:809
  335.1 53.5 %collective-permute-start.44 = (bf16[4,192,384]{2,1,0:T(8,128)(2,1)}, bf16[4,192,384]{2,1,0:T(8,128)(2,1)}, u32[]{:S(2)}, u32[]{:S(2)}) collective-permute-start(bf16[4,192,384]{2,1,0:T(8,128)(2,1)} %get-tuple-element.220), channel_id=1, source_target_pairs={{0,2},{1,3},{2,0},{3,1},{4,6},{5,7},{6,4},{7,5},{8,10},{9,11},{10,... | collective-permute-start | bytes 1769480 | tf_op jit(solution)/shard_map/ppermute | solution.py:809
  335.9 52.6 %collective-permute-start.43 = (bf16[4,192,384]{2,1,0:T(8,128)(2,1)}, bf16[4,192,384]{2,1,0:T(8,128)(2,1)}, u32[]{:S(2)}, u32[]{:S(2)}) collective-permute-start(bf16[4,192,384]{2,1,0:T(8,128)(2,1)} %get-tuple-element.219), channel_id=1, source_target_pairs={{0,4},{1,5},{2,6},{3,7},{4,0},{5,1},{6,2},{7,3},{8,12},{9,13},{10,... | collective-permute-start | bytes 1769480 | tf_op jit(solution)/shard_map/ppermute | solution.py:812
  392.3 37.3 %collective-permute-start.49 = (bf16[4,384,384]{2,1,0:T(8,128)(2,1)}, bf16[4,384,384]{2,1,0:T(8,128)(2,1)S(1)}, u32[]{:S(2)}, u32[]{:S(2)}) collective-permute-start(bf16[4,384,384]{2,1,0:T(8,128)(2,1)} %get-tuple-element.217), channel_id=1, source_target_pairs={{0,4},{1,5},{2,6},{3,7},{4,0},{5,1},{6,2},{7,3},{8,12},{9,13},{10,... | collective-permute-start | bytes 3538952 | tf_op jit(solution)/shard_map/ppermute | solution.py:812
  393.2 36.4 %collective-permute-start.48 = (bf16[4,384,384]{2,1,0:T(8,128)(2,1)S(1)}, bf16[4,384,384]{2,1,0:T(8,128)(2,1)}, u32[]{:S(2)}, u32[]{:S(2)}) collective-permute-start(bf16[4,384,384]{2,1,0:T(8,128)(2,1)S(1)} %get-tuple-element.218), channel_id=1, source_target_pairs={{0,2},{1,3},{2,0},{3,1},{4,6},{5,7},{6,4},{7,5},{8,10},{9,11},{10,... | collective-permute-start | bytes 3538952 | tf_op jit(solution)/shard_map/ppermute | solution.py:809
  394.4 81.7 %reduce-scatter.9.cloned.1.call-start = ((), (), s32[]{:S(2)}) async-start(), calls=%async_computation.6 | async-start | bytes 1474560 | tf_op jit(solution)/shard_map/reduce_scatter | solution.py:852
  395.8 29.0 %collective-permute-start.47 = (bf16[4,96,384]{2,1,0:T(8,128)(2,1)S(1)}, bf16[4,96,384]{2,1,0:T(8,128)(2,1)S(1)}, u32[]{:S(2)}, u32[]{:S(2)}) collective-permute-start(bf16[4,96,384]{2,1,0:T(8,128)(2,1)S(1)} %get-tuple-element.230), channel_id=1, source_target_pairs={{0,2},{1,3},{2,0},{3,1},{4,6},{5,7},{6,4},{7,5},{8,10},{9,11},{10,... | collective-permute-start | bytes 884744 | tf_op jit(solution)/shard_map/ppermute | solution.py:809
  396.7 28.1 %collective-permute-start.46 = (bf16[4,96,384]{2,1,0:T(8,128)(2,1)S(1)}, bf16[4,96,384]{2,1,0:T(8,128)(2,1)S(1)}, u32[]{:S(2)}, u32[]{:S(2)}) collective-permute-start(bf16[4,96,384]{2,1,0:T(8,128)(2,1)S(1)} %get-tuple-element.229), channel_id=1, source_target_pairs={{0,4},{1,5},{2,6},{3,7},{4,0},{5,1},{6,2},{7,3},{8,12},{9,13},{10,... | collective-permute-start | bytes 884744 | tf_op jit(solution)/shard_map/ppermute | solution.py:812
  447.8 51.2 %reduce-scatter.5.cloned.1.call-start = ((), (), s32[]{:S(2)}) async-start(), calls=%async_computation.4 | async-start | bytes 737280 | tf_op jit(solution)/shard_map/reduce_scatter | solution.py:852
  460.9 61.5 %reduce-scatter.7.cloned.1.call-start = ((), (), s32[]{:S(2)}) async-start(), calls=%async_computation.5 | async-start | bytes 798720 | tf_op jit(solution)/shard_map/reduce_scatter | solution.py:852
  471.6 27.4 %collective-permute-start.56 = (bf16[4,208,384]{2,1,0:T(8,128)(2,1)}, bf16[4,208,384]{2,1,0:T(8,128)(2,1)}, u32[]{:S(2)}, u32[]{:S(2)}) collective-permute-start(bf16[4,208,384]{2,1,0:T(8,128)(2,1)} %get-tuple-element.226), channel_id=1, source_target_pairs={{0,4},{1,5},{2,6},{3,7},{4,0},{5,1},{6,2},{7,3},{8,12},{9,13},{10,... | collective-permute-start | bytes 1916936 | tf_op jit(solution)/shard_map/ppermute | solution.py:812
  473.3 29.3 %collective-permute-start.60 = (f32[192,384]{1,0:T(8,128)}, f32[192,384]{1,0:T(8,128)}, u32[]{:S(2)}, u32[]{:S(2)}) collective-permute-start(f32[192,384]{1,0:T(8,128)} %fusion.14), channel_id=1, source_target_pairs={{0,1},{1,0},{2,3},{3,2},{4,5},{5,4},{6,7},{7,6},{8,9},{9,8},{10,11... | collective-permute-start | bytes 884744 | tf_op jit(solution)/shard_map/ppermute | solution.py:806
  (87 other events, 903.9 us)
Sparse Core Ops, SparseCore 0:
  14.8 37.0 all-gather.5
  54.7 40.0 all-gather.7
  394.5 28.1 reduce-scatter.10
  447.9 28.1 reduce-scatter.8
  478.3 20.6 reduce-scatter.4
  501.6 20.7 reduce-scatter.6

commit v3 on v2

--- a/solution.py
+++ b/solution.py
@@ -18,6 +18,8 @@
 VIDEO = 256
 ITEMS = 2
 ROWS = ITEMS * LAT
+TALL = 256
+CHUNK = 768
 AX = ("dp", "fsdp")
 F32 = jnp.float32
 BF16 = jnp.bfloat16
@@ -28,7 +30,6 @@
 SMALL = pl.BlockSpec(memory_space=pltpu.SMEM)
 VMEM_BYTES = 58 * 2**20
 EXTRA = 16
-SHARE = 0.1
 ATTN_SPLIT = 96
 MLP_SPLIT = 192
 
@@ -200,7 +201,7 @@
         input_output_aliases=aliases or {},
         compiler_params=pltpu.CompilerParams(vmem_limit_bytes=VMEM_BYTES),
         cost_estimate=pl.CostEstimate(
-            flops=int(flops * SHARE), bytes_accessed=int(moved * SHARE), transcendentals=0
+            flops=flops, bytes_accessed=moved, transcendentals=0
         ),
     )(*args)
 
@@ -209,8 +210,18 @@
     return pl.BlockSpec((ITEMS,) + shape, lambda i: (i,) + (0,) * len(shape))
 
 
-def rows_spec(width):
-    return pl.BlockSpec((ROWS, width), lambda i: (i, 0))
+def rows_spec(rows, width):
+    return pl.BlockSpec((rows, width), lambda i: (i, 0))
+
+
+def up_part(w_up, j):
+    return w_up[:, :, :, CHUNK * j : CHUNK * j + CHUNK].reshape(D, CHUNK)
+
+
+def down_part(w_down, j):
+    begin = CHUNK * j
+    rows = begin % D
+    return w_down[begin // D].reshape(D, D)[rows : rows + CHUNK]
 
 
 def whole_spec(*shape):
@@ -301,7 +312,7 @@
     k[...] = dot(zl, matrix(wk)).astype(BF16).reshape(ITEMS, LAT, D)
     v[...] = dot(zl, matrix(wv)).astype(BF16).reshape(ITEMS, LAT, D)
     for i in range(ITEMS):
-        attend(i, q, k, v, None, o, p, 2)
+        attend(i, q, k, v, None, o, p, 6)
     r[...] = z + dot(o[...].reshape(ROWS, D), matrix(wo))
 
 
@@ -344,21 +355,25 @@
     def _():
         wait_all(groups)
 
-    y = jnp.zeros((ROWS, D), F32)
-    for j in range(4):
-        lanes = slice(D * j, D * j + D)
-        value, grad = gelu_both(dot(h, w_up[:, :, :, lanes].reshape(D, D)))
+    y = jnp.zeros((TALL, D), F32)
+    parts = FF // CHUNK
+    u = dot(h, up_part(w_up, 0))
+    for j in range(parts):
+        lanes = slice(CHUNK * j, CHUNK * j + CHUNK)
+        following = dot(h, up_part(w_up, j + 1)) if j + 1 < parts else None
+        value, grad = gelu_both(u)
         value = value.astype(BF16)
         e[:, lanes] = value
         slope[:, lanes] = grad.astype(BF16)
-        y += dot(value, w_down[j].reshape(D, D))
+        y += dot(value, down_part(w_down, j))
+        u = following
     mid[...] = z + keep[...] * ((r - z) + y)
 
 
 def cross_mlp_forward(info, res, lat, keep, vec, pieces):
     m = res.shape[0]
-    steps = m // ROWS
-    spec = rows_spec
+    steps = m // TALL
+    spec = functools.partial(rows_spec, TALL)
     return call(
         cross_mlp_kernel,
         "cross_mlp_forward",
@@ -457,19 +472,23 @@
     def _():
         wait_all(groups)
 
-    y = jnp.zeros((ROWS, D), F32)
-    dh = jnp.zeros((ROWS, D), F32)
-    for j in range(4):
-        lanes = slice(D * j, D * j + D)
-        up = w_up[:, :, :, lanes].reshape(D, D)
-        down = w_down[j].reshape(D, D)
-        value, slope = gelu_both(dot(h, up))
+    y = jnp.zeros((TALL, D), F32)
+    dh = jnp.zeros((TALL, D), F32)
+    parts = FF // CHUNK
+    u, d_act = (dot(h, up_part(w_up, 0)), dot(dy, down_part(w_down, 0), NT))
+    for j in range(parts):
+        lanes = slice(CHUNK * j, CHUNK * j + CHUNK)
+        following = (None, None)
+        if j + 1 < parts:
+            following = (dot(h, up_part(w_up, j + 1)), dot(dy, down_part(w_down, j + 1), NT))
+        value, slope = gelu_both(u)
         value = value.astype(BF16)
         e_all[:, lanes] = value
-        y += dot(value, down)
-        du = (dot(dy, down, NT) * slope).astype(BF16)
+        du = (d_act * slope).astype(BF16)
         du_all[:, lanes] = du
-        dh += dot(du, up, NT)
+        y += dot(value, down_part(w_down, j))
+        dh += dot(du, up_part(w_up, j), NT)
+        u, d_act = following
     out[...] = (r + y).astype(BF16)
     dr, d_gain, d_shift = norm_back(hat, scale, gain, dh)
     t = dy.astype(F32) + dr
@@ -481,8 +500,8 @@
 
 def self_mlp(info, res, cot, vec, pieces):
     m = res.shape[0]
-    steps = m // ROWS
-    spec = rows_spec
+    steps = m // TALL
+    spec = functools.partial(rows_spec, TALL)
     return call(
         self_mlp_kernel,
         "self_mlp",
@@ -528,13 +547,16 @@
     def _():
         wait_all(groups)
 
-    dh = jnp.zeros((ROWS, D), F32)
-    for j in range(4):
-        lanes = slice(D * j, D * j + D)
-        d_act = dot(dy, w_down[j].reshape(D, D), NT)
+    dh = jnp.zeros((TALL, D), F32)
+    parts = FF // CHUNK
+    d_act = dot(dy, down_part(w_down, 0), NT)
+    for j in range(parts):
+        lanes = slice(CHUNK * j, CHUNK * j + CHUNK)
+        following = dot(dy, down_part(w_down, j + 1), NT) if j + 1 < parts else None
         du = (d_act * slope[:, lanes].astype(F32)).astype(BF16)
         du_all[:, lanes] = du
-        dh += dot(du, w_up[:, :, :, lanes].reshape(D, D), NT)
+        dh += dot(du, up_part(w_up, j), NT)
+        d_act = following
     dr, d_gain, d_shift = norm_back(hat, scale, gain, dh)
     total[...] = g + dr
     da[...] = (direct + dr).astype(BF16)
@@ -544,8 +566,8 @@
 
 def cross_mlp_back(info, up_grad, keep_rows, res, slope, vec, pieces):
     m = res.shape[0]
-    steps = m // ROWS
-    spec = rows_spec
+    steps = m // TALL
+    spec = functools.partial(rows_spec, TALL)
     return call(
         cross_mlp_back_kernel,
         "cross_mlp_back",
@@ -676,7 +698,7 @@
 
     do_rows[...] = dot(da[...], matrix(wo), NT).astype(BF16).reshape(ITEMS, LAT, D)
     for i in range(ITEMS):
-        attend_back(i, q, k, v, p, do_rows, dq, dk, dv, 3)
+        attend_back(i, q, k, v, p, do_rows, dq, dk, dv, 6)
     dz = dot(dq[...].reshape(ROWS, D), matrix(wq), NT)
     dz += dot(dk[...].reshape(ROWS, D), matrix(wk), NT)
     dz += dot(dv[...].reshape(ROWS, D), matrix(wv), NT)
@@ -690,7 +712,7 @@
     m = total.shape[0]
     n = m // LAT
     steps = m // ROWS
-    spec = rows_spec
+    spec = functools.partial(rows_spec, ROWS)
     return call(
         self_attn_back_kernel,
         "self_attn_back",
@@ -732,7 +754,7 @@
 
     do_rows[...] = dot(da[...], matrix(wo), NT).astype(BF16).reshape(ITEMS, LAT, D)
     for i in range(ITEMS):
-        attend_back(i, q, k, v, p, do_rows, dq, dk, dv, 3)
+        attend_back(i, q, k, v, p, do_rows, dq, dk, dv, 6)
         x = jnp.concatenate([inp[i].astype(F32), jnp.zeros((PAD - TOK, D), F32)], axis=0)
         x_hat, x_scale = norm_parts(x)
         x_gain = vec[1:2]
@@ -800,6 +822,8 @@
         self.to_core = [(2 * i + c, 2 * i + 1 - c) for i in chips for c in range(2)]
         self.to_x = [(2 * i + c, 2 * (i ^ 1) + c) for i in chips for c in range(2)]
         self.to_y = [(2 * i + c, 2 * (i ^ 2) + c) for i in chips for c in range(2)]
+        self.to_z = [(2 * i + c, 2 * (i ^ 4) + c) for i in chips for c in range(2)]
+        self.to_far_z = [(2 * i + c, 2 * (i ^ 8) + c) for i in chips for c in range(2)]
         self.columns = [[4 * z + i for z in range(4)] for i in range(4)]
 
     def swap_core(self, value):
@@ -837,19 +861,43 @@
     def send_diagonal(self, sums):
         return (self.swap_x(sums[0]), self.swap_y(sums[1]))
 
-    def sides(self, keep, arrived, first, second):
+    def sides(self, keep, arrived, first, second, parts=1):
         for_x = jnp.concatenate([jnp.zeros_like(first), second], axis=1)
         for_y = jnp.concatenate([first, jnp.zeros_like(second)], axis=1)
-        return (keep[1] + arrived[1] + for_x, keep[2] + arrived[2] + for_y)
+        sums = (keep[1] + arrived[1] + for_x, keep[2] + arrived[2] + for_y)
+        rows = 4 // parts
+        return [tuple((s[rows * i : rows * i + rows] for s in sums)) for i in range(parts)]
 
     def send_sides(self, sums):
         return (self.swap_x(sums[0]), self.swap_y(sums[1]))
 
-    def own_column(self, keep, arrived, sides):
-        return keep[0] + arrived[0] + sides[0] + sides[1]
+    def own_column(self, keep, arrived, *near):
+        from_x = jnp.concatenate([part[0] for part in near])
+        from_y = jnp.concatenate([part[1] for part in near])
+        return keep[0] + arrived[0] + from_x + from_y
 
     def scatter_z(self, own):
         return lax.psum_scatter(own, "dp", scatter_dimension=0, axis_index_groups=self.columns)
+
+    def z_bits(self):
+        z = lax.div(lax.axis_index("dp"), 4)
+        return (lax.rem(z, 2) == 1, z >= 2)
+
+    def scatter_z_by_hops(self, own):
+        odd, high = self.z_bits()
+        even_blocks, odd_blocks = (own[0::2], own[1::2])
+        keep, send = (jnp.where(odd, a, b) for a, b in ((odd_blocks, even_blocks), (even_blocks, odd_blocks)))
+        total = keep + lax.ppermute(send, AX, self.to_z)
+        keep, send = (jnp.where(high, total[i], total[1 - i]) for i in (1, 0))
+        return keep.astype(F32) + lax.ppermute(send, AX, self.to_far_z).astype(F32)
+
+    def gather_z_by_hops(self, unit):
+        odd, high = self.z_bits()
+        arrived = lax.ppermute(unit, AX, self.to_far_z)
+        pair = jnp.stack([jnp.where(high, arrived, unit), jnp.where(high, unit, arrived)])
+        arrived = lax.ppermute(pair, AX, self.to_z)
+        both = [jnp.where(odd, arrived, pair), jnp.where(odd, pair, arrived)]
+        return jnp.stack(both, axis=1).reshape((4,) + unit.shape)
 
     def to_rows(self, parts):
         parts = [part.astype(F32).reshape(part.shape[0], 2, -1, HALF) for part in parts]
@@ -892,7 +940,12 @@
     vectors = jnp.pad(vectors, ((0, 0), (0, HALF - 48)))
     cross_attn = jnp.concatenate([cross_attn, vectors], axis=0)
     own = grid.gather_z(jnp.concatenate([self_attn, self_mlp], axis=0))
-    return (grid.gather_z(cross_attn), grid.gather_z(cross_mlp), own[:, :192], own[:, 192:])
+    return (
+        grid.gather_z_by_hops(cross_attn),
+        grid.gather_z(cross_mlp),
+        own[:, :192],
+        own[:, 192:],
+    )
 
 
 def gathered_vectors(grid, pieces):
@@ -996,6 +1049,7 @@
     sm = grid.both_cores(sm_own, sm_near, sm_far)
     result, total, da, own_vec, h, du, own_e = self_mlp(info, own_res, cot_rows, vec, sm)
     a_keep, a_send = mlp_grads("self_mlp_grads", info, h, du, own_e, cot_rows)
+
     total, da = after((total, da), a_send)
     a_in = grid.swap_core(a_send)
     d_mid, self_vec, zl, dq, dk, dv = self_attn_back(info, total, da, sq, sk, sv, sp, mid, vec, sa)
@@ -1007,18 +1061,21 @@
     a_far = grid.send_diagonal(a_diag)
     total, da, mlp_vec, h, du, dy = cross_mlp_back(info, d_mid, keeping, res, slope, vec, cm)
 
-    a_sides = grid.sides(a_keep, a_in, *after(a_far, total))
+    a_sides = grid.sides(a_keep, a_in, *after(a_far, total), 2)
     h = after(h, a_sides)
-    a_near = grid.send_sides(a_sides)
+    a_near = grid.send_sides(a_sides[0])
     c_keep, c_send = mlp_grads("cross_mlp_grads", info, h, du, e, dy)
-    self_arrays = after(self_arrays, c_send)
-    c_in = grid.swap_core(c_send)
+
+    a_near = after(a_near, c_send)
+    a_near = (a_near, grid.send_sides(after(a_sides[1], a_near)))
+    self_arrays = after(self_arrays, c_send, a_near[0])
+    c_in = grid.swap_core(after(c_send, a_near[0]))
     pairs = ((0, 1), (0, 2), (0, 3), (4, 5))
     b_keep, b_send = attn_grads("self_attn_grads", info, self_arrays, pairs)
 
     c_in = after(c_in, b_send)
     c_diag = grid.diagonal(c_keep, c_in, MLP_SPLIT)
-    a_sum = grid.own_column(a_keep, a_in, after(a_near, b_send))
+    a_sum = grid.own_column(a_keep, a_in, *after(a_near, b_send))
     total = after(total, c_diag, a_sum)
     a_sum = grid.scatter_z(a_sum)
     c_far = grid.send_diagonal(c_diag)
@@ -1027,33 +1084,32 @@
     half = cross_attn_back(0, 2, None, info, total, *back)
 
     b_in, c_far = after((b_in, c_far), half[0])
-    c_sides = grid.sides(c_keep, c_in, *c_far)
-    c_near = grid.send_sides(c_sides)
+    c_sides = grid.sides(c_keep, c_in, *c_far, 2)
+    c_near = grid.send_sides(c_sides[0])
     b_diag = grid.diagonal(b_keep, b_in, ATTN_SPLIT)
     b_far = grid.send_diagonal(b_diag)
     total = after(total, c_sides, b_diag)
     cross_vec, d_lat, d_inp, zl, dq, xl, dk, dv = cross_attn_back(1, 2, half, info, total, *back)
 
     b_far, c_near = after((b_far, c_near), cross_vec)
-    b_sides = grid.sides(b_keep, b_in, *b_far)
-    c_sum = grid.own_column(c_keep, c_in, c_near)
-    zl = after(zl, b_sides, c_sum)
+    c_near = (c_near, grid.send_sides(after(c_sides[1], c_near)))
+    b_sides = grid.sides(b_keep, b_in, *b_far)[0]
+    zl = after(zl, b_sides, c_near[0])
     b_near = grid.send_sides(b_sides)
-    c_sum = grid.scatter_z(c_sum)
     pairs = ((0, 1), (2, 3), (2, 4), (5, 6))
     arrays = (zl, dq, xl, dk, dv, o, da.reshape(o.shape))
     vectors = (cross_vec, mlp_vec, self_vec, own_vec)
     d_keep, d_send = attn_grads("cross_attn_grads", info, arrays, pairs, vectors)
 
-    d_send = after(d_send, b_near, a_sum)
-    d_in = grid.swap_core(d_send)
+    c_near = after(c_near, d_send)
+    d_in = grid.swap_core(after(d_send, c_near))
     d_diag = grid.diagonal(d_keep, d_in, ATTN_SPLIT)
+    c_sum = grid.scatter_z(grid.own_column(c_keep, c_in, *c_near))
     d_far = grid.send_diagonal(d_diag)
-    b_sum = grid.scatter_z(grid.own_column(b_keep, b_in, after(b_near, d_diag)))
-    d_far = after(d_far, b_near)
-    d_near = grid.send_sides(grid.sides(d_keep, d_in, *d_far))
-    d_near = after(d_near, b_sum)
-    d_sum = grid.scatter_z(grid.own_column(d_keep, d_in, d_near))
+    d_near = grid.send_sides(grid.sides(d_keep, d_in, *d_far)[0])
+    c_sum = after(c_sum, d_near)
+    b_sum = grid.scatter_z(grid.own_column(b_keep, b_in, after(b_near, d_near)))
+    d_sum = grid.scatter_z_by_hops(grid.own_column(d_keep, d_in, d_near))
 
     s_up, s_down = finish_mlp(grid, a_sum)
     s_qkv, s_out, _ = finish_attn(grid, b_sum)

time: 539 us -> 503 us (0.933)
  blocking collectives: 24 us -> 0 us
  waiting for transfers between devices: 141 us -> 120 us
  starting transfers between devices: 39.9 us -> 54.3 us
  Pallas kernels: 246 us -> 239 us
    reduce_scatter x4 -> x3, waiting for transfers between devices: 31.4 us -> 0.53 us  [scatter_z(): lax.psum_scatter(own, 'dp', scatter_dimension=0, axis_index_groups=self.c...]
    ppermute x0 -> x4, waiting for transfers between devices: none -> 30.8 us  [the longest x1 12.2 us: scatter_z_by_hops(): return keep.astype(F32) + lax.ppermute(send, AX, self.to_far_z).astype(F32)]
    all_gather x1 -> x0, blocking collectives: 24 us -> none  [gather_z(): return lax.all_gather(unit, 'dp', axis=0, axis_index_groups=self.columns)]
    ppermute x0 -> x4, starting transfers between devices: none -> 11.1 us  [the longest x1 4.27 us: scatter_z_by_hops(): return keep.astype(F32) + lax.ppermute(send, AX, self.to_far_z).astype(F32)]
    ppermute x16 -> x18, waiting for transfers between devices: 53 us -> 44 us  [swap_x(): return lax.ppermute(value, AX, self.to_x)]
    pallas_call x12, Pallas kernels: 246 us -> 239 us  [call(): pl.pallas_call(kernel, grid=(grid,), in_specs=in_specs, out_specs=out_spe...]
    ppermute x16 -> x18, waiting for transfers between devices: 44.7 us -> 38.5 us  [swap_y(): return lax.ppermute(value, AX, self.to_y)]
    ppermute x29, waiting for transfers between devices: 12.2 us -> 6.12 us  [swap_core(): return lax.ppermute(value, AX, self.to_core)]
  transfers between devices with their start and end apart: 67 -> 74, of which waited for: 29 -> 27; matrix products, arithmetic and copies ran while one was open for 8% -> 9% of each run, Pallas kernels for 33% -> 38%
where the time goes in v3:
time: 503 us; the launch traced here: 499 us
  Pallas kernels  239 us (48%)
  waiting for transfers between devices  120 us (24%)
  starting transfers between devices  54.3 us (11%)
  other arithmetic  42.8 us (9%)
  local copies, waits for them, and re-layouts  27.7 us (6%)
  between operations  15.2 us (3%)
    pallas_call x12, Pallas kernels, call(): pl.pallas_call(kernel, grid=(grid,), in_specs=in_specs, out_specs=out_spe...  239 us
    ppermute x18, waiting for transfers between devices, swap_x(): return lax.ppermute(value, AX, self.to_x)  44 us
    ppermute x18, waiting for transfers between devices, swap_y(): return lax.ppermute(value, AX, self.to_y)  38.5 us
    ppermute x18, starting transfers between devices, swap_y(): return lax.ppermute(value, AX, self.to_y)  19.8 us
    ppermute x18, starting transfers between devices, swap_x(): return lax.ppermute(value, AX, self.to_x)  18.5 us
    ppermute x1, waiting for transfers between devices, scatter_z_by_hops(): return keep.astype(F32) + lax.ppermute(send, AX, self.to_far_z).astype(F32)  12.2 us
    add x4, other arithmetic, sides(): sums = (keep[1] + arrived[1] + for_x, keep[2] + arrived[2] + for_y)  11 us
    add x4, other arithmetic, own_column(): return keep[0] + arrived[0] + from_x + from_y  10.5 us
  transfers between devices with their start and end apart: 74, of which 27 were waited for; matrix products, arithmetic and copies ran while one was open for 9% of the time, Pallas kernels for 38%

profile of v3, /device:TPU:0, one launch (start us, length us, event | category | flops | bytes accessed | tf_op | source)
XLA Modules:
  0.0 498.8 jit_solution(14081035275843316328)
XLA Ops:
  18.7 7.1 %collective-permute-done.1 = bf16[208,384]{1,0:T(8,128)(2,1)S(1)} collective-permute-done((bf16[208,384]{1,0:T(8,128)(2,1)S(1)}, bf16[208,384]{1,0:T(8,128)(2,1)S(1)}, u32[]{:S(2)}, u32[]{:S(2)}) %collective-permute-start.1) | collective-permute-done | bytes 159776 | tf_op jit(solution)/shard_map/ppermute | solution.py:896
  27.6 7.5 %collective-permute-done.2 = bf16[2,208,384]{2,1,0:T(8,128)(2,1)S(1)} collective-permute-done((bf16[2,208,384]{2,1,0:T(8,128)(2,1)S(1)}, bf16[2,208,384]{2,1,0:T(8,128)(2,1)S(1)}, u32[]{:S(2)}, u32[]{:S(2)}) %collective-permute-start.2) | collective-permute-done | bytes 319520 | tf_op jit(solution)/shard_map/ppermute | solution.py:898
  38.4 12.1 %collective-permute-done.5.refs_2_ = bf16[4,208,384]{2,1,0:T(8,128)(2,1)S(1)} collective-permute-done((bf16[4,208,384]{2,1,0:T(8,128)(2,1)S(1)}, bf16[4,208,384]{2,1,0:T(8,128)(2,1)S(1)}, u32[]{:S(2)}, u32[]{:S(2)}) %collective-permute-start.5) | collective-permute-done | bytes 639008 | tf_op jit(solution)/shard_map/ppermute | solution.py:836
  65.3 25.6 %cross_attn_forward.1 = (f32[1024,768]{1,0:T(8,128)}, bf16[8,128,768]{2,1,0:T(8,128)(2,1)}, bf16[8,304,768]{2,1,0:T(8,128)(2,1)}, bf16[8,304,768]{2,1,0:T(8,128)...) custom-call(s32[2]{0:T(128)} %pad_add_fusion.1.info, bf16[8,128,768]{2,1,0:T(8,128)(2,1)} %lat.1, ...), custom_call_target="tpu_custom_call" | custom-call | flops 10066329600 | bytes 31260672 | tf_op jit(solution)/shard_map/cross_attn_forward/pallas_call | solution.py:193
  96.8 10.8 %collective-permute-done.14.refs_3_ = bf16[4,192,384]{2,1,0:T(8,128)(2,1)S(1)} collective-permute-done((bf16[4,192,384]{2,1,0:T(8,128)(2,1)S(1)}, bf16[4,192,384]{2,1,0:T(8,128)(2,1)S(1)}, u32[]{:S(2)}, u32[]{:S(2)}) %collective-permute-start.14) | collective-permute-done | bytes 589856 | tf_op jit(solution)/shard_map/ppermute | solution.py:833
  115.7 21.4 %cross_mlp_forward.1 = (f32[1024,768]{1,0:T(8,128)}, bf16[1024,3072]{1,0:T(8,128)(2,1)}, bf16[1024,3072]{1,0:T(8,128)(2,1)}) custom-call(s32[2]{0:T(128)} %pad_add_fusion.1.info, f32[1024,768]{1,0:T(8,128)} %get-tuple-element.126.res, bf16[1024,768]{1,0:T(8,128)(2,1)} %bitcast.171, f32[1024,1]{1,0:T(8,128)} %copy.52.keep.keep_rows, f32[16,768]{1,0:T(8,128)} %reshape.279.vec, ...), custom_call_target="tpu_custom_call" | custom-call | flops 9663676416 | bytes 29884416 | tf_op jit(solution)/shard_map/cross_mlp_forward/pallas_call | solution.py:193
  139.4 6.9 %collective-permute-done.23.refs_3_ = bf16[4,96,384]{2,1,0:T(8,128)(2,1)S(1)} collective-permute-done((bf16[4,96,384]{2,1,0:T(8,128)(2,1)S(1)}, bf16[4,96,384]{2,1,0:T(8,128)(2,1)S(1)}, u32[]{:S(2)}, u32[]{:S(2)}) %collective-permute-start.23) | collective-permute-done | bytes 294944 | tf_op jit(solution)/shard_map/ppermute | solution.py:833
  151.9 15.8 %self_attn_forward.1 = (f32[1024,768]{1,0:T(8,128)}, bf16[8,128,768]{2,1,0:T(8,128)(2,1)}, bf16[8,128,768]{2,1,0:T(8,128)(2,1)}, bf16[8,128,768]{2,1,0:T(8,128)(...) custom-call(s32[2]{0:T(128)} %pad_add_fusion.1.info, f32[1024,768]{1,0:T(8,128)} %get-tuple-element.130.mid, ...), custom_call_target="tpu_custom_call" | custom-call | flops 5637144576 | bytes 20447232 | tf_op jit(solution)/shard_map/self_attn_forward/pallas_call | solution.py:193
  167.7 5.5 %collective-permute-done.30.refs_1_ = bf16[4,384,384]{2,1,0:T(8,128)(2,1)S(1)} collective-permute-done((bf16[4,384,384]{2,1,0:T(8,128)(2,1)S(1)}, bf16[4,384,384]{2,1,0:T(8,128)(2,1)S(1)}, u32[]{:S(2)}, u32[]{:S(2)}) %collective-permute-start.30) | collective-permute-done | bytes 1179680 | tf_op jit(solution)/shard_map/ppermute | solution.py:833
  176.4 11.0 %collective-permute-done.33.refs_4_ = bf16[4,192,384]{2,1,0:T(8,128)(2,1)S(1)} collective-permute-done((bf16[4,192,384]{2,1,0:T(8,128)(2,1)S(1)}, bf16[4,192,384]{2,1,0:T(8,128)(2,1)S(1)}, u32[]{:S(2)}, u32[]{:S(2)}) %collective-permute-start.33) | collective-permute-done | bytes 589856 | tf_op jit(solution)/shard_map/ppermute | solution.py:836
  194.5 31.5 %self_mlp.1 = (bf16[1024,768]{1,0:T(8,128)(2,1)}, f32[1024,768]{1,0:T(8,128)}, bf16[1024,768]{1,0:T(8,128)(2,1)}, f32[8,768]{1,0:T(8,128)}, bf16[1024,768]{1,0:T...) custom-call(s32[2]{0:T(128)} %pad_add_fusion.1.info, f32[1024,768]{1,0:T(8,128)} %get-tuple-element.134.res, ...), custom_call_target="tpu_custom_call" | custom-call | flops 19327352832 | bytes 34603008 | tf_op jit(solution)/shard_map/self_mlp/pallas_call | solution.py:193
  226.0 18.1 %self_mlp_grads.1 = (bf16[4,4,384,384]{3,2,1,0:T(8,128)(2,1)}, bf16[4,4,384,384]{3,2,1,0:T(8,128)(2,1)}) custom-call(s32[2]{0:T(128)} %pad_add_fusion.1.info, bf16[1024,768]{1,0:T(8,128)(2,1)} %get-tuple-element.140.h, bf16[1024,3072]{1,0:T(8,128)(2,1)} %get-tuple-element.141.du, bf16[1024,3072]{1,0:T(8,128)(2,1)} %get-tuple-element.142.e, ...), custom_call_target="tpu_custom_call" | custom-call | flops 9663676416 | bytes 25165824 | tf_op jit(solution)/shard_map/self_mlp_grads/pallas_call | solution.py:193
  244.6 20.3 %self_attn_back.1 = (f32[1024,768]{1,0:T(8,128)}, f32[8,768]{1,0:T(8,128)}, bf16[8,128,768]{2,1,0:T(8,128)(2,1)}, bf16[8,128,768]{2,1,0:T(8,128)(2,1)}, bf16[8,1...) custom-call(s32[2]{0:T(128)} %pad_add_fusion.1.info, f32[1024,768]{1,0:T(8,128)} %get-tuple-element.144.total, ...), custom_call_target="tpu_custom_call" | custom-call | flops 6442450944 | bytes 29884416 | tf_op jit(solution)/shard_map/self_attn_back/pallas_call | solution.py:193
  269.7 21.3 %cross_mlp_back.1 = (f32[1024,768]{1,0:T(8,128)}, bf16[1024,768]{1,0:T(8,128)(2,1)}, f32[8,768]{1,0:T(8,128)}, bf16[1024,768]{1,0:T(8,128)(2,1)}, bf16[1024,3072]{1,0:T(8,128)(2,1)}, /*index=5*/bf16[1024,768]{1,0:T(8,128)(2,1)}) custom-call(s32[2]{0:T(128)} %pad_add_fusion.1.info, f32[1024,768]{1,0:T(8,128)} %get-tuple-element.154.up_grad, ...), custom_call_target="tpu_custom_call" | custom-call | flops 9663676416 | bytes 36175872 | tf_op jit(solution)/shard_map/cross_mlp_back/pallas_call | solution.py:193
  297.0 17.4 %cross_mlp_grads.1 = (bf16[4,4,384,384]{3,2,1,0:T(8,128)(2,1)}, bf16[4,4,384,384]{3,2,1,0:T(8,128)(2,1)}) custom-call(s32[2]{0:T(128)} %pad_add_fusion.1.info, bf16[1024,768]{1,0:T(8,128)(2,1)} %get-tuple-element.160.h, bf16[1024,3072]{1,0:T(8,128)(2,1)} %get-tuple-element.161.du, bf16[1024,3072]{1,0:T(8,128)(2,1)} %get-tuple-element.162.e, ...), custom_call_target="tpu_custom_call" | custom-call | flops 9663676416 | bytes 25165824 | tf_op jit(solution)/shard_map/cross_mlp_grads/pallas_call | solution.py:193
  316.9 10.1 %self_attn_grads.1 = (bf16[4,4,192,384]{3,2,1,0:T(8,128)(2,1)}, bf16[4,4,192,384]{3,2,1,0:T(8,128)(2,1)}) custom-call(s32[2]{0:T(128)} %pad_add_fusion.1.info, bf16[8,128,768]{2,1,0:T(8,128)(2,1)} %get-tuple-element.170.refs_0_, bf16[8,128,768]{2,1,0:T(8,128)(2,1)} %get-tuple-element.172.refs_1_, bf16[8,128,768]{2,1,0:T(8,128)(2,1)} %get-tuple-element.174.refs_2_, ...), custom_call_target="tpu_custom_call" | custom-call | flops 4831838208 | bytes 14155776 | tf_op jit(solution)/shard_map/self_attn_grads/pallas_call | solution.py:193
  337.4 21.7 %cross_attn_back_0.1 = (f32[8,768]{1,0:T(8,128)}, f32[1024,768]{1,0:T(8,128)}, f32[8,296,768]{2,1,0:T(8,128)}, bf16[8,128,768]{2,1,0:T(8,128)(2,1)}, bf16[8,128,...) custom-call(s32[2]{0:T(128)} %pad_add_fusion.1.info, ...), custom_call_target="tpu_custom_call" | custom-call | flops 5989466112 | bytes 31260672 | tf_op jit(solution)/shard_map/cross_attn_back_0/pallas_call | solution.py:193
  370.3 20.8 %cross_attn_back_1.1 = (f32[8,768]{1,0:T(8,128)}, f32[1024,768]{1,0:T(8,128)}, f32[8,296,768]{2,1,0:T(8,128)}, bf16[8,128,768]{2,1,0:T(8,128)(2,1)}, bf16[8,128,...) custom-call(s32[2]{0:T(128)} %pad_add_fusion.1.info, ...), custom_call_target="tpu_custom_call", output_to_operand_aliasing={{1}: (21, {}), {2}: (22, {}), {3}: (23, {}), {4}: (24, {}),... | custom-call | flops 5989466112 | bytes 31260672 | tf_op jit(solution)/shard_map/cross_attn_back_1/pallas_call | solution.py:193
  396.2 14.7 %cross_attn_grads.1 = (bf16[4,4,208,384]{3,2,1,0:T(8,128)(2,1)}, bf16[4,4,208,384]{3,2,1,0:T(8,128)(2,1)}) custom-call(s32[2]{0:T(128)} %pad_add_fusion.1.info, bf16[8,128,768]{2,1,0:T(8,128)(2,1)} %get-tuple-element.216.refs_0_, bf16[8,128,768]{2,1,0:T(8,128)(2,1)} %get-tuple-element.217.refs_1_, bf16[8,304,768]{2,1,0:T(8,128)(2,1)} %get-tuple-element.218.refs_2_, ...), custom_call_target="tpu_custom_call" | custom-call | flops 8153726976 | bytes 22216704 | tf_op jit(solution)/shard_map/cross_attn_grads/pallas_call | solution.py:193
  422.6 4.6 collective-permute-done.59
  438.5 4.9 collective-permute-done.66
  443.4 9.4 %collective-permute-done.58 = bf16[4,208,384]{2,1,0:T(8,128)(2,1)} collective-permute-done((bf16[4,208,384]{2,1,0:T(8,128)(2,1)}, bf16[4,208,384]{2,1,0:T(8,128)(2,1)}, u32[]{:S(2)}, u32[]{:S(2)}) %collective-permute-start.58) | collective-permute-done | bytes 639008 | tf_op jit(solution)/shard_map/ppermute | solution.py:833
  466.5 4.3 collective-permute-start.62
  470.9 12.2 %collective-permute-done.62 = bf16[208,384]{1,0:T(8,128)(2,1)S(1)} collective-permute-done((bf16[208,384]{1,0:T(8,128)(2,1)S(1)}, bf16[208,384]{1,0:T(8,128)(2,1)S(1)}, u32[]{:S(2)}, u32[]{:S(2)}) %collective-permute-start.62) | collective-permute-done | bytes 159776 | tf_op jit(solution)/shard_map/ppermute | solution.py:892
  (342 shorter events, 148.8 us)
Async XLA Ops:
  7.2 54.1 %all-gather.5.cloned.1.call-start = ((), (), s32[]{:S(2)}) async-start(), calls=%async_computation.6 | async-start | bytes 1474560 | tf_op jit(solution)/shard_map/all_gather | solution.py:845
  27.5 83.2 %all-gather.7.cloned.1.call-start = ((), (), s32[]{:S(2)}) async-start(), calls=%async_computation.7 | async-start | bytes 2211840 | tf_op jit(solution)/shard_map/all_gather | solution.py:845
  38.4 23.0 %collective-permute-start.7 = (bf16[4,208,384]{2,1,0:T(8,128)(2,1)S(1)}, bf16[4,208,384]{2,1,0:T(8,128)(2,1)S(1)}, u32[]{:S(2)}, u32[]{:S(2)}) collective-permute-start(bf16[4,208,384]{2,1,0:T(8,128)(2,1)S(1)} %bitcast.177), channel_id=1, source_target_pairs={{0,1},{1,0},{2,3},{3,2},{4,5},{5,4},{6,7},{7,6},{8,9},{9,8},{10,11... | collective-permute-start | bytes 1916936 | tf_op jit(solution)/shard_map/ppermute | solution.py:830
  58.5 355.7 %reduce-scatter.8.cloned.1.call-start = ((), (), s32[]{:S(2)}) async-start(), calls=%async_computation.5 | async-start | bytes 1474560 | tf_op jit(solution)/shard_map/reduce_scatter | solution.py:880
  61.3 29.6 %collective-permute-start.13 = (bf16[4,384,384]{2,1,0:T(8,128)(2,1)}, bf16[4,384,384]{2,1,0:T(8,128)(2,1)}, u32[]{:S(2)}, u32[]{:S(2)}) collective-permute-start(bf16[4,384,384]{2,1,0:T(8,128)(2,1)} %bitcast.237), channel_id=1, source_target_pairs={{0,4},{1,5},{2,6},{3,7},{4,0},{5,1},{6,2},{7,3},{8,12},{9,13},{10,... | collective-permute-start | bytes 3538952 | tf_op jit(solution)/shard_map/ppermute | solution.py:836
  62.9 28.4 %collective-permute-start.12 = (bf16[4,384,384]{2,1,0:T(8,128)(2,1)}, bf16[4,384,384]{2,1,0:T(8,128)(2,1)}, u32[]{:S(2)}, u32[]{:S(2)}) collective-permute-start(bf16[4,384,384]{2,1,0:T(8,128)(2,1)} %bitcast.238), channel_id=1, source_target_pairs={{0,2},{1,3},{2,0},{3,1},{4,6},{5,7},{6,4},{7,5},{8,10},{9,11},{10,... | collective-permute-start | bytes 3538952 | tf_op jit(solution)/shard_map/ppermute | solution.py:833
  64.5 47.4 %collective-permute-start.16 = (bf16[4,384,384]{2,1,0:T(8,128)(2,1)}, bf16[4,384,384]{2,1,0:T(8,128)(2,1)}, u32[]{:S(2)}, u32[]{:S(2)}) collective-permute-start(bf16[4,384,384]{2,1,0:T(8,128)(2,1)} %bitcast.239), channel_id=1, source_target_pairs={{0,1},{1,0},{2,3},{3,2},{4,5},{5,4},{6,7},{7,6},{8,9},{9,8},{10,11... | collective-permute-start | bytes 3538952 | tf_op jit(solution)/shard_map/ppermute | solution.py:830
  111.9 25.3 %collective-permute-start.22 = (bf16[4,192,384]{2,1,0:T(8,128)(2,1)S(1)}, bf16[4,192,384]{2,1,0:T(8,128)(2,1)S(1)}, u32[]{:S(2)}, u32[]{:S(2)}) collective-permute-start(bf16[4,192,384]{2,1,0:T(8,128)(2,1)S(1)} %slice.509.refs_0_), channel_id=1, source_target_pairs={{0,4},{1,5},{2,6},{3,7},{4,0},{5,1},{6,2},{7,3},{8,12},{9,13},{10,... | collective-permute-start | bytes 1769480 | tf_op jit(solution)/shard_map/ppermute | solution.py:836
  113.1 24.1 %collective-permute-start.21 = (bf16[4,192,384]{2,1,0:T(8,128)(2,1)S(1)}, bf16[4,192,384]{2,1,0:T(8,128)(2,1)S(1)}, u32[]{:S(2)}, u32[]{:S(2)}) collective-permute-start(bf16[4,192,384]{2,1,0:T(8,128)(2,1)S(1)} %slice.509.refs_0_), channel_id=1, source_target_pairs={{0,2},{1,3},{2,0},{3,1},{4,6},{5,7},{6,4},{7,5},{8,10},{9,11},{10,... | collective-permute-start | bytes 1769480 | tf_op jit(solution)/shard_map/ppermute | solution.py:833
  146.4 26.9 %collective-permute-start.30 = (bf16[4,384,384]{2,1,0:T(8,128)(2,1)S(1)}, bf16[4,384,384]{2,1,0:T(8,128)(2,1)S(1)}, u32[]{:S(2)}, u32[]{:S(2)}) collective-permute-start(bf16[4,384,384]{2,1,0:T(8,128)(2,1)S(1)} %slice.510.refs_0_), channel_id=1, source_target_pairs={{0,2},{1,3},{2,0},{3,1},{4,6},{5,7},{6,4},{7,5},{8,10},{9,11},{10,... | collective-permute-start | bytes 3538952 | tf_op jit(solution)/shard_map/ppermute | solution.py:833
  148.0 26.4 %collective-permute-start.31 = (bf16[4,384,384]{2,1,0:T(8,128)(2,1)S(1)}, bf16[4,384,384]{2,1,0:T(8,128)(2,1)S(1)}, u32[]{:S(2)}, u32[]{:S(2)}) collective-permute-start(bf16[4,384,384]{2,1,0:T(8,128)(2,1)S(1)} %slice.510.refs_0_), channel_id=1, source_target_pairs={{0,4},{1,5},{2,6},{3,7},{4,0},{5,1},{6,2},{7,3},{8,12},{9,13},{10,... | collective-permute-start | bytes 3538952 | tf_op jit(solution)/shard_map/ppermute | solution.py:836
  150.4 40.3 %collective-permute-start.34 = (bf16[4,384,384]{2,1,0:T(8,128)(2,1)S(1)}, bf16[4,384,384]{2,1,0:T(8,128)(2,1)S(1)}, u32[]{:S(2)}, u32[]{:S(2)}) collective-permute-start(bf16[4,384,384]{2,1,0:T(8,128)(2,1)S(1)} %slice.510.refs_0_), channel_id=1, source_target_pairs={{0,1},{1,0},{2,3},{3,2},{4,5},{5,4},{6,7},{7,6},{8,9},{9,8},{10,11... | collective-permute-start | bytes 3538952 | tf_op jit(solution)/shard_map/ppermute | solution.py:830
  267.4 23.6 %collective-permute-start.40 = (bf16[4,192,384]{2,1,0:T(8,128)(2,1)}, bf16[4,192,384]{2,1,0:T(8,128)(2,1)S(1)}, u32[]{:S(2)}, u32[]{:S(2)}) collective-permute-start(bf16[4,192,384]{2,1,0:T(8,128)(2,1)} %get-tuple-element.243), channel_id=1, source_target_pairs={{0,4},{1,5},{2,6},{3,7},{4,0},{5,1},{6,2},{7,3},{8,12},{9,13},{10,... | collective-permute-start | bytes 1769480 | tf_op jit(solution)/shard_map/ppermute | solution.py:836
  331.6 34.3 %collective-permute-start.49 = (bf16[4,4,192,384]{3,2,1,0:T(8,128)(2,1)}, bf16[4,4,192,384]{3,2,1,0:T(8,128)(2,1)}, u32[]{:S(2)}, u32[]{:S(2)}) collective-permute-start(bf16[4,4,192,384]{3,2,1,0:T(8,128)(2,1)} %get-tuple-element.198), channel_id=1, source_target_pairs={{0,1},{1,0},{2,3},{3,2},{4,5},{5,4},{6,7},{7,6},{8,9},{9,8},{10,11... | collective-permute-start | bytes 7077896 | tf_op jit(solution)/shard_map/ppermute | solution.py:830
  331.6 27.5 %collective-permute-start.47 = (bf16[4,192,384]{2,1,0:T(8,128)(2,1)}, bf16[4,192,384]{2,1,0:T(8,128)(2,1)}, u32[]{:S(2)}, u32[]{:S(2)}) collective-permute-start(bf16[4,192,384]{2,1,0:T(8,128)(2,1)} %get-tuple-element.239), channel_id=1, source_target_pairs={{0,4},{1,5},{2,6},{3,7},{4,0},{5,1},{6,2},{7,3},{8,12},{9,13},{10,... | collective-permute-start | bytes 1769480 | tf_op jit(solution)/shard_map/ppermute | solution.py:836
  332.6 26.5 %collective-permute-start.48 = (bf16[4,192,384]{2,1,0:T(8,128)(2,1)}, bf16[4,192,384]{2,1,0:T(8,128)(2,1)}, u32[]{:S(2)}, u32[]{:S(2)}) collective-permute-start(bf16[4,192,384]{2,1,0:T(8,128)(2,1)} %get-tuple-element.240), channel_id=1, source_target_pairs={{0,2},{1,3},{2,0},{3,1},{4,6},{5,7},{6,4},{7,5},{8,10},{9,11},{10,... | collective-permute-start | bytes 1769480 | tf_op jit(solution)/shard_map/ppermute | solution.py:833
  337.3 118.7 %reduce-scatter.4.cloned.1.call-start = ((), (), s32[]{:S(2)}) async-start(), calls=%async_computation.3 | async-start | bytes 1474560 | tf_op jit(solution)/shard_map/reduce_scatter | solution.py:880
  363.0 28.2 %collective-permute-start.53 = (bf16[2,384,384]{2,1,0:T(8,128)(2,1)}, bf16[2,384,384]{2,1,0:T(8,128)(2,1)S(1)}, u32[]{:S(2)}, u32[]{:S(2)}) collective-permute-start(bf16[2,384,384]{2,1,0:T(8,128)(2,1)} %get-tuple-element.256), channel_id=1, source_target_pairs={{0,4},{1,5},{2,6},{3,7},{4,0},{5,1},{6,2},{7,3},{8,12},{9,13},{10,... | collective-permute-start | bytes 1769480 | tf_op jit(solution)/shard_map/ppermute | solution.py:836
  365.2 25.9 %collective-permute-start.52 = (bf16[2,384,384]{2,1,0:T(8,128)(2,1)}, bf16[2,384,384]{2,1,0:T(8,128)(2,1)S(1)}, u32[]{:S(2)}, u32[]{:S(2)}) collective-permute-start(bf16[2,384,384]{2,1,0:T(8,128)(2,1)} %get-tuple-element.258), channel_id=1, source_target_pairs={{0,2},{1,3},{2,0},{3,1},{4,6},{5,7},{6,4},{7,5},{8,10},{9,11},{10,... | collective-permute-start | bytes 1769480 | tf_op jit(solution)/shard_map/ppermute | solution.py:833
  368.0 25.0 %collective-permute-start.50 = (bf16[4,96,384]{2,1,0:T(8,128)(2,1)}, bf16[4,96,384]{2,1,0:T(8,128)(2,1)S(1)}, u32[]{:S(2)}, u32[]{:S(2)}) collective-permute-start(bf16[4,96,384]{2,1,0:T(8,128)(2,1)} %get-tuple-element.249), channel_id=1, source_target_pairs={{0,4},{1,5},{2,6},{3,7},{4,0},{5,1},{6,2},{7,3},{8,12},{9,13},{10,... | collective-permute-start | bytes 884744 | tf_op jit(solution)/shard_map/ppermute | solution.py:836
  368.9 24.1 %collective-permute-start.51 = (bf16[4,96,384]{2,1,0:T(8,128)(2,1)}, bf16[4,96,384]{2,1,0:T(8,128)(2,1)}, u32[]{:S(2)}, u32[]{:S(2)}) collective-permute-start(bf16[4,96,384]{2,1,0:T(8,128)(2,1)} %get-tuple-element.250), channel_id=1, source_target_pairs={{0,2},{1,3},{2,0},{3,1},{4,6},{5,7},{6,4},{7,5},{8,10},{9,11},{10,... | collective-permute-start | bytes 884744 | tf_op jit(solution)/shard_map/ppermute | solution.py:833
  414.1 74.2 %reduce-scatter.6.cloned.1.call-start = ((), (), s32[]{:S(2)}) async-start(), calls=%async_computation.4 | async-start | bytes 737280 | tf_op jit(solution)/shard_map/reduce_scatter | solution.py:880
  420.7 22.7 %collective-permute-start.66 = (bf16[4,192,384]{2,1,0:T(8,128)(2,1)}, bf16[4,192,384]{2,1,0:T(8,128)(2,1)}, u32[]{:S(2)}, u32[]{:S(2)}) collective-permute-start(bf16[4,192,384]{2,1,0:T(8,128)(2,1)} %get-tuple-element.247), channel_id=1, source_target_pairs={{0,4},{1,5},{2,6},{3,7},{4,0},{5,1},{6,2},{7,3},{8,12},{9,13},{10,... | collective-permute-start | bytes 1769480 | tf_op jit(solution)/shard_map/ppermute | solution.py:836
  421.9 34.1 %collective-permute-start.65 = (bf16[4,192,384]{2,1,0:T(8,128)(2,1)}, bf16[4,192,384]{2,1,0:T(8,128)(2,1)}, u32[]{:S(2)}, u32[]{:S(2)}) collective-permute-start(bf16[4,192,384]{2,1,0:T(8,128)(2,1)} %get-tuple-element.248), channel_id=1, source_target_pairs={{0,2},{1,3},{2,0},{3,1},{4,6},{5,7},{6,4},{7,5},{8,10},{9,11},{10,... | collective-permute-start | bytes 1769480 | tf_op jit(solution)/shard_map/ppermute | solution.py:833
  (97 other events, 960.5 us)
Sparse Core Ops, SparseCore 0:
  27.6 31.4 all-gather.4
  61.3 40.1 all-gather.6
  337.4 31.0 reduce-scatter.7
  414.2 31.3 reduce-scatter.3
  462.4 25.7 reduce-scatter.5

commit v4 on v3

--- a/solution.py
+++ b/solution.py
@@ -388,12 +388,100 @@
     )
 
 
-def mlp_grads_kernel(info, h, du, e, dy, keep, send, stage, sems):
+def mlp_grads_kernel(info, h, du, e, dy, o_hbm, da_hbm, keep, send, stage, o, da, in_sems, sems):
     step = pl.program_id(0)
+    loads = [
+        pltpu.make_async_copy(o_hbm, o, in_sems.at[0]),
+        pltpu.make_async_copy(da_hbm, da, in_sems.at[1]),
+    ]
+
+    @pl.when(step == 0)
+    def _():
+        for load in loads:
+            load.start()
+
+    def square_copies(tile, begin):
+        view = stage.at[tile].reshape(4, 4, 48, D)
+        rows = pl.ds(pl.multiple_of(begin, 16), 48)
+        return grad_copies(
+            info,
+            lambda place, column: view.at[:, place, :, column],
+            (lambda i: keep.at[i, :, rows], lambda i: send.at[i, :, rows]),
+            sems.at[tile],
+        )
+
+    def down_copies(tile, z):
+        view = stage.at[tile].reshape(4, 192, D)
+        return grad_copies(
+            info,
+            lambda place, column: view.at[place, :, column],
+            (lambda i: keep.at[i, z, pl.ds(192, 192)], lambda i: send.at[i, z, pl.ds(192, 192)]),
+            sems.at[tile],
+        )
 
     @pl.when(step < 4)
     def _():
         stage[step] = dot(h[...], du[...], TN).astype(BF16)
+        for copy in square_copies(step, step * 48):
+            copy.start()
+
+    @pl.when((step >= 4) & (step < 8))
+    def _():
+        stage[step] = dot(e[...], dy[...], TN).astype(BF16)
+        for copy in down_copies(step, step - 4):
+            copy.start()
+
+    @pl.when(step == 8)
+    def _():
+        for load in loads:
+            load.wait()
+        stage[8] = dot(o[...], da[...], TN).astype(BF16)
+        for copy in square_copies(8, 384):
+            copy.start()
+        for tile in range(8):
+            for copy in down_copies(tile, 0):
+                copy.wait()
+        for copy in square_copies(8, 384):
+            copy.wait()
+
+
+def mlp_grads(name, info, h, du, e, dy, o, da):
+    m = h.shape[0]
+    return call(
+        mlp_grads_kernel,
+        name,
+        9,
+        [
+            SMALL,
+            whole_spec(m, D),
+            pl.BlockSpec((m, D), lambda i: (0, jnp.minimum(i, 3))),
+            pl.BlockSpec((m, D), lambda i: (0, jnp.clip(i - 4, 0, 3))),
+            whole_spec(m, D),
+            ANY,
+            ANY,
+        ],
+        [ANY, ANY],
+        [shaped((4, 4, 432, HALF), BF16)] * 2,
+        [
+            pltpu.VMEM((9, D, D), BF16),
+            pltpu.VMEM((m, D), BF16),
+            pltpu.VMEM((m, D), BF16),
+            pltpu.SemaphoreType.DMA((2,)),
+            pltpu.SemaphoreType.DMA((9, 8)),
+        ],
+        4 * m * D * FF + 2 * m * D * D,
+        m * (8 * D + 4 * FF) + 4 * D * FF,
+        (info, h, du, e, dy, o, da),
+    )
+
+
+def mlp_tiles(step, info, h, du, e, dy, stage, outs, sems):
+    keep, send = outs
+
+    @pl.when(step < 4)
+    def _():
+        at = pl.multiple_of(step * D, 128)
+        stage[step] = dot(h[...], du[:, pl.ds(at, D)], TN).astype(BF16)
         view = stage.at[step].reshape(4, 4, 48, D)
         rows = pl.ds(pl.multiple_of(step * 48, 16), 48)
         copies = grad_copies(
@@ -405,53 +493,48 @@
         for copy in copies:
             copy.start()
 
-    def down_copies(tile, z):
-        view = stage.at[tile].reshape(4, 192, D)
-        return grad_copies(
+    @pl.when(step >= 4)
+    def _():
+        z = step - 4
+        at = pl.multiple_of(z * D, 128)
+        stage[step] = dot(e[:, pl.ds(at, D)], dy[...], TN).astype(BF16)
+        view = stage.at[step].reshape(4, 192, D)
+        copies = grad_copies(
             info,
             lambda place, column: view.at[place, :, column],
             (lambda i: keep.at[i, z, pl.ds(192, 192)], lambda i: send.at[i, z, pl.ds(192, 192)]),
-            sems.at[tile],
+            sems.at[step],
         )
-
-    @pl.when(step >= 4)
-    def _():
-        stage[step] = dot(e[...], dy[...], TN).astype(BF16)
-        for copy in down_copies(step, step - 4):
+        for copy in copies:
             copy.start()
 
     @pl.when(step == 7)
     def _():
         for tile in range(8):
-            for copy in down_copies(tile, 0):
+            view = stage.at[tile].reshape(4, 192, D)
+            copies = grad_copies(
+                info,
+                lambda place, column: view.at[place, :, column],
+                (lambda i: keep.at[i, 0, pl.ds(192, 192)], lambda i: send.at[i, 0, pl.ds(192, 192)]),
+                sems.at[tile],
+            )
+            for copy in copies:
                 copy.wait()
 
 
-def mlp_grads(name, info, h, du, e, dy):
-    m = h.shape[0]
-    return call(
-        mlp_grads_kernel,
-        name,
-        8,
-        [
-            SMALL,
-            whole_spec(m, D),
-            pl.BlockSpec((m, D), lambda i: (0, jnp.minimum(i, 3))),
-            pl.BlockSpec((m, D), lambda i: (0, jnp.maximum(i - 4, 0))),
-            whole_spec(m, D),
-        ],
-        [ANY, ANY],
-        [shaped((4, 4, 384, HALF), BF16)] * 2,
-        [pltpu.VMEM((8, D, D), BF16), pltpu.SemaphoreType.DMA((8, 8))],
-        4 * m * D * FF,
-        m * (4 * D + 4 * FF) + 4 * D * FF,
-        (info, h, du, e, dy),
-    )
-
-
-def self_mlp_kernel(info, res, cot, vec, *refs):
-    pieces, outs, (w_up, w_down, sems) = (refs[:10], refs[10:17], refs[17:])
-    out, total, da, d_vec, h_all, du_all, e_all = outs
+def mlp_grad_scratch(m):
+    return [
+        pltpu.VMEM((m, D), BF16),
+        pltpu.VMEM((m, FF), BF16),
+        pltpu.VMEM((m, FF), BF16),
+        pltpu.VMEM((8, D, D), BF16),
+        pltpu.SemaphoreType.DMA((8, 8)),
+    ]
+
+
+def self_mlp_kernel(steps, info, res, cot, vec, *refs):
+    pieces, (out, total, da, d_vec, keep, send), scratch = (refs[:10], refs[10:16], refs[16:])
+    w_up, w_down, sems, h_all, du_all, e_all, stage, grad_sems = scratch
     step = pl.program_id(0)
     first = step == 0
     groups = mlp_copies(info, pieces, w_up, w_down, sems)
@@ -461,65 +544,70 @@
         start_all(groups)
         d_vec[...] = jnp.zeros_like(d_vec)
 
-    r = res[...]
-    dy = cot[...]
-    hat, scale = norm_parts(r)
-    gain = vec[7:8]
-    h = (hat * gain + vec[9:10]).astype(BF16)
-    h_all[...] = h
-
-    @pl.when(first)
-    def _():
-        wait_all(groups)
-
-    y = jnp.zeros((TALL, D), F32)
-    dh = jnp.zeros((TALL, D), F32)
-    parts = FF // CHUNK
-    u, d_act = (dot(h, up_part(w_up, 0)), dot(dy, down_part(w_down, 0), NT))
-    for j in range(parts):
-        lanes = slice(CHUNK * j, CHUNK * j + CHUNK)
-        following = (None, None)
-        if j + 1 < parts:
-            following = (dot(h, up_part(w_up, j + 1)), dot(dy, down_part(w_down, j + 1), NT))
-        value, slope = gelu_both(u)
-        value = value.astype(BF16)
-        e_all[:, lanes] = value
-        du = (d_act * slope).astype(BF16)
-        du_all[:, lanes] = du
-        y += dot(value, down_part(w_down, j))
-        dh += dot(du, up_part(w_up, j), NT)
-        u, d_act = following
-    out[...] = (r + y).astype(BF16)
-    dr, d_gain, d_shift = norm_back(hat, scale, gain, dh)
-    t = dy.astype(F32) + dr
-    total[...] = t
-    da[...] = t.astype(BF16)
-    d_vec[0:1] += d_gain
-    d_vec[1:2] += d_shift
+    @pl.when(step < steps)
+    def _():
+        rows = pl.ds(pl.multiple_of(step * ROWS, ROWS), ROWS)
+        r = res[...]
+        dy = cot[rows]
+        hat, scale = norm_parts(r)
+        gain = vec[7:8]
+        h = (hat * gain + vec[9:10]).astype(BF16)
+        h_all[rows] = h
+
+        @pl.when(first)
+        def _():
+            wait_all(groups)
+
+        y = jnp.zeros((ROWS, D), F32)
+        dh = jnp.zeros((ROWS, D), F32)
+        for j in range(4):
+            lanes = slice(D * j, D * j + D)
+            up = w_up[:, :, :, lanes].reshape(D, D)
+            down = w_down[j].reshape(D, D)
+            value, slope = gelu_both(dot(h, up))
+            value = value.astype(BF16)
+            e_all[rows, lanes] = value
+            y += dot(value, down)
+            du = (dot(dy, down, NT) * slope).astype(BF16)
+            du_all[rows, lanes] = du
+            dh += dot(du, up, NT)
+        out[...] = (r + y).astype(BF16)
+        dr, d_gain, d_shift = norm_back(hat, scale, gain, dh)
+        t = dy.astype(F32) + dr
+        total[...] = t
+        da[...] = t.astype(BF16)
+        d_vec[0:1] += d_gain
+        d_vec[1:2] += d_shift
+
+    @pl.when(step >= steps)
+    def _():
+        mlp_tiles(step - steps, info, h_all, du_all, e_all, cot, stage, (keep, send), grad_sems)
 
 
 def self_mlp(info, res, cot, vec, pieces):
     m = res.shape[0]
-    steps = m // TALL
-    spec = functools.partial(rows_spec, TALL)
+    steps = m // ROWS
+
+    def spec(width):
+        return pl.BlockSpec((ROWS, width), lambda i: (jnp.minimum(i, steps - 1), 0))
+
     return call(
-        self_mlp_kernel,
+        functools.partial(self_mlp_kernel, steps),
         "self_mlp",
-        steps,
-        [SMALL, spec(D), spec(D), whole_spec(16, D)] + [ANY] * 10,
-        [spec(D), spec(D), spec(D), whole_spec(8, D), spec(D), spec(FF), spec(FF)],
+        steps + 8,
+        [SMALL, spec(D), whole_spec(m, D), whole_spec(16, D)] + [ANY] * 10,
+        [spec(D), spec(D), spec(D), whole_spec(8, D), ANY, ANY],
         [
             shaped((m, D), BF16),
             shaped((m, D), F32),
             shaped((m, D), BF16),
             shaped((8, D), F32),
-            shaped((m, D), BF16),
-            shaped((m, FF), BF16),
-            shaped((m, FF), BF16),
+            shaped((4, 4, 384, HALF), BF16),
+            shaped((4, 4, 384, HALF), BF16),
         ],
-        MLP_SCRATCH,
-        8 * m * D * FF,
-        m * (D * 16 + 4 * FF) + 4 * D * FF,
+        MLP_SCRATCH + mlp_grad_scratch(m),
+        12 * m * D * FF,
+        m * D * 14 + 8 * D * FF,
         (info, res, cot, vec, *pieces),
     )
 
@@ -614,12 +702,12 @@
         )
 
     def last_copies():
-        rows = pl.ds(192, EXTRA)
+        rows = pl.ds(48 * len(pairs), EXTRA)
         return grad_copies(
             info,
             lambda place, column: last.at[:, :, column],
             (lambda i: keep.at[i, :, rows], lambda i: send.at[i, :, rows]),
-            sems.at[4],
+            sems.at[len(pairs)],
         )
 
     waited = set()
@@ -644,32 +732,32 @@
                 last[...] = jnp.broadcast_to(rows[None], (4, EXTRA, D))
                 for copy in last_copies():
                     copy.start()
-            if tile == 3:
+            if tile == len(pairs) - 1:
                 if vectors:
                     for copy in last_copies():
                         copy.wait()
-                for i in range(4):
+                for i in range(len(pairs)):
                     for copy in copies_of(i):
                         copy.wait()
 
 
 def attn_grads(name, info, arrays, pairs, vectors=()):
-    rows = 192 + (EXTRA if vectors else 0)
+    rows = 48 * len(pairs) + (EXTRA if vectors else 0)
     counts = [a.size // D for a in arrays]
     flops = sum(2 * counts[i] * D * D for i, _ in pairs)
     return call(
         functools.partial(attn_grads_kernel, pairs, counts),
         name,
-        4,
+        len(pairs),
         [SMALL] + [ANY] * len(arrays) + [whole_spec(8, D)] * len(vectors),
         [ANY, ANY],
         [shaped((4, 4, rows, HALF), BF16)] * 2,
         [pltpu.VMEM(a.shape, BF16) for a in arrays]
         + [
-            pltpu.VMEM((4, D, D), BF16),
+            pltpu.VMEM((len(pairs), D, D), BF16),
             pltpu.VMEM((4, EXTRA, D), BF16),
             pltpu.SemaphoreType.DMA((len(arrays),)),
-            pltpu.SemaphoreType.DMA((5, 8)),
+            pltpu.SemaphoreType.DMA((len(pairs) + 1, 8)),
         ],
         flops,
         sum(counts) * D * 2 + 8 * D * D,
@@ -883,11 +971,16 @@
         z = lax.div(lax.axis_index("dp"), 4)
         return (lax.rem(z, 2) == 1, z >= 2)
 
-    def scatter_z_by_hops(self, own):
-        odd, high = self.z_bits()
+
+    def near_z(self, own):
+        odd, _ = self.z_bits()
         even_blocks, odd_blocks = (own[0::2], own[1::2])
-        keep, send = (jnp.where(odd, a, b) for a, b in ((odd_blocks, even_blocks), (even_blocks, odd_blocks)))
-        total = keep + lax.ppermute(send, AX, self.to_z)
+        keep = jnp.where(odd, odd_blocks, even_blocks)
+        send = jnp.where(odd, even_blocks, odd_blocks)
+        return keep + lax.ppermute(send, AX, self.to_z)
+
+    def far_z(self, total):
+        _, high = self.z_bits()
         keep, send = (jnp.where(high, total[i], total[1 - i]) for i in (1, 0))
         return keep.astype(F32) + lax.ppermute(send, AX, self.to_far_z).astype(F32)
 
@@ -957,18 +1050,21 @@
     return jnp.stack(rows, axis=1).transpose(2, 0, 1, 3).reshape(EXTRA, D).astype(F32)
 
 
-def finish_attn(grid, total):
-    parts = [total[:192].reshape(4, 48, HALF)]
-    if total.shape[0] > 192:
-        parts.append(jnp.broadcast_to(total[192:], (2, EXTRA, HALF)).reshape(1, 2 * EXTRA, HALF))
+def finish_attn(grid, total, count):
+    parts = [total[: 48 * count].reshape(count, 48, HALF)]
+    if total.shape[0] > 48 * count:
+        vectors = jnp.broadcast_to(total[48 * count :], (2, EXTRA, HALF))
+        parts.append(vectors.reshape(1, 2 * EXTRA, HALF))
     rows = grid.to_rows(parts)
-    matrices = rows[:96].reshape(4, 24, D)
-    return (matrices[:3], matrices[3], rows[96:])
+    return (rows[: 24 * count].reshape(count, 24, D), rows[24 * count :])
 
 
 def finish_mlp(grid, total):
-    rows = grid.to_rows([total[:192].reshape(4, 48, HALF), total[192:].reshape(1, 192, HALF)])
-    return (rows[:96].reshape(4, 24, D).transpose(1, 0, 2).reshape(24, FF), rows[96:])
+    parts = [total[:192].reshape(4, 48, HALF), total[192:384].reshape(1, 192, HALF)]
+    if total.shape[0] > 384:
+        parts.append(total[384:].reshape(1, 48, HALF))
+    rows = grid.to_rows(parts)
+    return (rows[:96].reshape(4, 24, D).transpose(1, 0, 2).reshape(24, FF), rows[96:192], rows[192:])
 
 
 def unit_pieces(unit, split):
@@ -1000,21 +1096,29 @@
     return jnp.concatenate(terms, axis=-1).transpose(1, 0, 2, 3).astype(F32)
 
 
-def reduce_plain_attn(terms):
+def squares(unit, begin, count):
+    rows = [unit[:, :, begin + 48 * i : begin + 48 * i + 48] for i in range(count)]
+    return jnp.stack([part.reshape(D, D) for part in rows])
+
+
+def reduce_plain_attn(terms, count):
     scatter = functools.partial(lax.psum_scatter, axis_name=AX, tiled=True)
     unit = whole_terms(terms)
-    matrices = [unit[:, :, 48 * i : 48 * i + 48].reshape(D, D) for i in range(4)]
-    qkv = scatter(jnp.stack(matrices[:3]), scatter_dimension=1)
-    vectors = scatter(unit[0, 0, 192:], scatter_dimension=1) if unit.shape[2] > 192 else None
-    return (qkv, scatter(matrices[3], scatter_dimension=0), vectors)
+    vectors = unit[0, 0, 48 * count :]
+    if vectors.shape[0]:
+        vectors = scatter(vectors, scatter_dimension=1)
+    return (scatter(squares(unit, 0, count), scatter_dimension=1), vectors)
 
 
 def reduce_plain_mlp(terms):
     scatter = functools.partial(lax.psum_scatter, axis_name=AX, tiled=True)
     unit = whole_terms(terms)
     up = unit[:, :, :192].reshape(4, 4, 4, 48, D).transpose(0, 1, 3, 2, 4).reshape(D, FF)
-    down = unit[:, :, 192:].reshape(FF, D)
-    return (scatter(up, scatter_dimension=0), scatter(down, scatter_dimension=0))
+    down = unit[:, :, 192:384].reshape(FF, D)
+    out = None
+    if unit.shape[2] > 384:
+        out = scatter(squares(unit, 384, 1)[0], scatter_dimension=0)
+    return (scatter(up, scatter_dimension=0), scatter(down, scatter_dimension=0), out)
 
 
 def after(value, *events):
@@ -1047,8 +1151,7 @@
     own_res, sq, sk, sv, so, sp = self_attn_forward(info, mid, vec, sa)
     sm_far = grid.far(after(sm_near, own_res), MLP_SPLIT)
     sm = grid.both_cores(sm_own, sm_near, sm_far)
-    result, total, da, own_vec, h, du, own_e = self_mlp(info, own_res, cot_rows, vec, sm)
-    a_keep, a_send = mlp_grads("self_mlp_grads", info, h, du, own_e, cot_rows)
+    result, total, da, own_vec, a_keep, a_send = self_mlp(info, own_res, cot_rows, vec, sm)
 
     total, da = after((total, da), a_send)
     a_in = grid.swap_core(a_send)
@@ -1064,7 +1167,8 @@
     a_sides = grid.sides(a_keep, a_in, *after(a_far, total), 2)
     h = after(h, a_sides)
     a_near = grid.send_sides(a_sides[0])
-    c_keep, c_send = mlp_grads("cross_mlp_grads", info, h, du, e, dy)
+    o_rows = o.reshape(da.shape)
+    c_keep, c_send = mlp_grads("cross_mlp_grads", info, h, du, e, dy, o_rows, da)
 
     a_near = after(a_near, c_send)
     a_near = (a_near, grid.send_sides(after(a_sides[1], a_near)))
@@ -1074,7 +1178,7 @@
     b_keep, b_send = attn_grads("self_attn_grads", info, self_arrays, pairs)
 
     c_in = after(c_in, b_send)
-    c_diag = grid.diagonal(c_keep, c_in, MLP_SPLIT)
+    c_diag = grid.diagonal(c_keep, c_in, 216)
     a_sum = grid.own_column(a_keep, a_in, *after(a_near, b_send))
     total = after(total, c_diag, a_sum)
     a_sum = grid.scatter_z(a_sum)
@@ -1096,29 +1200,33 @@
     b_sides = grid.sides(b_keep, b_in, *b_far)[0]
     zl = after(zl, b_sides, c_near[0])
     b_near = grid.send_sides(b_sides)
-    pairs = ((0, 1), (2, 3), (2, 4), (5, 6))
-    arrays = (zl, dq, xl, dk, dv, o, da.reshape(o.shape))
+    pairs = ((0, 1), (2, 3), (2, 4))
+    arrays = (zl, dq, xl, dk, dv)
     vectors = (cross_vec, mlp_vec, self_vec, own_vec)
     d_keep, d_send = attn_grads("cross_attn_grads", info, arrays, pairs, vectors)
 
     c_near = after(c_near, d_send)
     d_in = grid.swap_core(after(d_send, c_near))
-    d_diag = grid.diagonal(d_keep, d_in, ATTN_SPLIT)
+    d_diag = grid.diagonal(d_keep, d_in, 80)
     c_sum = grid.scatter_z(grid.own_column(c_keep, c_in, *c_near))
     d_far = grid.send_diagonal(d_diag)
-    d_near = grid.send_sides(grid.sides(d_keep, d_in, *d_far)[0])
+    d_sides = grid.sides(d_keep, d_in, *d_far)[0]
+    d_near = grid.send_sides(d_sides)
     c_sum = after(c_sum, d_near)
-    b_sum = grid.scatter_z(grid.own_column(b_keep, b_in, after(b_near, d_near)))
-    d_sum = grid.scatter_z_by_hops(grid.own_column(d_keep, d_in, d_near))
-
-    s_up, s_down = finish_mlp(grid, a_sum)
-    s_qkv, s_out, _ = finish_attn(grid, b_sum)
-    c_up, c_down = finish_mlp(grid, c_sum)
-    c_qkv, c_out, vectors = finish_attn(grid, d_sum)
+    b_sum = grid.near_z(grid.own_column(b_keep, b_in, after(b_near, d_sides)))
+    d_sum = grid.near_z(grid.own_column(d_keep, d_in, d_near))
+    b_sum = grid.far_z(after(b_sum, d_near))
+    d_sum = grid.far_z(d_sum)
+    b_sum = after(b_sum, d_sum)
+
+    s_up, s_down, _ = finish_mlp(grid, a_sum)
+    s_proj, _ = finish_attn(grid, b_sum, 4)
+    c_up, c_down, c_out = finish_mlp(grid, c_sum)
+    c_qkv, vectors = finish_attn(grid, d_sum, 3)
     at = 24 * (2 * lax.axis_index("dp") + grid.core)
     vectors = lax.dynamic_slice_in_dim(vectors, at, 24, 1)
     cross_grads = (vectors[0:3], vectors[3:6], c_qkv, c_out, c_up, c_down)
-    self_grads = (vectors[6:8], vectors[8:10], s_qkv, s_out, s_up, s_down)
+    self_grads = (vectors[6:8], vectors[8:10], s_proj[:3], s_proj[3], s_up, s_down)
     return ((result, d_lat, d_inp), cross_grads + self_grads)
 
 
@@ -1129,27 +1237,26 @@
     res, q, k, v, o, p = cross_attn_forward(info, latents, inputs, bias, vec, ca)
     mid, e, slope = cross_mlp_forward(info, res, lat_rows, keeping, vec, cm)
     own_res, sq, sk, sv, so, sp = self_attn_forward(info, mid, vec, sa)
-    result, total, da, own_vec, h, du, own_e = self_mlp(info, own_res, cot_rows, vec, sm)
-    a_terms = mlp_grads("self_mlp_grads", info, h, du, own_e, cot_rows)
+    result, total, da, own_vec, *a_terms = self_mlp(info, own_res, cot_rows, vec, sm)
     d_mid, self_vec, zl, dq, dk, dv = self_attn_back(info, total, da, sq, sk, sv, sp, mid, vec, sa)
     pairs = ((0, 1), (0, 2), (0, 3), (4, 5))
     arrays = (zl, dq, dk, dv, so, da.reshape(so.shape))
     b_terms = attn_grads("self_attn_grads", info, arrays, pairs)
     total, da, mlp_vec, h, du, dy = cross_mlp_back(info, d_mid, keeping, res, slope, vec, cm)
-    c_terms = mlp_grads("cross_mlp_grads", info, h, du, e, dy)
+    c_terms = mlp_grads("cross_mlp_grads", info, h, du, e, dy, o.reshape(da.shape), da)
     cross_vec, d_lat, d_inp, zl, dq, xl, dk, dv = cross_attn_back(
         0, 1, None, info, total, da, q, k, v, p, lat_rows, inputs, vec, ca
     )
-    pairs = ((0, 1), (2, 3), (2, 4), (5, 6))
-    arrays = (zl, dq, xl, dk, dv, o, da.reshape(o.shape))
+    pairs = ((0, 1), (2, 3), (2, 4))
+    arrays = (zl, dq, xl, dk, dv)
     vectors = (cross_vec, mlp_vec, self_vec, own_vec)
     d_terms = attn_grads("cross_attn_grads", info, arrays, pairs, vectors)
-    s_up, s_down = reduce_plain_mlp(a_terms)
-    s_qkv, s_out, _ = reduce_plain_attn(b_terms)
-    c_up, c_down = reduce_plain_mlp(c_terms)
-    c_qkv, c_out, vectors = reduce_plain_attn(d_terms)
+    s_up, s_down, _ = reduce_plain_mlp(a_terms)
+    s_proj, _ = reduce_plain_attn(b_terms, 4)
+    c_up, c_down, c_out = reduce_plain_mlp(c_terms)
+    c_qkv, vectors = reduce_plain_attn(d_terms, 3)
     cross_grads = (vectors[0:3], vectors[3:6], c_qkv, c_out, c_up, c_down)
-    self_grads = (vectors[6:8], vectors[8:10], s_qkv, s_out, s_up, s_down)
+    self_grads = (vectors[6:8], vectors[8:10], s_proj[:3], s_proj[3], s_up, s_down)
     return ((result, d_lat, d_inp), cross_grads + self_grads)
 
 

time: 503 us -> 489 us (0.972)
  waiting for transfers between devices: 120 us -> 110 us
    ppermute x18, waiting for transfers between devices: 44 us -> 29.9 us  [swap_x(): return lax.ppermute(value, AX, self.to_x)]
    pallas_call x12 -> x11, Pallas kernels: 239 us -> 236 us  [call(): pl.pallas_call(kernel, grid=(grid,), in_specs=in_specs, out_specs=out_spe...]
    ppermute x2 -> x4, waiting for transfers between devices: 16.2 us -> 16.9 us  [the longest x2 9.09 us: near_z(): return keep + lax.ppermute(send, AX, self.to_z)]
  transfers between devices with their start and end apart: 74 -> 75, of which waited for: 27 -> 25; matrix products, arithmetic and copies ran while one was open for 9% -> 9% of each run, Pallas kernels for 38% -> 39%
where the time goes in v4:
time: 489 us; the launch traced here: 486 us
  Pallas kernels  236 us (48%)
  waiting for transfers between devices  110 us (22%)
  starting transfers between devices  56.9 us (12%)
  other arithmetic  38.8 us (8%)
  local copies, waits for them, and re-layouts  28.8 us (6%)
  between operations  15.2 us (3%)
    pallas_call x11, Pallas kernels, call(): pl.pallas_call(kernel, grid=(grid,), in_specs=in_specs, out_specs=out_spe...  236 us
    ppermute x18, waiting for transfers between devices, swap_y(): return lax.ppermute(value, AX, self.to_y)  43.4 us
    ppermute x18, waiting for transfers between devices, swap_x(): return lax.ppermute(value, AX, self.to_x)  29.9 us
    ppermute x18, starting transfers between devices, swap_y(): return lax.ppermute(value, AX, self.to_y)  19.9 us
    ppermute x18, starting transfers between devices, swap_x(): return lax.ppermute(value, AX, self.to_x)  19.1 us
    add x4, other arithmetic, sides(): sums = (keep[1] + arrived[1] + for_x, keep[2] + arrived[2] + for_y)  11 us
  transfers between devices with their start and end apart: 75, of which 25 were waited for; matrix products, arithmetic and copies ran while one was open for 9% of the time, Pallas kernels for 39%

profile of v4, /device:TPU:0, one launch (start us, length us, event | category | flops | bytes accessed | tf_op | source)
XLA Modules:
  0.0 485.8 jit_solution(13443096314825615372)
XLA Ops:
  14.7 4.0 collective-permute-start.1
  18.8 7.8 %collective-permute-done.1 = bf16[208,384]{1,0:T(8,128)(2,1)S(1)} collective-permute-done((bf16[208,384]{1,0:T(8,128)(2,1)S(1)}, bf16[208,384]{1,0:T(8,128)(2,1)S(1)}, u32[]{:S(2)}, u32[]{:S(2)}) %collective-permute-start.1) | collective-permute-done | bytes 159776 | tf_op jit(solution)/shard_map/ppermute | solution.py:989
  28.3 7.5 %collective-permute-done.2 = bf16[2,208,384]{2,1,0:T(8,128)(2,1)S(1)} collective-permute-done((bf16[2,208,384]{2,1,0:T(8,128)(2,1)S(1)}, bf16[2,208,384]{2,1,0:T(8,128)(2,1)S(1)}, u32[]{:S(2)}, u32[]{:S(2)}) %collective-permute-start.2) | collective-permute-done | bytes 319520 | tf_op jit(solution)/shard_map/ppermute | solution.py:991
  39.0 12.1 %collective-permute-done.5.refs_2_ = bf16[4,208,384]{2,1,0:T(8,128)(2,1)S(1)} collective-permute-done((bf16[4,208,384]{2,1,0:T(8,128)(2,1)S(1)}, bf16[4,208,384]{2,1,0:T(8,128)(2,1)S(1)}, u32[]{:S(2)}, u32[]{:S(2)}) %collective-permute-start.5) | collective-permute-done | bytes 639008 | tf_op jit(solution)/shard_map/ppermute | solution.py:924
  65.9 25.6 %cross_attn_forward.1 = (f32[1024,768]{1,0:T(8,128)}, bf16[8,128,768]{2,1,0:T(8,128)(2,1)}, bf16[8,304,768]{2,1,0:T(8,128)(2,1)}, bf16[8,304,768]{2,1,0:T(8,128)...) custom-call(s32[2]{0:T(128)} %pad_add_fusion.1.info, bf16[8,128,768]{2,1,0:T(8,128)(2,1)} %lat.1, ...), custom_call_target="tpu_custom_call" | custom-call | flops 10066329600 | bytes 31260672 | tf_op jit(solution)/shard_map/cross_attn_forward/pallas_call | solution.py:193
  97.4 10.8 %collective-permute-done.14.refs_3_ = bf16[4,192,384]{2,1,0:T(8,128)(2,1)S(1)} collective-permute-done((bf16[4,192,384]{2,1,0:T(8,128)(2,1)S(1)}, bf16[4,192,384]{2,1,0:T(8,128)(2,1)S(1)}, u32[]{:S(2)}, u32[]{:S(2)}) %collective-permute-start.14) | collective-permute-done | bytes 589856 | tf_op jit(solution)/shard_map/ppermute | solution.py:921
  115.2 21.5 %cross_mlp_forward.1 = (f32[1024,768]{1,0:T(8,128)}, bf16[1024,3072]{1,0:T(8,128)(2,1)}, bf16[1024,3072]{1,0:T(8,128)(2,1)}) custom-call(s32[2]{0:T(128)} %pad_add_fusion.1.info, f32[1024,768]{1,0:T(8,128)} %get-tuple-element.125.res, bf16[1024,768]{1,0:T(8,128)(2,1)} %bitcast.171, f32[1024,1]{1,0:T(8,128)} %copy.51.keep.keep_rows, f32[16,768]{1,0:T(8,128)} %reshape.292.vec, ...), custom_call_target="tpu_custom_call" | custom-call | flops 9663676416 | bytes 29884416 | tf_op jit(solution)/shard_map/cross_mlp_forward/pallas_call | solution.py:193
  138.9 6.8 %collective-permute-done.23.refs_3_ = bf16[4,96,384]{2,1,0:T(8,128)(2,1)S(1)} collective-permute-done((bf16[4,96,384]{2,1,0:T(8,128)(2,1)S(1)}, bf16[4,96,384]{2,1,0:T(8,128)(2,1)S(1)}, u32[]{:S(2)}, u32[]{:S(2)}) %collective-permute-start.23) | collective-permute-done | bytes 294944 | tf_op jit(solution)/shard_map/ppermute | solution.py:921
  152.1 15.8 %self_attn_forward.1 = (f32[1024,768]{1,0:T(8,128)}, bf16[8,128,768]{2,1,0:T(8,128)(2,1)}, bf16[8,128,768]{2,1,0:T(8,128)(2,1)}, bf16[8,128,768]{2,1,0:T(8,128)(...) custom-call(s32[2]{0:T(128)} %pad_add_fusion.1.info, f32[1024,768]{1,0:T(8,128)} %get-tuple-element.129.mid, ...), custom_call_target="tpu_custom_call" | custom-call | flops 5637144576 | bytes 20447232 | tf_op jit(solution)/shard_map/self_attn_forward/pallas_call | solution.py:193
  167.9 4.8 collective-permute-done.30.refs_1_
  175.9 10.9 %collective-permute-done.33.refs_4_ = bf16[4,192,384]{2,1,0:T(8,128)(2,1)S(1)} collective-permute-done((bf16[4,192,384]{2,1,0:T(8,128)(2,1)S(1)}, bf16[4,192,384]{2,1,0:T(8,128)(2,1)S(1)}, u32[]{:S(2)}, u32[]{:S(2)}) %collective-permute-start.33) | collective-permute-done | bytes 589856 | tf_op jit(solution)/shard_map/ppermute | solution.py:924
  193.2 46.6 %self_mlp.1 = (bf16[1024,768]{1,0:T(8,128)(2,1)}, f32[1024,768]{1,0:T(8,128)}, bf16[1024,768]{1,0:T(8,128)(2,1)}, f32[8,768]{1,0:T(8,128)}, bf16[4,4,384,384]{3,...) custom-call(s32[2]{0:T(128)} %pad_add_fusion.1.info, f32[1024,768]{1,0:T(8,128)} %get-tuple-element.133.res, ...), custom_call_target="tpu_custom_call" | custom-call | flops 28991029248 | bytes 29884416 | tf_op jit(solution)/shard_map/self_mlp/pallas_call | solution.py:193
  240.1 20.4 %self_attn_back.1 = (f32[1024,768]{1,0:T(8,128)}, f32[8,768]{1,0:T(8,128)}, bf16[8,128,768]{2,1,0:T(8,128)(2,1)}, bf16[8,128,768]{2,1,0:T(8,128)(2,1)}, bf16[8,1...) custom-call(s32[2]{0:T(128)} %pad_add_fusion.1.info, f32[1024,768]{1,0:T(8,128)} %get-tuple-element.140.total, ...), custom_call_target="tpu_custom_call" | custom-call | flops 6442450944 | bytes 29884416 | tf_op jit(solution)/shard_map/self_attn_back/pallas_call | solution.py:193
  265.3 21.3 %cross_mlp_back.1 = (f32[1024,768]{1,0:T(8,128)}, bf16[1024,768]{1,0:T(8,128)(2,1)}, f32[8,768]{1,0:T(8,128)}, bf16[1024,768]{1,0:T(8,128)(2,1)}, bf16[1024,3072]{1,0:T(8,128)(2,1)}, /*index=5*/bf16[1024,768]{1,0:T(8,128)(2,1)}) custom-call(s32[2]{0:T(128)} %pad_add_fusion.1.info, f32[1024,768]{1,0:T(8,128)} %get-tuple-element.150.up_grad, ...), custom_call_target="tpu_custom_call" | custom-call | flops 9663676416 | bytes 36175872 | tf_op jit(solution)/shard_map/cross_mlp_back/pallas_call | solution.py:193
  292.6 19.2 %cross_mlp_grads.1 = (bf16[4,4,432,384]{3,2,1,0:T(8,128)(2,1)}, bf16[4,4,432,384]{3,2,1,0:T(8,128)(2,1)}) custom-call(s32[2]{0:T(128)} %pad_add_fusion.1.info, bf16[1024,768]{1,0:T(8,128)(2,1)} %get-tuple-element.156.h, bf16[1024,3072]{1,0:T(8,128)(2,1)} %get-tuple-element.157.du, bf16[1024,3072]{1,0:T(8,128)(2,1)} %get-tuple-element.158.e, ...), custom_call_target="tpu_custom_call" | custom-call | flops 10871635968 | bytes 28311552 | tf_op jit(solution)/shard_map/cross_mlp_grads/pallas_call | solution.py:193
  315.0 9.9 %self_attn_grads.1 = (bf16[4,4,192,384]{3,2,1,0:T(8,128)(2,1)}, bf16[4,4,192,384]{3,2,1,0:T(8,128)(2,1)}) custom-call(s32[2]{0:T(128)} %pad_add_fusion.1.info, bf16[8,128,768]{2,1,0:T(8,128)(2,1)} %get-tuple-element.168.refs_0_, bf16[8,128,768]{2,1,0:T(8,128)(2,1)} %get-tuple-element.170.refs_1_, bf16[8,128,768]{2,1,0:T(8,128)(2,1)} %get-tuple-element.172.refs_2_, ...), custom_call_target="tpu_custom_call" | custom-call | flops 4831838208 | bytes 14155776 | tf_op jit(solution)/shard_map/self_attn_grads/pallas_call | solution.py:193
  335.7 21.9 %cross_attn_back_0.1 = (f32[8,768]{1,0:T(8,128)}, f32[1024,768]{1,0:T(8,128)}, f32[8,296,768]{2,1,0:T(8,128)}, bf16[8,128,768]{2,1,0:T(8,128)(2,1)}, bf16[8,128,...) custom-call(s32[2]{0:T(128)} %pad_add_fusion.1.info, ...), custom_call_target="tpu_custom_call" | custom-call | flops 5989466112 | bytes 31260672 | tf_op jit(solution)/shard_map/cross_attn_back_0/pallas_call | solution.py:193
  369.3 20.9 %cross_attn_back_1.1 = (f32[8,768]{1,0:T(8,128)}, f32[1024,768]{1,0:T(8,128)}, f32[8,296,768]{2,1,0:T(8,128)}, bf16[8,128,768]{2,1,0:T(8,128)(2,1)}, bf16[8,128,...) custom-call(s32[2]{0:T(128)} %pad_add_fusion.1.info, ...), custom_call_target="tpu_custom_call", output_to_operand_aliasing={{1}: (21, {}), {2}: (22, {}), {3}: (23, {}), {4}: (24, {}),... | custom-call | flops 5989466112 | bytes 31260672 | tf_op jit(solution)/shard_map/cross_attn_back_1/pallas_call | solution.py:193
  395.1 13.1 %cross_attn_grads.1 = (bf16[4,4,160,384]{3,2,1,0:T(8,128)(2,1)}, bf16[4,4,160,384]{3,2,1,0:T(8,128)(2,1)}) custom-call(s32[2]{0:T(128)} %pad_add_fusion.1.info, bf16[8,128,768]{2,1,0:T(8,128)(2,1)} %get-tuple-element.213.refs_0_, bf16[8,128,768]{2,1,0:T(8,128)(2,1)} %get-tuple-element.214.refs_1_, bf16[8,304,768]{2,1,0:T(8,128)(2,1)} %get-tuple-element.215.refs_2_, ...), custom_call_target="tpu_custom_call" | custom-call | flops 6945767424 | bytes 19070976 | tf_op jit(solution)/shard_map/cross_attn_grads/pallas_call | solution.py:193
  418.5 15.8 %collective-permute-done.57 = bf16[4,80,384]{2,1,0:T(8,128)(2,1)S(1)} collective-permute-done((bf16[4,80,384]{2,1,0:T(8,128)(2,1)S(1)}, bf16[4,80,384]{2,1,0:T(8,128)(2,1)S(1)}, u32[]{:S(2)}, u32[]{:S(2)}) %collective-permute-start.57) | collective-permute-done | bytes 245792 | tf_op jit(solution)/shard_map/ppermute | solution.py:924
  444.7 5.5 %collective-permute-done.67 = bf16[2,192,384]{2,1,0:T(8,128)(2,1)S(1)} collective-permute-done((bf16[2,192,384]{2,1,0:T(8,128)(2,1)S(1)}, bf16[2,192,384]{2,1,0:T(8,128)(2,1)S(1)}, u32[]{:S(2)}, u32[]{:S(2)}) %collective-permute-start.67) | collective-permute-done | bytes 294944 | tf_op jit(solution)/shard_map/ppermute | solution.py:980
  453.1 4.6 collective-permute-start.68
  463.2 3.6 collective-permute-done.61
  469.2 4.9 collective-permute-done.62
  (351 shorter events, 135.2 us)
Async XLA Ops:
  7.2 54.7 %all-gather.5.cloned.1.call-start = ((), (), s32[]{:S(2)}) async-start(), calls=%async_computation.4 | async-start | bytes 1474560 | tf_op jit(solution)/shard_map/all_gather | solution.py:933
  28.2 83.1 %all-gather.7.cloned.1.call-start = ((), (), s32[]{:S(2)}) async-start(), calls=%async_computation.5 | async-start | bytes 2211840 | tf_op jit(solution)/shard_map/all_gather | solution.py:933
  39.0 23.0 %collective-permute-start.7 = (bf16[4,208,384]{2,1,0:T(8,128)(2,1)S(1)}, bf16[4,208,384]{2,1,0:T(8,128)(2,1)S(1)}, u32[]{:S(2)}, u32[]{:S(2)}) collective-permute-start(bf16[4,208,384]{2,1,0:T(8,128)(2,1)S(1)} %bitcast.176), channel_id=1, source_target_pairs={{0,1},{1,0},{2,3},{3,2},{4,5},{5,4},{6,7},{7,6},{8,9},{9,8},{10,11... | collective-permute-start | bytes 1916936 | tf_op jit(solution)/shard_map/ppermute | solution.py:918
  59.1 352.7 %reduce-scatter.5.cloned.1.call-start = ((), (), s32[]{:S(2)}) async-start(), calls=%async_computation.3 | async-start | bytes 1474560 | tf_op jit(solution)/shard_map/reduce_scatter | solution.py:968
  62.0 29.6 %collective-permute-start.13 = (bf16[4,384,384]{2,1,0:T(8,128)(2,1)}, bf16[4,384,384]{2,1,0:T(8,128)(2,1)}, u32[]{:S(2)}, u32[]{:S(2)}) collective-permute-start(bf16[4,384,384]{2,1,0:T(8,128)(2,1)} %bitcast.237), channel_id=1, source_target_pairs={{0,4},{1,5},{2,6},{3,7},{4,0},{5,1},{6,2},{7,3},{8,12},{9,13},{10,... | collective-permute-start | bytes 3538952 | tf_op jit(solution)/shard_map/ppermute | solution.py:924
  63.5 28.4 %collective-permute-start.12 = (bf16[4,384,384]{2,1,0:T(8,128)(2,1)}, bf16[4,384,384]{2,1,0:T(8,128)(2,1)}, u32[]{:S(2)}, u32[]{:S(2)}) collective-permute-start(bf16[4,384,384]{2,1,0:T(8,128)(2,1)} %bitcast.238), channel_id=1, source_target_pairs={{0,2},{1,3},{2,0},{3,1},{4,6},{5,7},{6,4},{7,5},{8,10},{9,11},{10,... | collective-permute-start | bytes 3538952 | tf_op jit(solution)/shard_map/ppermute | solution.py:921
  65.1 47.4 %collective-permute-start.16 = (bf16[4,384,384]{2,1,0:T(8,128)(2,1)}, bf16[4,384,384]{2,1,0:T(8,128)(2,1)}, u32[]{:S(2)}, u32[]{:S(2)}) collective-permute-start(bf16[4,384,384]{2,1,0:T(8,128)(2,1)} %bitcast.239), channel_id=1, source_target_pairs={{0,1},{1,0},{2,3},{3,2},{4,5},{5,4},{6,7},{7,6},{8,9},{9,8},{10,11... | collective-permute-start | bytes 3538952 | tf_op jit(solution)/shard_map/ppermute | solution.py:918
  112.5 24.3 %collective-permute-start.22 = (bf16[4,192,384]{2,1,0:T(8,128)(2,1)S(1)}, bf16[4,192,384]{2,1,0:T(8,128)(2,1)S(1)}, u32[]{:S(2)}, u32[]{:S(2)}) collective-permute-start(bf16[4,192,384]{2,1,0:T(8,128)(2,1)S(1)} %slice.531.refs_0_), channel_id=1, source_target_pairs={{0,4},{1,5},{2,6},{3,7},{4,0},{5,1},{6,2},{7,3},{8,12},{9,13},{10,... | collective-permute-start | bytes 1769480 | tf_op jit(solution)/shard_map/ppermute | solution.py:924
  113.6 23.1 %collective-permute-start.21 = (bf16[4,192,384]{2,1,0:T(8,128)(2,1)S(1)}, bf16[4,192,384]{2,1,0:T(8,128)(2,1)S(1)}, u32[]{:S(2)}, u32[]{:S(2)}) collective-permute-start(bf16[4,192,384]{2,1,0:T(8,128)(2,1)S(1)} %slice.531.refs_0_), channel_id=1, source_target_pairs={{0,2},{1,3},{2,0},{3,1},{4,6},{5,7},{6,4},{7,5},{8,10},{9,11},{10,... | collective-permute-start | bytes 1769480 | tf_op jit(solution)/shard_map/ppermute | solution.py:921
  145.9 26.9 %collective-permute-start.30 = (bf16[4,384,384]{2,1,0:T(8,128)(2,1)S(1)}, bf16[4,384,384]{2,1,0:T(8,128)(2,1)S(1)}, u32[]{:S(2)}, u32[]{:S(2)}) collective-permute-start(bf16[4,384,384]{2,1,0:T(8,128)(2,1)S(1)} %slice.532.refs_0_), channel_id=1, source_target_pairs={{0,2},{1,3},{2,0},{3,1},{4,6},{5,7},{6,4},{7,5},{8,10},{9,11},{10,... | collective-permute-start | bytes 3538952 | tf_op jit(solution)/shard_map/ppermute | solution.py:921
  147.5 26.3 %collective-permute-start.31 = (bf16[4,384,384]{2,1,0:T(8,128)(2,1)S(1)}, bf16[4,384,384]{2,1,0:T(8,128)(2,1)S(1)}, u32[]{:S(2)}, u32[]{:S(2)}) collective-permute-start(bf16[4,384,384]{2,1,0:T(8,128)(2,1)S(1)} %slice.532.refs_0_), channel_id=1, source_target_pairs={{0,4},{1,5},{2,6},{3,7},{4,0},{5,1},{6,2},{7,3},{8,12},{9,13},{10,... | collective-permute-start | bytes 3538952 | tf_op jit(solution)/shard_map/ppermute | solution.py:924
  149.9 40.3 %collective-permute-start.34 = (bf16[4,384,384]{2,1,0:T(8,128)(2,1)S(1)}, bf16[4,384,384]{2,1,0:T(8,128)(2,1)S(1)}, u32[]{:S(2)}, u32[]{:S(2)}) collective-permute-start(bf16[4,384,384]{2,1,0:T(8,128)(2,1)S(1)} %slice.532.refs_0_), channel_id=1, source_target_pairs={{0,1},{1,0},{2,3},{3,2},{4,5},{5,4},{6,7},{7,6},{8,9},{9,8},{10,11... | collective-permute-start | bytes 3538952 | tf_op jit(solution)/shard_map/ppermute | solution.py:918
  263.0 23.6 %collective-permute-start.40 = (bf16[4,192,384]{2,1,0:T(8,128)(2,1)}, bf16[4,192,384]{2,1,0:T(8,128)(2,1)S(1)}, u32[]{:S(2)}, u32[]{:S(2)}) collective-permute-start(bf16[4,192,384]{2,1,0:T(8,128)(2,1)} %get-tuple-element.241), channel_id=1, source_target_pairs={{0,4},{1,5},{2,6},{3,7},{4,0},{5,1},{6,2},{7,3},{8,12},{9,13},{10,... | collective-permute-start | bytes 1769480 | tf_op jit(solution)/shard_map/ppermute | solution.py:924
  329.7 35.1 %collective-permute-start.49 = (bf16[4,4,192,384]{3,2,1,0:T(8,128)(2,1)}, bf16[4,4,192,384]{3,2,1,0:T(8,128)(2,1)}, u32[]{:S(2)}, u32[]{:S(2)}) collective-permute-start(bf16[4,4,192,384]{3,2,1,0:T(8,128)(2,1)} %get-tuple-element.195), channel_id=1, source_target_pairs={{0,1},{1,0},{2,3},{3,2},{4,5},{5,4},{6,7},{7,6},{8,9},{9,8},{10,11... | collective-permute-start | bytes 7077896 | tf_op jit(solution)/shard_map/ppermute | solution.py:918
  329.7 28.0 %collective-permute-start.47 = (bf16[4,216,384]{2,1,0:T(8,128)(2,1)S(1)}, bf16[4,216,384]{2,1,0:T(8,128)(2,1)}, u32[]{:S(2)}, u32[]{:S(2)}) collective-permute-start(bf16[4,216,384]{2,1,0:T(8,128)(2,1)S(1)} %get-tuple-element.237), channel_id=1, source_target_pairs={{0,4},{1,5},{2,6},{3,7},{4,0},{5,1},{6,2},{7,3},{8,12},{9,13},{10,... | collective-permute-start | bytes 1990664 | tf_op jit(solution)/shard_map/ppermute | solution.py:924
  330.8 26.9 %collective-permute-start.48 = (bf16[4,216,384]{2,1,0:T(8,128)(2,1)}, bf16[4,216,384]{2,1,0:T(8,128)(2,1)}, u32[]{:S(2)}, u32[]{:S(2)}) collective-permute-start(bf16[4,216,384]{2,1,0:T(8,128)(2,1)} %get-tuple-element.238), channel_id=1, source_target_pairs={{0,2},{1,3},{2,0},{3,1},{4,6},{5,7},{6,4},{7,5},{8,10},{9,11},{10,... | collective-permute-start | bytes 1990664 | tf_op jit(solution)/shard_map/ppermute | solution.py:921
  335.6 114.6 %reduce-scatter.3.cloned.1.call-start = ((), (), s32[]{:S(2)}) async-start(), calls=%async_computation.2 | async-start | bytes 1658880 | tf_op jit(solution)/shard_map/reduce_scatter | solution.py:968
  361.9 28.3 %collective-permute-start.53 = (bf16[2,432,384]{2,1,0:T(8,128)(2,1)}, bf16[2,432,384]{2,1,0:T(8,128)(2,1)S(1)}, u32[]{:S(2)}, u32[]{:S(2)}) collective-permute-start(bf16[2,432,384]{2,1,0:T(8,128)(2,1)} %get-tuple-element.256), channel_id=1, source_target_pairs={{0,4},{1,5},{2,6},{3,7},{4,0},{5,1},{6,2},{7,3},{8,12},{9,13},{10,... | collective-permute-start | bytes 1990664 | tf_op jit(solution)/shard_map/ppermute | solution.py:924
  364.1 26.1 %collective-permute-start.52 = (bf16[2,432,384]{2,1,0:T(8,128)(2,1)}, bf16[2,432,384]{2,1,0:T(8,128)(2,1)}, u32[]{:S(2)}, u32[]{:S(2)}) collective-permute-start(bf16[2,432,384]{2,1,0:T(8,128)(2,1)} %get-tuple-element.258), channel_id=1, source_target_pairs={{0,2},{1,3},{2,0},{3,1},{4,6},{5,7},{6,4},{7,5},{8,10},{9,11},{10,... | collective-permute-start | bytes 1990664 | tf_op jit(solution)/shard_map/ppermute | solution.py:921
  366.9 25.0 %collective-permute-start.50 = (bf16[4,96,384]{2,1,0:T(8,128)(2,1)}, bf16[4,96,384]{2,1,0:T(8,128)(2,1)}, u32[]{:S(2)}, u32[]{:S(2)}) collective-permute-start(bf16[4,96,384]{2,1,0:T(8,128)(2,1)} %get-tuple-element.245), channel_id=1, source_target_pairs={{0,4},{1,5},{2,6},{3,7},{4,0},{5,1},{6,2},{7,3},{8,12},{9,13},{10,... | collective-permute-start | bytes 884744 | tf_op jit(solution)/shard_map/ppermute | solution.py:924
  367.9 24.0 %collective-permute-start.51 = (bf16[4,96,384]{2,1,0:T(8,128)(2,1)}, bf16[4,96,384]{2,1,0:T(8,128)(2,1)}, u32[]{:S(2)}, u32[]{:S(2)}) collective-permute-start(bf16[4,96,384]{2,1,0:T(8,128)(2,1)} %get-tuple-element.246), channel_id=1, source_target_pairs={{0,2},{1,3},{2,0},{3,1},{4,6},{5,7},{6,4},{7,5},{8,10},{9,11},{10,... | collective-permute-start | bytes 884744 | tf_op jit(solution)/shard_map/ppermute | solution.py:921
  413.0 26.6 %collective-permute-start.66 = (bf16[4,192,384]{2,1,0:T(8,128)(2,1)}, bf16[4,192,384]{2,1,0:T(8,128)(2,1)S(1)}, u32[]{:S(2)}, u32[]{:S(2)}) collective-permute-start(bf16[4,192,384]{2,1,0:T(8,128)(2,1)} %get-tuple-element.243), channel_id=1, source_target_pairs={{0,4},{1,5},{2,6},{3,7},{4,0},{5,1},{6,2},{7,3},{8,12},{9,13},{10,... | collective-permute-start | bytes 1769480 | tf_op jit(solution)/shard_map/ppermute | solution.py:924
  414.1 25.6 %collective-permute-start.65 = (bf16[4,192,384]{2,1,0:T(8,128)(2,1)S(1)}, bf16[4,192,384]{2,1,0:T(8,128)(2,1)S(1)}, u32[]{:S(2)}, u32[]{:S(2)}) collective-permute-start(bf16[4,192,384]{2,1,0:T(8,128)(2,1)S(1)} %copy-done.14), channel_id=1, source_target_pairs={{0,2},{1,3},{2,0},{3,1},{4,6},{5,7},{6,4},{7,5},{8,10},{9,11},{10,... | collective-permute-start | bytes 1769480 | tf_op jit(solution)/shard_map/ppermute | solution.py:921
  418.4 24.8 %collective-permute-start.70 = (f32[192,384]{1,0:T(8,128)S(1)}, f32[192,384]{1,0:T(8,128)S(1)}, u32[]{:S(2)}, u32[]{:S(2)}) collective-permute-start(f32[192,384]{1,0:T(8,128)S(1)} %fusion.13), channel_id=1, source_target_pairs={{0,1},{1,0},{2,3},{3,2},{4,5},{5,4},{6,7},{7,6},{8,9},{9,8},{10,11... | collective-permute-start | bytes 884744 | tf_op jit(solution)/shard_map/ppermute | solution.py:918
  (100 other events, 984.8 us)
Sparse Core Ops, SparseCore 0:
  28.4 31.4 all-gather.4
  62.0 40.0 all-gather.6
  335.8 31.0 reduce-scatter.4
  411.9 33.8 reduce-scatter.2

commit v5 on v4

--- a/solution.py
+++ b/solution.py
@@ -68,19 +68,19 @@
     place, core = (info[0], info[1])
     groups = []
     number = 0
-    for start, rows, ref, base in targets:
+    for start, rows, ref, base, z in targets:
         group = []
         for side in range(2):
             half = core if side == 0 else 1 - core
             column = pl.multiple_of(base + half * HALF, 128)
             for relative in range(4):
                 if relative < 3:
-                    source = pieces[5 * side + relative].at[:, pl.ds(start, rows)]
+                    source = pieces[5 * side + relative].at[z, pl.ds(start, rows)]
                 elif start < split:
-                    source = pieces[5 * side + 3].at[:, pl.ds(start, rows)]
+                    source = pieces[5 * side + 3].at[z, pl.ds(start, rows)]
                 else:
-                    source = pieces[5 * side + 4].at[:, pl.ds(start - split, rows)]
-                target = ref.at[:, place ^ relative, :, pl.ds(column, HALF)]
+                    source = pieces[5 * side + 4].at[z, pl.ds(start - split, rows)]
+                target = ref.at[z, place ^ relative, :, pl.ds(column, HALF)]
                 group.append(pltpu.make_async_copy(source, target, sems.at[number]))
                 number += 1
         groups.append(group)
@@ -88,13 +88,25 @@
 
 
 def attn_copies(info, pieces, weights, sems):
-    targets = [(48 * i, 48, weights[i], 0) for i in range(4)]
+    targets = [(48 * i, 48, weights[i], 0, slice(None)) for i in range(4)]
     return weight_copies(info, pieces, ATTN_SPLIT, targets, sems)
 
 
 def mlp_copies(info, pieces, w_up, w_down, sems):
-    targets = [(48 * i, 48, w_up, D * i) for i in range(4)] + [(192, 192, w_down, 0)]
-    return weight_copies(info, pieces, MLP_SPLIT, targets, sems)
+    targets = [(48 * i, 48, w_up, D * i, slice(None)) for i in range(4)]
+    targets += [(192, 192, w_down, 0, i) for i in range(4)]
+    groups = weight_copies(info, pieces, MLP_SPLIT, targets, sems)
+    return [groups[i] + groups[i + 4] for i in range(4)]
+
+
+def in_steps(step, steps, groups, body):
+    @pl.when(step == 0)
+    def _():
+        body(lambda i: wait_all(groups[i : i + 1]))
+
+    @pl.when((step > 0) & (step < steps))
+    def _():
+        body(lambda i: None)
 
 
 def start_all(groups):
@@ -117,7 +129,7 @@
 MLP_SCRATCH = [
     pltpu.VMEM((4, 4, 48, FF), BF16),
     pltpu.VMEM((4, 4, 192, D), BF16),
-    pltpu.SemaphoreType.DMA((40,)),
+    pltpu.SemaphoreType.DMA((64,)),
 ]
 
 
@@ -242,25 +254,29 @@
     def _():
         start_all(groups)
 
-    z = lat[...].reshape(ROWS, D).astype(F32)
-    hat, scale = norm_parts(z)
-    zl = (hat * vec[0:1] + vec[3:4]).astype(BF16)
-    xl = []
-    for i in range(ITEMS):
-        x = jnp.concatenate([inp[i].astype(F32), jnp.zeros((PAD - TOK, D), F32)], axis=0)
-        hat, scale = norm_parts(x)
-        xl.append((hat * vec[1:2] + vec[4:5]).astype(BF16))
-
-    @pl.when(first)
-    def _():
-        wait_all(groups)
-
-    q[...] = dot(zl, matrix(wq)).astype(BF16).reshape(ITEMS, LAT, D)
-    for i in range(ITEMS):
-        k[i] = dot(xl[i], matrix(wk)).astype(BF16)
-        v[i] = dot(xl[i], matrix(wv)).astype(BF16)
-        attend(i, q, k, v, jnp.broadcast_to(bias[i], (PAD, 256)), o, p, PAIRS)
-    r[...] = z + dot(o[...].reshape(ROWS, D), matrix(wo))
+    def body(wait):
+        z = lat[...].reshape(ROWS, D).astype(F32)
+        hat, scale = norm_parts(z)
+        zl = (hat * vec[0:1] + vec[3:4]).astype(BF16)
+        xl = []
+        for i in range(ITEMS):
+            x = jnp.concatenate([inp[i].astype(F32), jnp.zeros((PAD - TOK, D), F32)], axis=0)
+            hat, scale = norm_parts(x)
+            xl.append((hat * vec[1:2] + vec[4:5]).astype(BF16))
+
+        wait(0)
+        q[...] = dot(zl, matrix(wq)).astype(BF16).reshape(ITEMS, LAT, D)
+        for i in range(ITEMS):
+            if i == 0:
+                wait(1)
+                wait(2)
+            k[i] = dot(xl[i], matrix(wk)).astype(BF16)
+            v[i] = dot(xl[i], matrix(wv)).astype(BF16)
+            attend(i, q, k, v, jnp.broadcast_to(bias[i], (PAD, 256)), o, p, PAIRS)
+        wait(3)
+        r[...] = z + dot(o[...].reshape(ROWS, D), matrix(wo))
+
+    in_steps(pl.program_id(0), pl.num_programs(0), groups, body)
 
 
 def cross_attn_forward(info, lat, inp, bias, vec, pieces):
@@ -300,20 +316,23 @@
     def _():
         start_all(groups)
 
-    z = mid[...]
-    hat, scale = norm_parts(z)
-    zl = (hat * vec[6:7] + vec[8:9]).astype(BF16)
-
-    @pl.when(first)
-    def _():
-        wait_all(groups)
-
-    q[...] = dot(zl, matrix(wq)).astype(BF16).reshape(ITEMS, LAT, D)
-    k[...] = dot(zl, matrix(wk)).astype(BF16).reshape(ITEMS, LAT, D)
-    v[...] = dot(zl, matrix(wv)).astype(BF16).reshape(ITEMS, LAT, D)
-    for i in range(ITEMS):
-        attend(i, q, k, v, None, o, p, 6)
-    r[...] = z + dot(o[...].reshape(ROWS, D), matrix(wo))
+    def body(wait):
+        z = mid[...]
+        hat, scale = norm_parts(z)
+        zl = (hat * vec[6:7] + vec[8:9]).astype(BF16)
+
+        wait(0)
+        q[...] = dot(zl, matrix(wq)).astype(BF16).reshape(ITEMS, LAT, D)
+        wait(1)
+        k[...] = dot(zl, matrix(wk)).astype(BF16).reshape(ITEMS, LAT, D)
+        wait(2)
+        v[...] = dot(zl, matrix(wv)).astype(BF16).reshape(ITEMS, LAT, D)
+        for i in range(ITEMS):
+            attend(i, q, k, v, None, o, p, 6)
+        wait(3)
+        r[...] = z + dot(o[...].reshape(ROWS, D), matrix(wo))
+
+    in_steps(pl.program_id(0), pl.num_programs(0), groups, body)
 
 
 def self_attn_forward(info, mid, vec, pieces):
@@ -544,8 +563,7 @@
         start_all(groups)
         d_vec[...] = jnp.zeros_like(d_vec)
 
-    @pl.when(step < steps)
-    def _():
+    def body(wait):
         rows = pl.ds(pl.multiple_of(step * ROWS, ROWS), ROWS)
         r = res[...]
         dy = cot[rows]
@@ -554,14 +572,11 @@
         h = (hat * gain + vec[9:10]).astype(BF16)
         h_all[rows] = h
 
-        @pl.when(first)
-        def _():
-            wait_all(groups)
-
         y = jnp.zeros((ROWS, D), F32)
         dh = jnp.zeros((ROWS, D), F32)
         for j in range(4):
             lanes = slice(D * j, D * j + D)
+            wait(j)
             up = w_up[:, :, :, lanes].reshape(D, D)
             down = w_down[j].reshape(D, D)
             value, slope = gelu_both(dot(h, up))
@@ -578,6 +593,8 @@
         da[...] = t.astype(BF16)
         d_vec[0:1] += d_gain
         d_vec[1:2] += d_shift
+
+    in_steps(step, steps, groups, body)
 
     @pl.when(step >= steps)
     def _():
@@ -623,33 +640,35 @@
         start_all(groups)
         d_vec[...] = jnp.zeros_like(d_vec)
 
-    g = up_grad[...]
-    direct = keep_rows[...] * g
-    dy = direct.astype(BF16)
-    dy_all[...] = dy
-    hat, scale = norm_parts(res[...])
-    gain = vec[2:3]
-    h_all[...] = (hat * gain + vec[5:6]).astype(BF16)
-
-    @pl.when(first)
-    def _():
-        wait_all(groups)
-
-    dh = jnp.zeros((TALL, D), F32)
-    parts = FF // CHUNK
-    d_act = dot(dy, down_part(w_down, 0), NT)
-    for j in range(parts):
-        lanes = slice(CHUNK * j, CHUNK * j + CHUNK)
-        following = dot(dy, down_part(w_down, j + 1), NT) if j + 1 < parts else None
-        du = (d_act * slope[:, lanes].astype(F32)).astype(BF16)
-        du_all[:, lanes] = du
-        dh += dot(du, up_part(w_up, j), NT)
-        d_act = following
-    dr, d_gain, d_shift = norm_back(hat, scale, gain, dh)
-    total[...] = g + dr
-    da[...] = (direct + dr).astype(BF16)
-    d_vec[0:1] += d_gain
-    d_vec[1:2] += d_shift
+    def body(wait):
+        g = up_grad[...]
+        direct = keep_rows[...] * g
+        dy = direct.astype(BF16)
+        dy_all[...] = dy
+        hat, scale = norm_parts(res[...])
+        gain = vec[2:3]
+        h_all[...] = (hat * gain + vec[5:6]).astype(BF16)
+
+        dh = jnp.zeros((TALL, D), F32)
+        parts = FF // CHUNK
+        wait(0)
+        d_act = dot(dy, down_part(w_down, 0), NT)
+        for j in range(parts):
+            lanes = slice(CHUNK * j, CHUNK * j + CHUNK)
+            if j + 1 < parts:
+                wait(j + 1)
+            following = dot(dy, down_part(w_down, j + 1), NT) if j + 1 < parts else None
+            du = (d_act * slope[:, lanes].astype(F32)).astype(BF16)
+            du_all[:, lanes] = du
+            dh += dot(du, up_part(w_up, j), NT)
+            d_act = following
+        dr, d_gain, d_shift = norm_back(hat, scale, gain, dh)
+        total[...] = g + dr
+        da[...] = (direct + dr).astype(BF16)
+        d_vec[0:1] += d_gain
+        d_vec[1:2] += d_shift
+
+    in_steps(pl.program_id(0), pl.num_programs(0), groups, body)
 
 
 def cross_mlp_back(info, up_grad, keep_rows, res, slope, vec, pieces):
@@ -773,27 +792,29 @@
 
     @pl.when(first)
     def _():
-        start_all(groups)
+        start_all(groups[3:] + groups[:3])
         d_vec[...] = jnp.zeros_like(d_vec)
 
-    hat, scale = norm_parts(mid[...])
-    gain = vec[6:7]
-    zl[...] = (hat * gain + vec[8:9]).astype(BF16).reshape(ITEMS, LAT, D)
-
-    @pl.when(first)
-    def _():
-        wait_all(groups)
-
-    do_rows[...] = dot(da[...], matrix(wo), NT).astype(BF16).reshape(ITEMS, LAT, D)
-    for i in range(ITEMS):
-        attend_back(i, q, k, v, p, do_rows, dq, dk, dv, 6)
-    dz = dot(dq[...].reshape(ROWS, D), matrix(wq), NT)
-    dz += dot(dk[...].reshape(ROWS, D), matrix(wk), NT)
-    dz += dot(dv[...].reshape(ROWS, D), matrix(wv), NT)
-    dz, d_gain, d_shift = norm_back(hat, scale, gain, dz)
-    d_mid[...] = total[...] + dz
-    d_vec[0:1] += d_gain
-    d_vec[1:2] += d_shift
+    def body(wait):
+        hat, scale = norm_parts(mid[...])
+        gain = vec[6:7]
+        zl[...] = (hat * gain + vec[8:9]).astype(BF16).reshape(ITEMS, LAT, D)
+
+        wait(3)
+        do_rows[...] = dot(da[...], matrix(wo), NT).astype(BF16).reshape(ITEMS, LAT, D)
+        for i in range(ITEMS):
+            attend_back(i, q, k, v, p, do_rows, dq, dk, dv, 6)
+        for i in range(3):
+            wait(i)
+        dz = dot(dq[...].reshape(ROWS, D), matrix(wq), NT)
+        dz += dot(dk[...].reshape(ROWS, D), matrix(wk), NT)
+        dz += dot(dv[...].reshape(ROWS, D), matrix(wv), NT)
+        dz, d_gain, d_shift = norm_back(hat, scale, gain, dz)
+        d_mid[...] = total[...] + dz
+        d_vec[0:1] += d_gain
+        d_vec[1:2] += d_shift
+
+    in_steps(pl.program_id(0), pl.num_programs(0), groups, body)
 
 
 def self_attn_back(info, total, da, q, k, v, p, mid, vec, pieces):
@@ -829,34 +850,38 @@
 
     @pl.when(first)
     def _():
-        start_all(groups)
+        start_all(groups[3:] + groups[1:3] + groups[:1])
         d_vec[...] = before[...] if later else jnp.zeros_like(d_vec)
 
-    hat, scale = norm_parts(lat[...].astype(F32))
-    gain = vec[0:1]
-    zl[...] = (hat * gain + vec[3:4]).astype(BF16).reshape(ITEMS, LAT, D)
-
-    @pl.when(first)
-    def _():
-        wait_all(groups)
-
-    do_rows[...] = dot(da[...], matrix(wo), NT).astype(BF16).reshape(ITEMS, LAT, D)
-    for i in range(ITEMS):
-        attend_back(i, q, k, v, p, do_rows, dq, dk, dv, 6)
-        x = jnp.concatenate([inp[i].astype(F32), jnp.zeros((PAD - TOK, D), F32)], axis=0)
-        x_hat, x_scale = norm_parts(x)
-        x_gain = vec[1:2]
-        xl[i] = (x_hat * x_gain + vec[4:5]).astype(BF16)
-        dx = dot(dk[i], matrix(wk), NT) + dot(dv[i], matrix(wv), NT)
-        dx, d_gain, d_shift = norm_back(x_hat, x_scale, x_gain, dx)
-        d_inp[i] = dx[:TOK]
-        d_vec[1:2] += d_gain
-        d_vec[3:4] += d_shift
-    dz = dot(dq[...].reshape(ROWS, D), matrix(wq), NT)
-    dz, d_gain, d_shift = norm_back(hat, scale, gain, dz)
-    d_lat[...] = total[...] + dz
-    d_vec[0:1] += d_gain
-    d_vec[2:3] += d_shift
+    def body(wait):
+        hat, scale = norm_parts(lat[...].astype(F32))
+        gain = vec[0:1]
+        zl[...] = (hat * gain + vec[3:4]).astype(BF16).reshape(ITEMS, LAT, D)
+
+        wait(3)
+        do_rows[...] = dot(da[...], matrix(wo), NT).astype(BF16).reshape(ITEMS, LAT, D)
+        for i in range(ITEMS):
+            attend_back(i, q, k, v, p, do_rows, dq, dk, dv, 6)
+            x = jnp.concatenate([inp[i].astype(F32), jnp.zeros((PAD - TOK, D), F32)], axis=0)
+            x_hat, x_scale = norm_parts(x)
+            x_gain = vec[1:2]
+            xl[i] = (x_hat * x_gain + vec[4:5]).astype(BF16)
+            if i == 0:
+                wait(1)
+                wait(2)
+            dx = dot(dk[i], matrix(wk), NT) + dot(dv[i], matrix(wv), NT)
+            dx, d_gain, d_shift = norm_back(x_hat, x_scale, x_gain, dx)
+            d_inp[i] = dx[:TOK]
+            d_vec[1:2] += d_gain
+            d_vec[3:4] += d_shift
+        wait(0)
+        dz = dot(dq[...].reshape(ROWS, D), matrix(wq), NT)
+        dz, d_gain, d_shift = norm_back(hat, scale, gain, dz)
+        d_lat[...] = total[...] + dz
+        d_vec[0:1] += d_gain
+        d_vec[2:3] += d_shift
+
+    in_steps(pl.program_id(0), pl.num_programs(0), groups, body)
 
 
 def cross_attn_back(part, parts, before, info, total, da, q, k, v, p, lat, inp, vec, pieces):
@@ -1006,30 +1031,46 @@
     return jnp.concatenate([grid.by_core(mine, theirs), grid.by_core(theirs, mine)], axis=axis)
 
 
-def shard_of_block(qkv, w_out, w_up, w_down):
-    depth = w_out.shape[0]
-    attn = jnp.concatenate([qkv, w_out[None]], axis=0)
-    up = w_up.reshape(depth, 4, D).transpose(1, 0, 2)
-    return jnp.concatenate([attn.reshape(-1, D), up.reshape(-1, D), w_down], axis=0)
-
-
-def units_of_block(grid, mine, theirs):
-    attn = pack_rows(grid, mine[:96].reshape(4, 24, HALF), theirs[:96].reshape(4, 24, HALF), 1)
-    up = pack_rows(grid, mine[96:192].reshape(4, 24, HALF), theirs[96:192].reshape(4, 24, HALF), 1)
-    down = pack_rows(grid, mine[192:], theirs[192:], 0)
-    return (attn.reshape(192, HALF), jnp.concatenate([up.reshape(192, HALF), down], axis=0))
+def attn_shard(qkv, w_out):
+    return jnp.concatenate([qkv, w_out[None]], axis=0).reshape(-1, D)
+
+
+def mlp_shard(w_up, w_down):
+    up = w_up.reshape(w_up.shape[0], 4, D).transpose(1, 0, 2)
+    return jnp.concatenate([up.reshape(-1, D), w_down], axis=0)
+
+
+def attn_unit(grid, mine, theirs):
+    return pack_rows(grid, mine.reshape(4, 24, HALF), theirs.reshape(4, 24, HALF), 1).reshape(192, HALF)
+
+
+def mlp_unit(grid, mine, theirs):
+    up = pack_rows(grid, mine[:96].reshape(4, 24, HALF), theirs[:96].reshape(4, 24, HALF), 1)
+    down = pack_rows(grid, mine[96:], theirs[96:], 0)
+    return jnp.concatenate([up.reshape(192, HALF), down], axis=0)
+
+
+def after(value, *events):
+    return jax.tree.map(lambda x: lax.optimization_barrier((x, events))[0], value)
 
 
 def gather_planned(grid, cross, own_block):
     low = jnp.concatenate([cross[0], cross[1], own_block[0], own_block[1]], axis=0)
     low = jnp.pad(low, ((0, EXTRA - 10), (0, HALF - 24)))
-    shard = jnp.concatenate([shard_of_block(*cross[2:]), shard_of_block(*own_block[2:])], axis=0)
-    left, right = (shard[:, :HALF], shard[:, HALF:])
-    keep, send = (grid.by_core(left, right), grid.by_core(right, left))
+    def halves(shard):
+        left, right = (shard[:, :HALF], shard[:, HALF:])
+        return (grid.by_core(left, right), grid.by_core(right, left))
+
+    keep, send = halves(attn_shard(*cross[2:4]))
     arrived = grid.swap_core(jnp.concatenate([send, low], axis=0))
-    cross_attn, cross_mlp = units_of_block(grid, keep[:288], arrived[:288])
-    self_attn, self_mlp = units_of_block(grid, keep[288:], arrived[288:576])
-    vectors = pack_rows(grid, low[:, :24], arrived[576:, :24], 1)
+    cross_attn = attn_unit(grid, keep, arrived[:96])
+    rest = [mlp_shard(*cross[4:]), attn_shard(*own_block[2:4]), mlp_shard(*own_block[4:])]
+    rest_keep, rest_send = halves(after(jnp.concatenate(rest, axis=0), arrived))
+    rest_in = grid.swap_core(rest_send)
+    cross_mlp = mlp_unit(grid, rest_keep[:192], rest_in[:192])
+    self_attn = attn_unit(grid, rest_keep[192:288], rest_in[192:288])
+    self_mlp = mlp_unit(grid, rest_keep[288:], rest_in[288:])
+    vectors = pack_rows(grid, low[:, :24], arrived[96:, :24], 1)
     vectors = jnp.pad(vectors, ((0, 0), (0, HALF - 48)))
     cross_attn = jnp.concatenate([cross_attn, vectors], axis=0)
     own = grid.gather_z(jnp.concatenate([self_attn, self_mlp], axis=0))
@@ -1119,10 +1160,6 @@
     if unit.shape[2] > 384:
         out = scatter(squares(unit, 384, 1)[0], scatter_dimension=0)
     return (scatter(up, scatter_dimension=0), scatter(down, scatter_dimension=0), out)
-
-
-def after(value, *events):
-    return jax.tree.map(lambda x: lax.optimization_barrier((x, events))[0], value)
 
 
 def planned_steps(args, cross, own_block):

time: 489 us -> 486 us (level)
  transfers between devices with their start and end apart: 75 -> 76, of which waited for: 25 -> 26; matrix products, arithmetic and copies ran while one was open for 9% -> 10% of each run, Pallas kernels for 39% -> 39%
where the time goes in v5:
time: 486 us; the launch traced here: 482 us
  Pallas kernels  233 us (48%)
  waiting for transfers between devices  111 us (23%)
  starting transfers between devices  55.3 us (11%)
  other arithmetic  38.9 us (8%)
  local copies, waits for them, and re-layouts  28.5 us (6%)
  between operations  15.2 us (3%)
    pallas_call x11, Pallas kernels, call(): pl.pallas_call(kernel, grid=(grid,), in_specs=in_specs, out_specs=out_spe...  233 us
    ppermute x18, waiting for transfers between devices, swap_y(): return lax.ppermute(value, AX, self.to_y)  44.4 us
    ppermute x18, waiting for transfers between devices, swap_x(): return lax.ppermute(value, AX, self.to_x)  32.2 us
    ppermute x18, starting transfers between devices, swap_y(): return lax.ppermute(value, AX, self.to_y)  20.3 us
    ppermute x18, starting transfers between devices, swap_x(): return lax.ppermute(value, AX, self.to_x)  17.8 us
    add x4, other arithmetic, sides(): sums = (keep[1] + arrived[1] + for_x, keep[2] + arrived[2] + for_y)  11 us
  transfers between devices with their start and end apart: 76, of which 26 were waited for; matrix products, arithmetic and copies ran while one was open for 10% of the time, Pallas kernels for 39%

profile of v5, /device:TPU:0, one launch (start us, length us, event | category | flops | bytes accessed | tf_op | source)
XLA Modules:
  0.0 482.2 jit_solution(4783964371109413699)
XLA Ops:
  11.8 3.7 collective-permute-start.1
  15.8 7.8 %collective-permute-done.1 = bf16[208,384]{1,0:T(8,128)(2,1)S(1)} collective-permute-done((bf16[208,384]{1,0:T(8,128)(2,1)S(1)}, bf16[208,384]{1,0:T(8,128)(2,1)S(1)}, u32[]{:S(2)}, u32[]{:S(2)}) %collective-permute-start.1) | collective-permute-done | bytes 159776 | tf_op jit(solution)/shard_map/ppermute | solution.py:1014
  26.2 7.0 %collective-permute-done.2 = bf16[2,208,384]{2,1,0:T(8,128)(2,1)S(1)} collective-permute-done((bf16[2,208,384]{2,1,0:T(8,128)(2,1)S(1)}, bf16[2,208,384]{2,1,0:T(8,128)(2,1)S(1)}, u32[]{:S(2)}, u32[]{:S(2)}) %collective-permute-start.2) | collective-permute-done | bytes 319520 | tf_op jit(solution)/shard_map/ppermute | solution.py:1016
  36.6 12.3 %collective-permute-done.5.refs_2_ = bf16[4,208,384]{2,1,0:T(8,128)(2,1)S(1)} collective-permute-done((bf16[4,208,384]{2,1,0:T(8,128)(2,1)S(1)}, bf16[4,208,384]{2,1,0:T(8,128)(2,1)S(1)}, u32[]{:S(2)}, u32[]{:S(2)}) %collective-permute-start.5) | collective-permute-done | bytes 639008 | tf_op jit(solution)/shard_map/ppermute | solution.py:949
  64.8 25.3 %cross_attn_forward.1 = (f32[1024,768]{1,0:T(8,128)}, bf16[8,128,768]{2,1,0:T(8,128)(2,1)}, bf16[8,304,768]{2,1,0:T(8,128)(2,1)}, bf16[8,304,768]{2,1,0:T(8,128)...) custom-call(s32[2]{0:T(128)} %pad_add_fusion.1.info, bf16[8,128,768]{2,1,0:T(8,128)(2,1)} %lat.1, ...), custom_call_target="tpu_custom_call" | custom-call | flops 10066329600 | bytes 31260672 | tf_op jit(solution)/shard_map/cross_attn_forward/pallas_call | solution.py:205
  95.5 11.6 %collective-permute-done.15.refs_3_ = bf16[4,192,384]{2,1,0:T(8,128)(2,1)S(1)} collective-permute-done((bf16[4,192,384]{2,1,0:T(8,128)(2,1)S(1)}, bf16[4,192,384]{2,1,0:T(8,128)(2,1)S(1)}, u32[]{:S(2)}, u32[]{:S(2)}) %collective-permute-start.15) | collective-permute-done | bytes 589856 | tf_op jit(solution)/shard_map/ppermute | solution.py:946
  113.8 22.2 %cross_mlp_forward.1 = (f32[1024,768]{1,0:T(8,128)}, bf16[1024,3072]{1,0:T(8,128)(2,1)}, bf16[1024,3072]{1,0:T(8,128)(2,1)}) custom-call(s32[2]{0:T(128)} %pad_add_fusion.1.info, f32[1024,768]{1,0:T(8,128)} %get-tuple-element.126.res, bf16[1024,768]{1,0:T(8,128)(2,1)} %bitcast.171, f32[1024,1]{1,0:T(8,128)} %copy.51.keep.keep_rows, f32[16,768]{1,0:T(8,128)} %reshape.292.vec, ...), custom_call_target="tpu_custom_call" | custom-call | flops 9663676416 | bytes 29884416 | tf_op jit(solution)/shard_map/cross_mlp_forward/pallas_call | solution.py:205
  139.1 5.9 %collective-permute-done.24.refs_3_ = bf16[4,96,384]{2,1,0:T(8,128)(2,1)S(1)} collective-permute-done((bf16[4,96,384]{2,1,0:T(8,128)(2,1)S(1)}, bf16[4,96,384]{2,1,0:T(8,128)(2,1)S(1)}, u32[]{:S(2)}, u32[]{:S(2)}) %collective-permute-start.24) | collective-permute-done | bytes 294944 | tf_op jit(solution)/shard_map/ppermute | solution.py:946
  151.1 15.5 %self_attn_forward.1 = (f32[1024,768]{1,0:T(8,128)}, bf16[8,128,768]{2,1,0:T(8,128)(2,1)}, bf16[8,128,768]{2,1,0:T(8,128)(2,1)}, bf16[8,128,768]{2,1,0:T(8,128)(...) custom-call(s32[2]{0:T(128)} %pad_add_fusion.1.info, f32[1024,768]{1,0:T(8,128)} %get-tuple-element.131.mid, ...), custom_call_target="tpu_custom_call" | custom-call | flops 5637144576 | bytes 20447232 | tf_op jit(solution)/shard_map/self_attn_forward/pallas_call | solution.py:205
  166.6 5.5 %collective-permute-done.31.refs_1_ = bf16[4,384,384]{2,1,0:T(8,128)(2,1)S(1)} collective-permute-done((bf16[4,384,384]{2,1,0:T(8,128)(2,1)S(1)}, bf16[4,384,384]{2,1,0:T(8,128)(2,1)S(1)}, u32[]{:S(2)}, u32[]{:S(2)}) %collective-permute-start.31) | collective-permute-done | bytes 1179680 | tf_op jit(solution)/shard_map/ppermute | solution.py:946
  176.2 10.0 %collective-permute-done.34.refs_4_ = bf16[4,192,384]{2,1,0:T(8,128)(2,1)S(1)} collective-permute-done((bf16[4,192,384]{2,1,0:T(8,128)(2,1)S(1)}, bf16[4,192,384]{2,1,0:T(8,128)(2,1)S(1)}, u32[]{:S(2)}, u32[]{:S(2)}) %collective-permute-start.34) | collective-permute-done | bytes 589856 | tf_op jit(solution)/shard_map/ppermute | solution.py:949
  186.1 3.9 collective-permute-done.33.refs_3_
  193.8 45.3 %self_mlp.1 = (bf16[1024,768]{1,0:T(8,128)(2,1)}, f32[1024,768]{1,0:T(8,128)}, bf16[1024,768]{1,0:T(8,128)(2,1)}, f32[8,768]{1,0:T(8,128)}, bf16[4,4,384,384]{3,...) custom-call(s32[2]{0:T(128)} %pad_add_fusion.1.info, f32[1024,768]{1,0:T(8,128)} %get-tuple-element.135.res, ...), custom_call_target="tpu_custom_call" | custom-call | flops 28991029248 | bytes 29884416 | tf_op jit(solution)/shard_map/self_mlp/pallas_call | solution.py:205
  239.7 19.3 %self_attn_back.1 = (f32[1024,768]{1,0:T(8,128)}, f32[8,768]{1,0:T(8,128)}, bf16[8,128,768]{2,1,0:T(8,128)(2,1)}, bf16[8,128,768]{2,1,0:T(8,128)(2,1)}, bf16[8,1...) custom-call(s32[2]{0:T(128)} %pad_add_fusion.1.info, f32[1024,768]{1,0:T(8,128)} %get-tuple-element.142.total, ...), custom_call_target="tpu_custom_call" | custom-call | flops 6442450944 | bytes 29884416 | tf_op jit(solution)/shard_map/self_attn_back/pallas_call | solution.py:205
  263.1 20.6 %cross_mlp_back.1 = (f32[1024,768]{1,0:T(8,128)}, bf16[1024,768]{1,0:T(8,128)(2,1)}, f32[8,768]{1,0:T(8,128)}, bf16[1024,768]{1,0:T(8,128)(2,1)}, bf16[1024,3072]{1,0:T(8,128)(2,1)}, /*index=5*/bf16[1024,768]{1,0:T(8,128)(2,1)}) custom-call(s32[2]{0:T(128)} %pad_add_fusion.1.info, f32[1024,768]{1,0:T(8,128)} %get-tuple-element.152.up_grad, ...), custom_call_target="tpu_custom_call" | custom-call | flops 9663676416 | bytes 36175872 | tf_op jit(solution)/shard_map/cross_mlp_back/pallas_call | solution.py:205
  290.3 19.1 %cross_mlp_grads.1 = (bf16[4,4,432,384]{3,2,1,0:T(8,128)(2,1)}, bf16[4,4,432,384]{3,2,1,0:T(8,128)(2,1)}) custom-call(s32[2]{0:T(128)} %pad_add_fusion.1.info, bf16[1024,768]{1,0:T(8,128)(2,1)} %get-tuple-element.158.h, bf16[1024,3072]{1,0:T(8,128)(2,1)} %get-tuple-element.159.du, bf16[1024,3072]{1,0:T(8,128)(2,1)} %get-tuple-element.160.e, ...), custom_call_target="tpu_custom_call" | custom-call | flops 10871635968 | bytes 28311552 | tf_op jit(solution)/shard_map/cross_mlp_grads/pallas_call | solution.py:205
  312.0 10.1 %self_attn_grads.1 = (bf16[4,4,192,384]{3,2,1,0:T(8,128)(2,1)}, bf16[4,4,192,384]{3,2,1,0:T(8,128)(2,1)}) custom-call(s32[2]{0:T(128)} %pad_add_fusion.1.info, bf16[8,128,768]{2,1,0:T(8,128)(2,1)} %get-tuple-element.170.refs_0_, bf16[8,128,768]{2,1,0:T(8,128)(2,1)} %get-tuple-element.172.refs_1_, bf16[8,128,768]{2,1,0:T(8,128)(2,1)} %get-tuple-element.174.refs_2_, ...), custom_call_target="tpu_custom_call" | custom-call | flops 4831838208 | bytes 14155776 | tf_op jit(solution)/shard_map/self_attn_grads/pallas_call | solution.py:205
  332.9 22.0 %cross_attn_back_0.1 = (f32[8,768]{1,0:T(8,128)}, f32[1024,768]{1,0:T(8,128)}, f32[8,296,768]{2,1,0:T(8,128)}, bf16[8,128,768]{2,1,0:T(8,128)(2,1)}, bf16[8,128,...) custom-call(s32[2]{0:T(128)} %pad_add_fusion.1.info, ...), custom_call_target="tpu_custom_call" | custom-call | flops 5989466112 | bytes 31260672 | tf_op jit(solution)/shard_map/cross_attn_back_0/pallas_call | solution.py:205
  366.6 20.8 %cross_attn_back_1.1 = (f32[8,768]{1,0:T(8,128)}, f32[1024,768]{1,0:T(8,128)}, f32[8,296,768]{2,1,0:T(8,128)}, bf16[8,128,768]{2,1,0:T(8,128)(2,1)}, bf16[8,128,...) custom-call(s32[2]{0:T(128)} %pad_add_fusion.1.info, ...), custom_call_target="tpu_custom_call", output_to_operand_aliasing={{1}: (21, {}), {2}: (22, {}), {3}: (23, {}), {4}: (24, {}),... | custom-call | flops 5989466112 | bytes 31260672 | tf_op jit(solution)/shard_map/cross_attn_back_1/pallas_call | solution.py:205
  392.8 12.9 %cross_attn_grads.1 = (bf16[4,4,160,384]{3,2,1,0:T(8,128)(2,1)}, bf16[4,4,160,384]{3,2,1,0:T(8,128)(2,1)}) custom-call(s32[2]{0:T(128)} %pad_add_fusion.1.info, bf16[8,128,768]{2,1,0:T(8,128)(2,1)} %get-tuple-element.215.refs_0_, bf16[8,128,768]{2,1,0:T(8,128)(2,1)} %get-tuple-element.216.refs_1_, bf16[8,304,768]{2,1,0:T(8,128)(2,1)} %get-tuple-element.217.refs_2_, ...), custom_call_target="tpu_custom_call" | custom-call | flops 6945767424 | bytes 19070976 | tf_op jit(solution)/shard_map/cross_attn_grads/pallas_call | solution.py:205
  415.9 15.8 %collective-permute-done.58 = bf16[4,80,384]{2,1,0:T(8,128)(2,1)S(1)} collective-permute-done((bf16[4,80,384]{2,1,0:T(8,128)(2,1)S(1)}, bf16[4,80,384]{2,1,0:T(8,128)(2,1)S(1)}, u32[]{:S(2)}, u32[]{:S(2)}) %collective-permute-start.58) | collective-permute-done | bytes 245792 | tf_op jit(solution)/shard_map/ppermute | solution.py:949
  441.4 5.5 %collective-permute-done.68 = bf16[2,192,384]{2,1,0:T(8,128)(2,1)S(1)} collective-permute-done((bf16[2,192,384]{2,1,0:T(8,128)(2,1)S(1)}, bf16[2,192,384]{2,1,0:T(8,128)(2,1)S(1)}, u32[]{:S(2)}, u32[]{:S(2)}) %collective-permute-start.68) | collective-permute-done | bytes 294944 | tf_op jit(solution)/shard_map/ppermute | solution.py:1005
  450.2 4.0 collective-permute-start.69
  465.7 4.9 %collective-permute-done.63 = bf16[160,384]{1,0:T(8,128)(2,1)S(1)} collective-permute-done((bf16[160,384]{1,0:T(8,128)(2,1)S(1)}, bf16[160,384]{1,0:T(8,128)(2,1)S(1)}, u32[]{:S(2)}, u32[]{:S(2)}) %collective-permute-start.63) | collective-permute-done | bytes 122912 | tf_op jit(solution)/shard_map/ppermute | solution.py:1010
  (350 shorter events, 136.2 us)
Async XLA Ops:
  7.2 53.7 %all-gather.5.cloned.1.call-start = ((), (), s32[]{:S(2)}) async-start(), calls=%async_computation.4 | async-start | bytes 1474560 | tf_op jit(solution)/shard_map/all_gather | solution.py:958
  26.1 84.6 %all-gather.7.cloned.1.call-start = ((), (), s32[]{:S(2)}) async-start(), calls=%async_computation.5 | async-start | bytes 2211840 | tf_op jit(solution)/shard_map/all_gather | solution.py:958
  36.5 24.4 %collective-permute-start.7 = (bf16[4,208,384]{2,1,0:T(8,128)(2,1)S(1)}, bf16[4,208,384]{2,1,0:T(8,128)(2,1)S(1)}, u32[]{:S(2)}, u32[]{:S(2)}) collective-permute-start(bf16[4,208,384]{2,1,0:T(8,128)(2,1)S(1)} %bitcast.176), channel_id=1, source_target_pairs={{0,1},{1,0},{2,3},{3,2},{4,5},{5,4},{6,7},{7,6},{8,9},{9,8},{10,11... | collective-permute-start | bytes 1916936 | tf_op jit(solution)/shard_map/ppermute | solution.py:943
  57.0 352.1 %reduce-scatter.5.cloned.1.call-start = ((), (), s32[]{:S(2)}) async-start(), calls=%async_computation.3 | async-start | bytes 1474560 | tf_op jit(solution)/shard_map/reduce_scatter | solution.py:993
  60.9 29.2 %collective-permute-start.14 = (bf16[4,384,384]{2,1,0:T(8,128)(2,1)}, bf16[4,384,384]{2,1,0:T(8,128)(2,1)}, u32[]{:S(2)}, u32[]{:S(2)}) collective-permute-start(bf16[4,384,384]{2,1,0:T(8,128)(2,1)} %bitcast.30.refs_0_), channel_id=1, source_target_pairs={{0,4},{1,5},{2,6},{3,7},{4,0},{5,1},{6,2},{7,3},{8,12},{9,13},{10,... | collective-permute-start | bytes 3538952 | tf_op jit(solution)/shard_map/ppermute | solution.py:949
  62.4 28.4 %collective-permute-start.13 = (bf16[4,384,384]{2,1,0:T(8,128)(2,1)}, bf16[4,384,384]{2,1,0:T(8,128)(2,1)}, u32[]{:S(2)}, u32[]{:S(2)}) collective-permute-start(bf16[4,384,384]{2,1,0:T(8,128)(2,1)} %bitcast.30.refs_0_), channel_id=1, source_target_pairs={{0,2},{1,3},{2,0},{3,1},{4,6},{5,7},{6,4},{7,5},{8,10},{9,11},{10,... | collective-permute-start | bytes 3538952 | tf_op jit(solution)/shard_map/ppermute | solution.py:946
  111.9 24.1 %collective-permute-start.23 = (bf16[4,192,384]{2,1,0:T(8,128)(2,1)S(1)}, bf16[4,192,384]{2,1,0:T(8,128)(2,1)S(1)}, u32[]{:S(2)}, u32[]{:S(2)}) collective-permute-start(bf16[4,192,384]{2,1,0:T(8,128)(2,1)S(1)} %slice.530.refs_0_), channel_id=1, source_target_pairs={{0,4},{1,5},{2,6},{3,7},{4,0},{5,1},{6,2},{7,3},{8,12},{9,13},{10,... | collective-permute-start | bytes 1769480 | tf_op jit(solution)/shard_map/ppermute | solution.py:949
  112.4 23.6 %collective-permute-start.22 = (bf16[4,192,384]{2,1,0:T(8,128)(2,1)S(1)}, bf16[4,192,384]{2,1,0:T(8,128)(2,1)S(1)}, u32[]{:S(2)}, u32[]{:S(2)}) collective-permute-start(bf16[4,192,384]{2,1,0:T(8,128)(2,1)S(1)} %slice.530.refs_0_), channel_id=1, source_target_pairs={{0,2},{1,3},{2,0},{3,1},{4,6},{5,7},{6,4},{7,5},{8,10},{9,11},{10,... | collective-permute-start | bytes 1769480 | tf_op jit(solution)/shard_map/ppermute | solution.py:946
  145.4 26.6 %collective-permute-start.31 = (bf16[4,384,384]{2,1,0:T(8,128)(2,1)S(1)}, bf16[4,384,384]{2,1,0:T(8,128)(2,1)S(1)}, u32[]{:S(2)}, u32[]{:S(2)}) collective-permute-start(bf16[4,384,384]{2,1,0:T(8,128)(2,1)S(1)} %slice.531.refs_0_), channel_id=1, source_target_pairs={{0,2},{1,3},{2,0},{3,1},{4,6},{5,7},{6,4},{7,5},{8,10},{9,11},{10,... | collective-permute-start | bytes 3538952 | tf_op jit(solution)/shard_map/ppermute | solution.py:946
  146.8 26.4 %collective-permute-start.32 = (bf16[4,384,384]{2,1,0:T(8,128)(2,1)S(1)}, bf16[4,384,384]{2,1,0:T(8,128)(2,1)S(1)}, u32[]{:S(2)}, u32[]{:S(2)}) collective-permute-start(bf16[4,384,384]{2,1,0:T(8,128)(2,1)S(1)} %slice.531.refs_0_), channel_id=1, source_target_pairs={{0,4},{1,5},{2,6},{3,7},{4,0},{5,1},{6,2},{7,3},{8,12},{9,13},{10,... | collective-permute-start | bytes 3538952 | tf_op jit(solution)/shard_map/ppermute | solution.py:949
  149.6 40.5 %collective-permute-start.35 = (bf16[4,384,384]{2,1,0:T(8,128)(2,1)S(1)}, bf16[4,384,384]{2,1,0:T(8,128)(2,1)S(1)}, u32[]{:S(2)}, u32[]{:S(2)}) collective-permute-start(bf16[4,384,384]{2,1,0:T(8,128)(2,1)S(1)} %slice.531.refs_0_), channel_id=1, source_target_pairs={{0,1},{1,0},{2,3},{3,2},{4,5},{5,4},{6,7},{7,6},{8,9},{9,8},{10,11... | collective-permute-start | bytes 3538952 | tf_op jit(solution)/shard_map/ppermute | solution.py:943
  261.4 22.4 %collective-permute-start.41 = (bf16[4,192,384]{2,1,0:T(8,128)(2,1)}, bf16[4,192,384]{2,1,0:T(8,128)(2,1)S(1)}, u32[]{:S(2)}, u32[]{:S(2)}) collective-permute-start(bf16[4,192,384]{2,1,0:T(8,128)(2,1)} %get-tuple-element.243), channel_id=1, source_target_pairs={{0,4},{1,5},{2,6},{3,7},{4,0},{5,1},{6,2},{7,3},{8,12},{9,13},{10,... | collective-permute-start | bytes 1769480 | tf_op jit(solution)/shard_map/ppermute | solution.py:949
  287.1 22.3 %collective-permute-start.44 = (bf16[2,384,384]{2,1,0:T(8,128)(2,1)S(1)}, bf16[2,384,384]{2,1,0:T(8,128)(2,1)S(1)}, u32[]{:S(2)}, u32[]{:S(2)}) collective-permute-start(bf16[2,384,384]{2,1,0:T(8,128)(2,1)S(1)} %get-tuple-element.262), channel_id=1, source_target_pairs={{0,4},{1,5},{2,6},{3,7},{4,0},{5,1},{6,2},{7,3},{8,12},{9,13},{10,... | collective-permute-start | bytes 1769480 | tf_op jit(solution)/shard_map/ppermute | solution.py:949
  326.9 35.6 %collective-permute-start.50 = (bf16[4,4,192,384]{3,2,1,0:T(8,128)(2,1)}, bf16[4,4,192,384]{3,2,1,0:T(8,128)(2,1)}, u32[]{:S(2)}, u32[]{:S(2)}) collective-permute-start(bf16[4,4,192,384]{3,2,1,0:T(8,128)(2,1)} %get-tuple-element.197), channel_id=1, source_target_pairs={{0,1},{1,0},{2,3},{3,2},{4,5},{5,4},{6,7},{7,6},{8,9},{9,8},{10,11... | collective-permute-start | bytes 7077896 | tf_op jit(solution)/shard_map/ppermute | solution.py:943
  327.4 27.6 %collective-permute-start.48 = (bf16[4,216,384]{2,1,0:T(8,128)(2,1)S(1)}, bf16[4,216,384]{2,1,0:T(8,128)(2,1)}, u32[]{:S(2)}, u32[]{:S(2)}) collective-permute-start(bf16[4,216,384]{2,1,0:T(8,128)(2,1)S(1)} %get-tuple-element.239), channel_id=1, source_target_pairs={{0,4},{1,5},{2,6},{3,7},{4,0},{5,1},{6,2},{7,3},{8,12},{9,13},{10,... | collective-permute-start | bytes 1990664 | tf_op jit(solution)/shard_map/ppermute | solution.py:949
  328.6 26.3 %collective-permute-start.49 = (bf16[4,216,384]{2,1,0:T(8,128)(2,1)}, bf16[4,216,384]{2,1,0:T(8,128)(2,1)}, u32[]{:S(2)}, u32[]{:S(2)}) collective-permute-start(bf16[4,216,384]{2,1,0:T(8,128)(2,1)} %get-tuple-element.240), channel_id=1, source_target_pairs={{0,2},{1,3},{2,0},{3,1},{4,6},{5,7},{6,4},{7,5},{8,10},{9,11},{10,... | collective-permute-start | bytes 1990664 | tf_op jit(solution)/shard_map/ppermute | solution.py:946
  332.8 114.2 %reduce-scatter.3.cloned.1.call-start = ((), (), s32[]{:S(2)}) async-start(), calls=%async_computation.2 | async-start | bytes 1658880 | tf_op jit(solution)/shard_map/reduce_scatter | solution.py:993
  359.1 28.2 %collective-permute-start.54 = (bf16[2,432,384]{2,1,0:T(8,128)(2,1)}, bf16[2,432,384]{2,1,0:T(8,128)(2,1)S(1)}, u32[]{:S(2)}, u32[]{:S(2)}) collective-permute-start(bf16[2,432,384]{2,1,0:T(8,128)(2,1)} %get-tuple-element.258), channel_id=1, source_target_pairs={{0,4},{1,5},{2,6},{3,7},{4,0},{5,1},{6,2},{7,3},{8,12},{9,13},{10,... | collective-permute-start | bytes 1990664 | tf_op jit(solution)/shard_map/ppermute | solution.py:949
  361.5 25.9 %collective-permute-start.53 = (bf16[2,432,384]{2,1,0:T(8,128)(2,1)}, bf16[2,432,384]{2,1,0:T(8,128)(2,1)}, u32[]{:S(2)}, u32[]{:S(2)}) collective-permute-start(bf16[2,432,384]{2,1,0:T(8,128)(2,1)} %get-tuple-element.260), channel_id=1, source_target_pairs={{0,2},{1,3},{2,0},{3,1},{4,6},{5,7},{6,4},{7,5},{8,10},{9,11},{10,... | collective-permute-start | bytes 1990664 | tf_op jit(solution)/shard_map/ppermute | solution.py:946
  364.7 24.9 %collective-permute-start.51 = (bf16[4,96,384]{2,1,0:T(8,128)(2,1)}, bf16[4,96,384]{2,1,0:T(8,128)(2,1)}, u32[]{:S(2)}, u32[]{:S(2)}) collective-permute-start(bf16[4,96,384]{2,1,0:T(8,128)(2,1)} %get-tuple-element.247), channel_id=1, source_target_pairs={{0,4},{1,5},{2,6},{3,7},{4,0},{5,1},{6,2},{7,3},{8,12},{9,13},{10,... | collective-permute-start | bytes 884744 | tf_op jit(solution)/shard_map/ppermute | solution.py:949
  365.9 23.7 %collective-permute-start.52 = (bf16[4,96,384]{2,1,0:T(8,128)(2,1)}, bf16[4,96,384]{2,1,0:T(8,128)(2,1)}, u32[]{:S(2)}, u32[]{:S(2)}) collective-permute-start(bf16[4,96,384]{2,1,0:T(8,128)(2,1)} %get-tuple-element.248), channel_id=1, source_target_pairs={{0,2},{1,3},{2,0},{3,1},{4,6},{5,7},{6,4},{7,5},{8,10},{9,11},{10,... | collective-permute-start | bytes 884744 | tf_op jit(solution)/shard_map/ppermute | solution.py:946
  410.4 26.3 %collective-permute-start.67 = (bf16[4,192,384]{2,1,0:T(8,128)(2,1)}, bf16[4,192,384]{2,1,0:T(8,128)(2,1)S(1)}, u32[]{:S(2)}, u32[]{:S(2)}) collective-permute-start(bf16[4,192,384]{2,1,0:T(8,128)(2,1)} %get-tuple-element.245), channel_id=1, source_target_pairs={{0,4},{1,5},{2,6},{3,7},{4,0},{5,1},{6,2},{7,3},{8,12},{9,13},{10,... | collective-permute-start | bytes 1769480 | tf_op jit(solution)/shard_map/ppermute | solution.py:949
  411.7 25.0 %collective-permute-start.66 = (bf16[4,192,384]{2,1,0:T(8,128)(2,1)S(1)}, bf16[4,192,384]{2,1,0:T(8,128)(2,1)S(1)}, u32[]{:S(2)}, u32[]{:S(2)}) collective-permute-start(bf16[4,192,384]{2,1,0:T(8,128)(2,1)S(1)} %copy-done.14), channel_id=1, source_target_pairs={{0,2},{1,3},{2,0},{3,1},{4,6},{5,7},{6,4},{7,5},{8,10},{9,11},{10,... | collective-permute-start | bytes 1769480 | tf_op jit(solution)/shard_map/ppermute | solution.py:946
  415.8 24.1 %collective-permute-start.71 = (f32[192,384]{1,0:T(8,128)S(1)}, f32[192,384]{1,0:T(8,128)S(1)}, u32[]{:S(2)}, u32[]{:S(2)}) collective-permute-start(f32[192,384]{1,0:T(8,128)S(1)} %fusion.13), channel_id=1, source_target_pairs={{0,1},{1,0},{2,3},{3,2},{4,5},{5,4},{6,7},{7,6},{8,9},{9,8},{10,11... | collective-permute-start | bytes 884744 | tf_op jit(solution)/shard_map/ppermute | solution.py:943
  (99 other events, 1025.5 us)
Sparse Core Ops, SparseCore 0:
  26.3 31.4 all-gather.4
  59.9 39.4 all-gather.6
  332.9 30.3 reduce-scatter.4
  409.3 32.7 reduce-scatter.2

commit v6 on v5

--- a/solution.py
+++ b/solution.py
@@ -74,12 +74,14 @@
             half = core if side == 0 else 1 - core
             column = pl.multiple_of(base + half * HALF, 128)
             for relative in range(4):
-                if relative < 3:
+                later = start >= split
+                begin = start - split if later else start
+                if len(pieces) == 16:
+                    source = pieces[8 * side + 2 * relative + later].at[z, pl.ds(begin, rows)]
+                elif relative < 3:
                     source = pieces[5 * side + relative].at[z, pl.ds(start, rows)]
-                elif start < split:
-                    source = pieces[5 * side + 3].at[z, pl.ds(start, rows)]
                 else:
-                    source = pieces[5 * side + 4].at[z, pl.ds(start - split, rows)]
+                    source = pieces[5 * side + 3 + later].at[z, pl.ds(begin, rows)]
                 target = ref.at[z, place ^ relative, :, pl.ds(column, HALF)]
                 group.append(pltpu.make_async_copy(source, target, sems.at[number]))
                 number += 1
@@ -552,7 +554,7 @@
 
 
 def self_mlp_kernel(steps, info, res, cot, vec, *refs):
-    pieces, (out, total, da, d_vec, keep, send), scratch = (refs[:10], refs[10:16], refs[16:])
+    pieces, (out, total, da, d_vec, keep, send), scratch = (refs[:16], refs[16:22], refs[22:])
     w_up, w_down, sems, h_all, du_all, e_all, stage, grad_sems = scratch
     step = pl.program_id(0)
     first = step == 0
@@ -612,7 +614,7 @@
         functools.partial(self_mlp_kernel, steps),
         "self_mlp",
         steps + 8,
-        [SMALL, spec(D), whole_spec(m, D), whole_spec(16, D)] + [ANY] * 10,
+        [SMALL, spec(D), whole_spec(m, D), whole_spec(16, D)] + [ANY] * 16,
         [spec(D), spec(D), spec(D), whole_spec(8, D), ANY, ANY],
         [
             shaped((m, D), BF16),
@@ -1009,9 +1011,12 @@
         keep, send = (jnp.where(high, total[i], total[1 - i]) for i in (1, 0))
         return keep.astype(F32) + lax.ppermute(send, AX, self.to_far_z).astype(F32)
 
-    def gather_z_by_hops(self, unit):
+
+    def gather_far_z(self, unit):
+        return lax.ppermute(unit, AX, self.to_far_z)
+
+    def gather_near_z(self, unit, arrived):
         odd, high = self.z_bits()
-        arrived = lax.ppermute(unit, AX, self.to_far_z)
         pair = jnp.stack([jnp.where(high, arrived, unit), jnp.where(high, unit, arrived)])
         arrived = lax.ppermute(pair, AX, self.to_z)
         both = [jnp.where(odd, arrived, pair), jnp.where(odd, pair, arrived)]
@@ -1074,11 +1079,12 @@
     vectors = jnp.pad(vectors, ((0, 0), (0, HALF - 48)))
     cross_attn = jnp.concatenate([cross_attn, vectors], axis=0)
     own = grid.gather_z(jnp.concatenate([self_attn, self_mlp], axis=0))
+    arrived = grid.gather_far_z(cross_attn)
     return (
-        grid.gather_z_by_hops(cross_attn),
-        grid.gather_z(cross_mlp),
+        grid.gather_near_z(cross_attn, arrived),
+        grid.gather_z(after(cross_mlp, arrived)),
         own[:, :192],
-        own[:, 192:],
+        (own[:, 192:384], own[:, 384:]),
     )
 
 
@@ -1114,6 +1120,15 @@
         pieces += tuple((unit[:, i, :, half] for i in range(3)))
         pieces += (unit[:, 3, :split, half], unit[:, 3, split:, half])
     return pieces
+
+
+def all_parted(pieces, split):
+    parted = ()
+    for side in (pieces[:5], pieces[5:]):
+        for piece in side[:3]:
+            parted += (piece[:, :split], piece[:, split:])
+        parted += side[3:]
+    return parted
 
 
 def gather_plain(cross, own_block):
@@ -1180,14 +1195,20 @@
     cm = grid.both_cores(cm_own, cm_near, cm_far)
     sa_own = after(sa_own, cm_far)
     sa_near = grid.near(sa_own)
+    up, down = after(sm_own, cm)
+    sm_first = (grid.swap_y(up), grid.swap_x(down))
     mid, e, slope = cross_mlp_forward(info, res, lat_rows, keeping, vec, cm)
-    sa_near = after(sa_near, mid)
-    sa_far = grid.far(sa_near, ATTN_SPLIT)
-    sm_near = grid.near(after(sm_own, sa_far))
+    sa_near, sm_first = after((sa_near, sm_first), mid)
+    sa_far = grid.far(after(sa_near, sm_first), ATTN_SPLIT)
     sa = grid.both_cores(sa_own, sa_near, sa_far)
+    up, down = after((up, down), sa_far)
+    up_y, down_x = after(sm_first, sa_far)
+    sm_second = (grid.swap_x(up), grid.swap_y(down), grid.swap_x(up_y), grid.swap_y(down_x))
     own_res, sq, sk, sv, so, sp = self_attn_forward(info, mid, vec, sa)
-    sm_far = grid.far(after(sm_near, own_res), MLP_SPLIT)
-    sm = grid.both_cores(sm_own, sm_near, sm_far)
+    up_x, down_y, up_far, down_far = after(sm_second, own_res)
+    up, down, up_y, down_x = after((up, down, up_y, down_x), own_res)
+    sm = (up, down, up_x, down_x, up_y, down_y, up_far, down_far)
+    sm += tuple((grid.swap_core(piece) for piece in sm))
     result, total, da, own_vec, a_keep, a_send = self_mlp(info, own_res, cot_rows, vec, sm)
 
     total, da = after((total, da), a_send)
@@ -1271,6 +1292,7 @@
     lat_rows, cot_rows, latents, inputs, bias, keeping = args
     info = jnp.zeros((2,), jnp.int32)
     vec, ca, cm, sa, sm = gather_plain(cross, own_block)
+    sm = all_parted(sm, MLP_SPLIT)
     res, q, k, v, o, p = cross_attn_forward(info, latents, inputs, bias, vec, ca)
     mid, e, slope = cross_mlp_forward(info, res, lat_rows, keeping, vec, cm)
     own_res, sq, sk, sv, so, sp = self_attn_forward(info, mid, vec, sa)

time: 486 us -> 479 us (0.986)
  waiting for transfers between devices: 111 us -> 101 us
  starting transfers between devices: 55.3 us -> 60.3 us
    ppermute x18 -> x19, waiting for transfers between devices: 32.2 us -> 23.1 us  [swap_x(): return lax.ppermute(value, AX, self.to_x)]
    ppermute x18 -> x19, starting transfers between devices: 17.8 us -> 21.9 us  [swap_x(): return lax.ppermute(value, AX, self.to_x)]
    ppermute x18 -> x19, waiting for transfers between devices: 44.4 us -> 41.1 us  [swap_y(): return lax.ppermute(value, AX, self.to_y)]
    ppermute x18 -> x19, starting transfers between devices: 20.3 us -> 18.2 us  [swap_y(): return lax.ppermute(value, AX, self.to_y)]
  transfers between devices with their start and end apart: 76 -> 81, of which waited for: 26 -> 24; matrix products, arithmetic and copies ran while one was open for 10% -> 10% of each run, Pallas kernels for 39% -> 40%
where the time goes in v6:
time: 479 us; the launch traced here: 475 us
  Pallas kernels  233 us (49%)
  waiting for transfers between devices  101 us (21%)
  starting transfers between devices  60.3 us (13%)
  other arithmetic  38.2 us (8%)
  local copies, waits for them, and re-layouts  27 us (6%)
  between operations  15.2 us (3%)
    pallas_call x11, Pallas kernels, call(): pl.pallas_call(kernel, grid=(grid,), in_specs=in_specs, out_specs=out_spe...  233 us
    ppermute x19, waiting for transfers between devices, swap_y(): return lax.ppermute(value, AX, self.to_y)  41.1 us
    ppermute x19, waiting for transfers between devices, swap_x(): return lax.ppermute(value, AX, self.to_x)  23.1 us
    ppermute x19, starting transfers between devices, swap_x(): return lax.ppermute(value, AX, self.to_x)  21.9 us
    ppermute x19, starting transfers between devices, swap_y(): return lax.ppermute(value, AX, self.to_y)  18.2 us
    add x4, other arithmetic, sides(): sums = (keep[1] + arrived[1] + for_x, keep[2] + arrived[2] + for_y)  11 us
  transfers between devices with their start and end apart: 81, of which 24 were waited for; matrix products, arithmetic and copies ran while one was open for 10% of the time, Pallas kernels for 40%

profile of v6, /device:TPU:0, one launch (start us, length us, event | category | flops | bytes accessed | tf_op | source)
XLA Modules:
  0.0 475.1 jit_solution(7070340030151132452)
XLA Ops:
  12.0 4.1 collective-permute-start.1
  17.0 6.9 %collective-permute-done.1 = bf16[208,384]{1,0:T(8,128)(2,1)S(1)} collective-permute-done((bf16[208,384]{1,0:T(8,128)(2,1)S(1)}, bf16[208,384]{1,0:T(8,128)(2,1)S(1)}, u32[]{:S(2)}, u32[]{:S(2)}) %collective-permute-start.1) | collective-permute-done | bytes 159776 | tf_op jit(solution)/shard_map/ppermute | solution.py:1016
  24.9 8.2 %collective-permute-done.2 = bf16[2,208,384]{2,1,0:T(8,128)(2,1)S(1)} collective-permute-done((bf16[2,208,384]{2,1,0:T(8,128)(2,1)S(1)}, bf16[2,208,384]{2,1,0:T(8,128)(2,1)S(1)}, u32[]{:S(2)}, u32[]{:S(2)}) %collective-permute-start.2) | collective-permute-done | bytes 319520 | tf_op jit(solution)/shard_map/ppermute | solution.py:1021
  36.3 11.9 %collective-permute-done.5.refs_2_ = bf16[4,208,384]{2,1,0:T(8,128)(2,1)S(1)} collective-permute-done((bf16[4,208,384]{2,1,0:T(8,128)(2,1)S(1)}, bf16[4,208,384]{2,1,0:T(8,128)(2,1)S(1)}, u32[]{:S(2)}, u32[]{:S(2)}) %collective-permute-start.5) | collective-permute-done | bytes 639008 | tf_op jit(solution)/shard_map/ppermute | solution.py:951
  64.1 25.4 %cross_attn_forward.1 = (f32[1024,768]{1,0:T(8,128)}, bf16[8,128,768]{2,1,0:T(8,128)(2,1)}, bf16[8,304,768]{2,1,0:T(8,128)(2,1)}, bf16[8,304,768]{2,1,0:T(8,128)...) custom-call(s32[2]{0:T(128)} %pad_add_fusion.1.info, bf16[8,128,768]{2,1,0:T(8,128)(2,1)} %lat.1, ...), custom_call_target="tpu_custom_call" | custom-call | flops 10066329600 | bytes 31260672 | tf_op jit(solution)/shard_map/cross_attn_forward/pallas_call | solution.py:207
  94.8 11.7 %collective-permute-done.15.refs_3_ = bf16[4,192,384]{2,1,0:T(8,128)(2,1)S(1)} collective-permute-done((bf16[4,192,384]{2,1,0:T(8,128)(2,1)S(1)}, bf16[4,192,384]{2,1,0:T(8,128)(2,1)S(1)}, u32[]{:S(2)}, u32[]{:S(2)}) %collective-permute-start.15) | collective-permute-done | bytes 589856 | tf_op jit(solution)/shard_map/ppermute | solution.py:948
  116.4 22.2 %cross_mlp_forward.1 = (f32[1024,768]{1,0:T(8,128)}, bf16[1024,3072]{1,0:T(8,128)(2,1)}, bf16[1024,3072]{1,0:T(8,128)(2,1)}) custom-call(s32[2]{0:T(128)} %pad_add_fusion.1.info, f32[1024,768]{1,0:T(8,128)} %get-tuple-element.142.res, bf16[1024,768]{1,0:T(8,128)(2,1)} %bitcast.171, f32[1024,1]{1,0:T(8,128)} %copy.51.keep.keep_rows, f32[16,768]{1,0:T(8,128)} %reshape.292.vec, ...), custom_call_target="tpu_custom_call" | custom-call | flops 9663676416 | bytes 29884416 | tf_op jit(solution)/shard_map/cross_mlp_forward/pallas_call | solution.py:207
  143.7 5.8 %collective-permute-done.26.refs_3_ = bf16[4,96,384]{2,1,0:T(8,128)(2,1)S(1)} collective-permute-done((bf16[4,96,384]{2,1,0:T(8,128)(2,1)S(1)}, bf16[4,96,384]{2,1,0:T(8,128)(2,1)S(1)}, u32[]{:S(2)}, u32[]{:S(2)}) %collective-permute-start.26) | collective-permute-done | bytes 294944 | tf_op jit(solution)/shard_map/ppermute | solution.py:948
  155.4 15.4 %self_attn_forward.1 = (f32[1024,768]{1,0:T(8,128)}, bf16[8,128,768]{2,1,0:T(8,128)(2,1)}, bf16[8,128,768]{2,1,0:T(8,128)(2,1)}, bf16[8,128,768]{2,1,0:T(8,128)(...) custom-call(s32[2]{0:T(128)} %pad_add_fusion.1.info, f32[1024,768]{1,0:T(8,128)} %get-tuple-element.148.mid, ...), custom_call_target="tpu_custom_call" | custom-call | flops 5637144576 | bytes 20447232 | tf_op jit(solution)/shard_map/self_attn_forward/pallas_call | solution.py:207
  171.5 7.7 %collective-permute-done.34.refs_5_ = bf16[4,192,384]{2,1,0:T(8,128)(2,1)} collective-permute-done((bf16[4,192,384]{2,1,0:T(8,128)(2,1)S(1)}, bf16[4,192,384]{2,1,0:T(8,128)(2,1)}, u32[]{:S(2)}, u32[]{:S(2)}) %collective-permute-start.34) | collective-permute-done | bytes 589856 | tf_op jit(solution)/shard_map/ppermute | solution.py:951
  186.0 45.3 %self_mlp.1 = (bf16[1024,768]{1,0:T(8,128)(2,1)}, f32[1024,768]{1,0:T(8,128)}, bf16[1024,768]{1,0:T(8,128)(2,1)}, f32[8,768]{1,0:T(8,128)}, bf16[4,4,384,384]{3,...) custom-call(s32[2]{0:T(128)} %pad_add_fusion.1.info, f32[1024,768]{1,0:T(8,128)} %get-tuple-element.158.res, ...), custom_call_target="tpu_custom_call" | custom-call | flops 28991029248 | bytes 29884416 | tf_op jit(solution)/shard_map/self_mlp/pallas_call | solution.py:207
  231.5 19.3 %self_attn_back.1 = (f32[1024,768]{1,0:T(8,128)}, f32[8,768]{1,0:T(8,128)}, bf16[8,128,768]{2,1,0:T(8,128)(2,1)}, bf16[8,128,768]{2,1,0:T(8,128)(2,1)}, bf16[8,1...) custom-call(s32[2]{0:T(128)} %pad_add_fusion.1.info, f32[1024,768]{1,0:T(8,128)} %get-tuple-element.174.total, ...), custom_call_target="tpu_custom_call" | custom-call | flops 6442450944 | bytes 29884416 | tf_op jit(solution)/shard_map/self_attn_back/pallas_call | solution.py:207
  255.4 20.6 %cross_mlp_back.1 = (f32[1024,768]{1,0:T(8,128)}, bf16[1024,768]{1,0:T(8,128)(2,1)}, f32[8,768]{1,0:T(8,128)}, bf16[1024,768]{1,0:T(8,128)(2,1)}, bf16[1024,3072]{1,0:T(8,128)(2,1)}, /*index=5*/bf16[1024,768]{1,0:T(8,128)(2,1)}) custom-call(s32[2]{0:T(128)} %pad_add_fusion.1.info, f32[1024,768]{1,0:T(8,128)} %get-tuple-element.184.up_grad, ...), custom_call_target="tpu_custom_call" | custom-call | flops 9663676416 | bytes 36175872 | tf_op jit(solution)/shard_map/cross_mlp_back/pallas_call | solution.py:207
  282.1 19.1 %cross_mlp_grads.1 = (bf16[4,4,432,384]{3,2,1,0:T(8,128)(2,1)}, bf16[4,4,432,384]{3,2,1,0:T(8,128)(2,1)}) custom-call(s32[2]{0:T(128)} %pad_add_fusion.1.info, bf16[1024,768]{1,0:T(8,128)(2,1)} %get-tuple-element.190.h, bf16[1024,3072]{1,0:T(8,128)(2,1)} %get-tuple-element.191.du, bf16[1024,3072]{1,0:T(8,128)(2,1)} %get-tuple-element.192.e, ...), custom_call_target="tpu_custom_call" | custom-call | flops 10871635968 | bytes 28311552 | tf_op jit(solution)/shard_map/cross_mlp_grads/pallas_call | solution.py:207
  304.2 10.2 %self_attn_grads.1 = (bf16[4,4,192,384]{3,2,1,0:T(8,128)(2,1)}, bf16[4,4,192,384]{3,2,1,0:T(8,128)(2,1)}) custom-call(s32[2]{0:T(128)} %pad_add_fusion.1.info, bf16[8,128,768]{2,1,0:T(8,128)(2,1)} %get-tuple-element.202.refs_0_, bf16[8,128,768]{2,1,0:T(8,128)(2,1)} %get-tuple-element.204.refs_1_, bf16[8,128,768]{2,1,0:T(8,128)(2,1)} %get-tuple-element.206.refs_2_, ...), custom_call_target="tpu_custom_call" | custom-call | flops 4831838208 | bytes 14155776 | tf_op jit(solution)/shard_map/self_attn_grads/pallas_call | solution.py:207
  321.1 3.5 fusion.1
  324.7 22.1 %cross_attn_back_0.1 = (f32[8,768]{1,0:T(8,128)}, f32[1024,768]{1,0:T(8,128)}, f32[8,296,768]{2,1,0:T(8,128)}, bf16[8,128,768]{2,1,0:T(8,128)(2,1)}, bf16[8,128,...) custom-call(s32[2]{0:T(128)} %pad_add_fusion.1.info, ...), custom_call_target="tpu_custom_call" | custom-call | flops 5989466112 | bytes 31260672 | tf_op jit(solution)/shard_map/cross_attn_back_0/pallas_call | solution.py:207
  358.4 20.8 %cross_attn_back_1.1 = (f32[8,768]{1,0:T(8,128)}, f32[1024,768]{1,0:T(8,128)}, f32[8,296,768]{2,1,0:T(8,128)}, bf16[8,128,768]{2,1,0:T(8,128)(2,1)}, bf16[8,128,...) custom-call(s32[2]{0:T(128)} %pad_add_fusion.1.info, ...), custom_call_target="tpu_custom_call", output_to_operand_aliasing={{1}: (21, {}), {2}: (22, {}), {3}: (23, {}), {4}: (24, {}),... | custom-call | flops 5989466112 | bytes 31260672 | tf_op jit(solution)/shard_map/cross_attn_back_1/pallas_call | solution.py:207
  384.7 12.8 %cross_attn_grads.1 = (bf16[4,4,160,384]{3,2,1,0:T(8,128)(2,1)}, bf16[4,4,160,384]{3,2,1,0:T(8,128)(2,1)}) custom-call(s32[2]{0:T(128)} %pad_add_fusion.1.info, bf16[8,128,768]{2,1,0:T(8,128)(2,1)} %get-tuple-element.247.refs_0_, bf16[8,128,768]{2,1,0:T(8,128)(2,1)} %get-tuple-element.248.refs_1_, bf16[8,304,768]{2,1,0:T(8,128)(2,1)} %get-tuple-element.249.refs_2_, ...), custom_call_target="tpu_custom_call" | custom-call | flops 6945767424 | bytes 19070976 | tf_op jit(solution)/shard_map/cross_attn_grads/pallas_call | solution.py:207
  407.7 15.8 %collective-permute-done.63 = bf16[4,80,384]{2,1,0:T(8,128)(2,1)S(1)} collective-permute-done((bf16[4,80,384]{2,1,0:T(8,128)(2,1)S(1)}, bf16[4,80,384]{2,1,0:T(8,128)(2,1)S(1)}, u32[]{:S(2)}, u32[]{:S(2)}) %collective-permute-start.63) | collective-permute-done | bytes 245792 | tf_op jit(solution)/shard_map/ppermute | solution.py:951
  434.2 5.4 %collective-permute-done.73 = bf16[2,192,384]{2,1,0:T(8,128)(2,1)S(1)} collective-permute-done((bf16[2,192,384]{2,1,0:T(8,128)(2,1)S(1)}, bf16[2,192,384]{2,1,0:T(8,128)(2,1)S(1)}, u32[]{:S(2)}, u32[]{:S(2)}) %collective-permute-start.73) | collective-permute-done | bytes 294944 | tf_op jit(solution)/shard_map/ppermute | solution.py:1007
  441.9 4.9 %collective-permute-start.74 = (bf16[192,384]{1,0:T(8,128)(2,1)S(1)}, bf16[192,384]{1,0:T(8,128)(2,1)S(1)}, u32[]{:S(2)}, u32[]{:S(2)}) collective-permute-start(bf16[192,384]{1,0:T(8,128)(2,1)S(1)} %select_bitcast_fusion.4), channel_id=1, source_target_pairs={{0,16},{1,17},{2,18},{3,19},{4,20},{5,21},{6,22},{7,23},{8,24},{9,... | collective-permute-start | bytes 442376 | tf_op jit(solution)/shard_map/ppermute | solution.py:1012
  452.4 3.6 collective-permute-done.67
  458.4 5.1 %collective-permute-done.68 = bf16[160,384]{1,0:T(8,128)(2,1)S(1)} collective-permute-done((bf16[160,384]{1,0:T(8,128)(2,1)S(1)}, bf16[160,384]{1,0:T(8,128)(2,1)S(1)}, u32[]{:S(2)}, u32[]{:S(2)}) %collective-permute-start.68) | collective-permute-done | bytes 122912 | tf_op jit(solution)/shard_map/ppermute | solution.py:1012
  (355 shorter events, 132.3 us)
Async XLA Ops:
  7.2 53.0 %all-gather.5.cloned.1.call-start = ((), (), s32[]{:S(2)}) async-start(), calls=%async_computation.4 | async-start | bytes 1474560 | tf_op jit(solution)/shard_map/all_gather | solution.py:960
  23.9 86.3 %all-gather.7.cloned.1.call-start = ((), (), s32[]{:S(2)}) async-start(), calls=%async_computation.5 | async-start | bytes 2211840 | tf_op jit(solution)/shard_map/all_gather | solution.py:960
  36.2 24.0 %collective-permute-start.7 = (bf16[4,208,384]{2,1,0:T(8,128)(2,1)S(1)}, bf16[4,208,384]{2,1,0:T(8,128)(2,1)S(1)}, u32[]{:S(2)}, u32[]{:S(2)}) collective-permute-start(bf16[4,208,384]{2,1,0:T(8,128)(2,1)S(1)} %bitcast.176), channel_id=1, source_target_pairs={{0,1},{1,0},{2,3},{3,2},{4,5},{5,4},{6,7},{7,6},{8,9},{9,8},{10,11... | collective-permute-start | bytes 1916936 | tf_op jit(solution)/shard_map/ppermute | solution.py:945
  50.7 350.3 %reduce-scatter.5.cloned.1.call-start = ((), (), s32[]{:S(2)}) async-start(), calls=%async_computation.3 | async-start | bytes 1474560 | tf_op jit(solution)/shard_map/reduce_scatter | solution.py:995
  60.2 29.4 %collective-permute-start.14 = (bf16[4,384,384]{2,1,0:T(8,128)(2,1)}, bf16[4,384,384]{2,1,0:T(8,128)(2,1)}, u32[]{:S(2)}, u32[]{:S(2)}) collective-permute-start(bf16[4,384,384]{2,1,0:T(8,128)(2,1)} %bitcast.30.refs_0_), channel_id=1, source_target_pairs={{0,4},{1,5},{2,6},{3,7},{4,0},{5,1},{6,2},{7,3},{8,12},{9,13},{10,... | collective-permute-start | bytes 3538952 | tf_op jit(solution)/shard_map/ppermute | solution.py:951
  61.7 28.4 %collective-permute-start.13 = (bf16[4,384,384]{2,1,0:T(8,128)(2,1)}, bf16[4,384,384]{2,1,0:T(8,128)(2,1)}, u32[]{:S(2)}, u32[]{:S(2)}) collective-permute-start(bf16[4,384,384]{2,1,0:T(8,128)(2,1)} %bitcast.30.refs_0_), channel_id=1, source_target_pairs={{0,2},{1,3},{2,0},{3,1},{4,6},{5,7},{6,4},{7,5},{8,10},{9,11},{10,... | collective-permute-start | bytes 3538952 | tf_op jit(solution)/shard_map/ppermute | solution.py:948
  111.8 38.7 %collective-permute-start.28 = (bf16[4,192,384]{2,1,0:T(8,128)(2,1)S(1)}, bf16[4,192,384]{2,1,0:T(8,128)(2,1)}, u32[]{:S(2)}, u32[]{:S(2)}) collective-permute-start(bf16[4,192,384]{2,1,0:T(8,128)(2,1)S(1)} %get-tuple-element.149.refs_0_), channel_id=1, source_target_pairs={{0,1},{1,0},{2,3},{3,2},{4,5},{5,4},{6,7},{7,6},{8,9},{9,8},{10,11... | collective-permute-start | bytes 1769480 | tf_op jit(solution)/shard_map/ppermute | solution.py:945
  112.4 26.4 %collective-permute-start.23 = (bf16[4,192,384]{2,1,0:T(8,128)(2,1)S(1)}, bf16[4,192,384]{2,1,0:T(8,128)(2,1)S(1)}, u32[]{:S(2)}, u32[]{:S(2)}) collective-permute-start(bf16[4,192,384]{2,1,0:T(8,128)(2,1)S(1)} %get-tuple-element.149.refs_0_), channel_id=1, source_target_pairs={{0,4},{1,5},{2,6},{3,7},{4,0},{5,1},{6,2},{7,3},{8,12},{9,13},{10,... | collective-permute-start | bytes 1769480 | tf_op jit(solution)/shard_map/ppermute | solution.py:951
  113.1 25.6 %collective-permute-start.22 = (bf16[4,192,384]{2,1,0:T(8,128)(2,1)S(1)}, bf16[4,192,384]{2,1,0:T(8,128)(2,1)S(1)}, u32[]{:S(2)}, u32[]{:S(2)}) collective-permute-start(bf16[4,192,384]{2,1,0:T(8,128)(2,1)S(1)} %get-tuple-element.149.refs_0_), channel_id=1, source_target_pairs={{0,2},{1,3},{2,0},{3,1},{4,6},{5,7},{6,4},{7,5},{8,10},{9,11},{10,... | collective-permute-start | bytes 1769480 | tf_op jit(solution)/shard_map/ppermute | solution.py:948
  114.2 27.4 %collective-permute-start.24 = (bf16[4,192,384]{2,1,0:T(8,128)(2,1)S(1)}, bf16[4,192,384]{2,1,0:T(8,128)(2,1)S(1)}, u32[]{:S(2)}, u32[]{:S(2)}) collective-permute-start(bf16[4,192,384]{2,1,0:T(8,128)(2,1)S(1)} %get-tuple-element.160.refs_0_), channel_id=1, source_target_pairs={{0,4},{1,5},{2,6},{3,7},{4,0},{5,1},{6,2},{7,3},{8,12},{9,13},{10,... | collective-permute-start | bytes 1769480 | tf_op jit(solution)/shard_map/ppermute | solution.py:951
  115.0 25.7 %collective-permute-start.25 = (bf16[4,192,384]{2,1,0:T(8,128)(2,1)S(1)}, bf16[4,192,384]{2,1,0:T(8,128)(2,1)S(1)}, u32[]{:S(2)}, u32[]{:S(2)}) collective-permute-start(bf16[4,192,384]{2,1,0:T(8,128)(2,1)S(1)} %get-tuple-element.162.refs_1_), channel_id=1, source_target_pairs={{0,2},{1,3},{2,0},{3,1},{4,6},{5,7},{6,4},{7,5},{8,10},{9,11},{10,... | collective-permute-start | bytes 1769480 | tf_op jit(solution)/shard_map/ppermute | solution.py:948
  152.8 26.7 %collective-permute-start.33 = (bf16[4,192,384]{2,1,0:T(8,128)(2,1)S(1)}, bf16[4,192,384]{2,1,0:T(8,128)(2,1)}, u32[]{:S(2)}, u32[]{:S(2)}) collective-permute-start(bf16[4,192,384]{2,1,0:T(8,128)(2,1)S(1)} %get-tuple-element.160.refs_0_), channel_id=1, source_target_pairs={{0,2},{1,3},{2,0},{3,1},{4,6},{5,7},{6,4},{7,5},{8,10},{9,11},{10,... | collective-permute-start | bytes 1769480 | tf_op jit(solution)/shard_map/ppermute | solution.py:948
  154.2 25.0 %collective-permute-start.34 = (bf16[4,192,384]{2,1,0:T(8,128)(2,1)S(1)}, bf16[4,192,384]{2,1,0:T(8,128)(2,1)}, u32[]{:S(2)}, u32[]{:S(2)}) collective-permute-start(bf16[4,192,384]{2,1,0:T(8,128)(2,1)S(1)} %get-tuple-element.162.refs_1_), channel_id=1, source_target_pairs={{0,4},{1,5},{2,6},{3,7},{4,0},{5,1},{6,2},{7,3},{8,12},{9,13},{10,... | collective-permute-start | bytes 1769480 | tf_op jit(solution)/shard_map/ppermute | solution.py:951
  319.2 35.3 %collective-permute-start.55 = (bf16[4,4,192,384]{3,2,1,0:T(8,128)(2,1)}, bf16[4,4,192,384]{3,2,1,0:T(8,128)(2,1)}, u32[]{:S(2)}, u32[]{:S(2)}) collective-permute-start(bf16[4,4,192,384]{3,2,1,0:T(8,128)(2,1)} %get-tuple-element.229), channel_id=1, source_target_pairs={{0,1},{1,0},{2,3},{3,2},{4,5},{5,4},{6,7},{7,6},{8,9},{9,8},{10,11... | collective-permute-start | bytes 7077896 | tf_op jit(solution)/shard_map/ppermute | solution.py:945
  319.2 27.6 %collective-permute-start.53 = (bf16[4,216,384]{2,1,0:T(8,128)(2,1)S(1)}, bf16[4,216,384]{2,1,0:T(8,128)(2,1)}, u32[]{:S(2)}, u32[]{:S(2)}) collective-permute-start(bf16[4,216,384]{2,1,0:T(8,128)(2,1)S(1)} %get-tuple-element.271), channel_id=1, source_target_pairs={{0,4},{1,5},{2,6},{3,7},{4,0},{5,1},{6,2},{7,3},{8,12},{9,13},{10,... | collective-permute-start | bytes 1990664 | tf_op jit(solution)/shard_map/ppermute | solution.py:951
  320.0 26.7 %collective-permute-start.54 = (bf16[4,216,384]{2,1,0:T(8,128)(2,1)}, bf16[4,216,384]{2,1,0:T(8,128)(2,1)}, u32[]{:S(2)}, u32[]{:S(2)}) collective-permute-start(bf16[4,216,384]{2,1,0:T(8,128)(2,1)} %get-tuple-element.272), channel_id=1, source_target_pairs={{0,2},{1,3},{2,0},{3,1},{4,6},{5,7},{6,4},{7,5},{8,10},{9,11},{10,... | collective-permute-start | bytes 1990664 | tf_op jit(solution)/shard_map/ppermute | solution.py:948
  324.6 115.2 %reduce-scatter.3.cloned.1.call-start = ((), (), s32[]{:S(2)}) async-start(), calls=%async_computation.2 | async-start | bytes 1658880 | tf_op jit(solution)/shard_map/reduce_scatter | solution.py:995
  350.9 28.2 %collective-permute-start.59 = (bf16[2,432,384]{2,1,0:T(8,128)(2,1)}, bf16[2,432,384]{2,1,0:T(8,128)(2,1)S(1)}, u32[]{:S(2)}, u32[]{:S(2)}) collective-permute-start(bf16[2,432,384]{2,1,0:T(8,128)(2,1)} %get-tuple-element.293), channel_id=1, source_target_pairs={{0,4},{1,5},{2,6},{3,7},{4,0},{5,1},{6,2},{7,3},{8,12},{9,13},{10,... | collective-permute-start | bytes 1990664 | tf_op jit(solution)/shard_map/ppermute | solution.py:951
  353.0 26.2 %collective-permute-start.58 = (bf16[2,432,384]{2,1,0:T(8,128)(2,1)}, bf16[2,432,384]{2,1,0:T(8,128)(2,1)}, u32[]{:S(2)}, u32[]{:S(2)}) collective-permute-start(bf16[2,432,384]{2,1,0:T(8,128)(2,1)} %get-tuple-element.295), channel_id=1, source_target_pairs={{0,2},{1,3},{2,0},{3,1},{4,6},{5,7},{6,4},{7,5},{8,10},{9,11},{10,... | collective-permute-start | bytes 1990664 | tf_op jit(solution)/shard_map/ppermute | solution.py:948
  356.6 25.0 %collective-permute-start.56 = (bf16[4,96,384]{2,1,0:T(8,128)(2,1)}, bf16[4,96,384]{2,1,0:T(8,128)(2,1)}, u32[]{:S(2)}, u32[]{:S(2)}) collective-permute-start(bf16[4,96,384]{2,1,0:T(8,128)(2,1)} %get-tuple-element.279), channel_id=1, source_target_pairs={{0,4},{1,5},{2,6},{3,7},{4,0},{5,1},{6,2},{7,3},{8,12},{9,13},{10,... | collective-permute-start | bytes 884744 | tf_op jit(solution)/shard_map/ppermute | solution.py:951
  357.3 24.2 %collective-permute-start.57 = (bf16[4,96,384]{2,1,0:T(8,128)(2,1)}, bf16[4,96,384]{2,1,0:T(8,128)(2,1)}, u32[]{:S(2)}, u32[]{:S(2)}) collective-permute-start(bf16[4,96,384]{2,1,0:T(8,128)(2,1)} %get-tuple-element.280), channel_id=1, source_target_pairs={{0,2},{1,3},{2,0},{3,1},{4,6},{5,7},{6,4},{7,5},{8,10},{9,11},{10,... | collective-permute-start | bytes 884744 | tf_op jit(solution)/shard_map/ppermute | solution.py:948
  402.3 25.8 %collective-permute-start.72 = (bf16[4,192,384]{2,1,0:T(8,128)(2,1)}, bf16[4,192,384]{2,1,0:T(8,128)(2,1)S(1)}, u32[]{:S(2)}, u32[]{:S(2)}) collective-permute-start(bf16[4,192,384]{2,1,0:T(8,128)(2,1)} %get-tuple-element.277), channel_id=1, source_target_pairs={{0,4},{1,5},{2,6},{3,7},{4,0},{5,1},{6,2},{7,3},{8,12},{9,13},{10,... | collective-permute-start | bytes 1769480 | tf_op jit(solution)/shard_map/ppermute | solution.py:951
  403.1 25.0 %collective-permute-start.71 = (bf16[4,192,384]{2,1,0:T(8,128)(2,1)S(1)}, bf16[4,192,384]{2,1,0:T(8,128)(2,1)S(1)}, u32[]{:S(2)}, u32[]{:S(2)}) collective-permute-start(bf16[4,192,384]{2,1,0:T(8,128)(2,1)S(1)} %copy-done.14), channel_id=1, source_target_pairs={{0,2},{1,3},{2,0},{3,1},{4,6},{5,7},{6,4},{7,5},{8,10},{9,11},{10,... | collective-permute-start | bytes 1769480 | tf_op jit(solution)/shard_map/ppermute | solution.py:948
  407.7 25.0 %collective-permute-start.76 = (f32[192,384]{1,0:T(8,128)S(1)}, f32[192,384]{1,0:T(8,128)S(1)}, u32[]{:S(2)}, u32[]{:S(2)}) collective-permute-start(f32[192,384]{1,0:T(8,128)S(1)} %fusion.13), channel_id=1, source_target_pairs={{0,1},{1,0},{2,3},{3,2},{4,5},{5,4},{6,7},{7,6},{8,9},{9,8},{10,11... | collective-permute-start | bytes 884744 | tf_op jit(solution)/shard_map/ppermute | solution.py:945
  (103 other events, 1168.5 us)
Sparse Core Ops, SparseCore 0:
  24.0 31.6 all-gather.4
  57.8 39.4 all-gather.6
  324.7 31.9 reduce-scatter.4
  401.1 33.6 reduce-scatter.2

commit v7 on v6

--- a/solution.py
+++ b/solution.py
@@ -1191,7 +1191,7 @@
     cm_near = grid.near(cm_own)
     res, q, k, v, o, p = cross_attn_forward(info, latents, inputs, bias, vec, ca)
     cm_near = after(cm_near, res)
-    cm_far = grid.far(cm_near, MLP_SPLIT)
+    cm_far = after(grid.far(cm_near, MLP_SPLIT), sa_own, sm_own, keeping)
     cm = grid.both_cores(cm_own, cm_near, cm_far)
     sa_own = after(sa_own, cm_far)
     sa_near = grid.near(sa_own)

time: 479 us -> 476 us (level)
  no operation moved by 1% of the time
where the time goes in v7:
time: 476 us; the launch traced here: 472 us
  Pallas kernels  233 us (49%)
  waiting for transfers between devices  100 us (21%)
  starting transfers between devices  59.9 us (13%)
  other arithmetic  38.1 us (8%)
  local copies, waits for them, and re-layouts  25 us (5%)
  between operations  15.2 us (3%)
    pallas_call x11, Pallas kernels, call(): pl.pallas_call(kernel, grid=(grid,), in_specs=in_specs, out_specs=out_spe...  233 us
    ppermute x19, waiting for transfers between devices, swap_y(): return lax.ppermute(value, AX, self.to_y)  40.4 us
    ppermute x19, starting transfers between devices, swap_y(): return lax.ppermute(value, AX, self.to_y)  21.5 us
    ppermute x19, starting transfers between devices, swap_x(): return lax.ppermute(value, AX, self.to_x)  20.6 us
    ppermute x19, waiting for transfers between devices, swap_x(): return lax.ppermute(value, AX, self.to_x)  19.3 us
    add x4, other arithmetic, sides(): sums = (keep[1] + arrived[1] + for_x, keep[2] + arrived[2] + for_y)  11 us
  transfers between devices with their start and end apart: 81, of which 24 were waited for; matrix products, arithmetic and copies ran while one was open for 10% of the time, Pallas kernels for 40%

profile of v7, /device:TPU:0, one launch (start us, length us, event | category | flops | bytes accessed | tf_op | source)
XLA Modules:
  0.0 471.8 jit_solution(16231439915690888597)
XLA Ops:
  12.0 4.1 collective-permute-start.1
  17.0 6.9 %collective-permute-done.1 = bf16[208,384]{1,0:T(8,128)(2,1)S(1)} collective-permute-done((bf16[208,384]{1,0:T(8,128)(2,1)S(1)}, bf16[208,384]{1,0:T(8,128)(2,1)S(1)}, u32[]{:S(2)}, u32[]{:S(2)}) %collective-permute-start.1) | collective-permute-done | bytes 159776 | tf_op jit(solution)/shard_map/ppermute | solution.py:1016
  24.9 8.2 %collective-permute-done.2 = bf16[2,208,384]{2,1,0:T(8,128)(2,1)S(1)} collective-permute-done((bf16[2,208,384]{2,1,0:T(8,128)(2,1)S(1)}, bf16[2,208,384]{2,1,0:T(8,128)(2,1)S(1)}, u32[]{:S(2)}, u32[]{:S(2)}) %collective-permute-start.2) | collective-permute-done | bytes 319520 | tf_op jit(solution)/shard_map/ppermute | solution.py:1021
  37.2 11.0 %collective-permute-done.5.refs_2_ = bf16[4,208,384]{2,1,0:T(8,128)(2,1)S(1)} collective-permute-done((bf16[4,208,384]{2,1,0:T(8,128)(2,1)S(1)}, bf16[4,208,384]{2,1,0:T(8,128)(2,1)S(1)}, u32[]{:S(2)}, u32[]{:S(2)}) %collective-permute-start.5) | collective-permute-done | bytes 639008 | tf_op jit(solution)/shard_map/ppermute | solution.py:951
  51.4 3.9 collective-permute-done.6.refs_3_
  62.8 25.5 %cross_attn_forward.1 = (f32[1024,768]{1,0:T(8,128)}, bf16[8,128,768]{2,1,0:T(8,128)(2,1)}, bf16[8,304,768]{2,1,0:T(8,128)(2,1)}, bf16[8,304,768]{2,1,0:T(8,128)...) custom-call(s32[2]{0:T(128)} %pad_add_fusion.1.info, bf16[8,128,768]{2,1,0:T(8,128)(2,1)} %lat.1, ...), custom_call_target="tpu_custom_call" | custom-call | flops 10066329600 | bytes 31260672 | tf_op jit(solution)/shard_map/cross_attn_forward/pallas_call | solution.py:207
  93.4 3.9 all-gather.7.cloned.1.call-done
  98.9 6.3 %collective-permute-done.15.refs_3_ = bf16[4,192,384]{2,1,0:T(8,128)(2,1)} collective-permute-done((bf16[4,192,384]{2,1,0:T(8,128)(2,1)S(1)}, bf16[4,192,384]{2,1,0:T(8,128)(2,1)}, u32[]{:S(2)}, u32[]{:S(2)}) %collective-permute-start.15) | collective-permute-done | bytes 589856 | tf_op jit(solution)/shard_map/ppermute | solution.py:948
  113.5 22.2 %cross_mlp_forward.1 = (f32[1024,768]{1,0:T(8,128)}, bf16[1024,3072]{1,0:T(8,128)(2,1)}, bf16[1024,3072]{1,0:T(8,128)(2,1)}) custom-call(s32[2]{0:T(128)} %pad_add_fusion.1.info, f32[1024,768]{1,0:T(8,128)} %get-tuple-element.144.res, bf16[1024,768]{1,0:T(8,128)(2,1)} %bitcast.171, f32[1024,1]{1,0:T(8,128)} %copy.51.keep.keep_rows, f32[16,768]{1,0:T(8,128)} %reshape.292.vec, ...), custom_call_target="tpu_custom_call" | custom-call | flops 9663676416 | bytes 29884416 | tf_op jit(solution)/shard_map/cross_mlp_forward/pallas_call | solution.py:207
  141.3 5.4 %collective-permute-done.26.refs_3_ = bf16[4,96,384]{2,1,0:T(8,128)(2,1)S(1)} collective-permute-done((bf16[4,96,384]{2,1,0:T(8,128)(2,1)S(1)}, bf16[4,96,384]{2,1,0:T(8,128)(2,1)S(1)}, u32[]{:S(2)}, u32[]{:S(2)}) %collective-permute-start.26) | collective-permute-done | bytes 294944 | tf_op jit(solution)/shard_map/ppermute | solution.py:948
  152.6 15.4 %self_attn_forward.1 = (f32[1024,768]{1,0:T(8,128)}, bf16[8,128,768]{2,1,0:T(8,128)(2,1)}, bf16[8,128,768]{2,1,0:T(8,128)(2,1)}, bf16[8,128,768]{2,1,0:T(8,128)(...) custom-call(s32[2]{0:T(128)} %pad_add_fusion.1.info, f32[1024,768]{1,0:T(8,128)} %get-tuple-element.152.mid, ...), custom_call_target="tpu_custom_call" | custom-call | flops 5637144576 | bytes 20447232 | tf_op jit(solution)/shard_map/self_attn_forward/pallas_call | solution.py:207
  168.8 7.6 %collective-permute-done.34.refs_5_ = bf16[4,192,384]{2,1,0:T(8,128)(2,1)} collective-permute-done((bf16[4,192,384]{2,1,0:T(8,128)(2,1)S(1)}, bf16[4,192,384]{2,1,0:T(8,128)(2,1)}, u32[]{:S(2)}, u32[]{:S(2)}) %collective-permute-start.34) | collective-permute-done | bytes 589856 | tf_op jit(solution)/shard_map/ppermute | solution.py:951
  183.0 45.3 %self_mlp.1 = (bf16[1024,768]{1,0:T(8,128)(2,1)}, f32[1024,768]{1,0:T(8,128)}, bf16[1024,768]{1,0:T(8,128)(2,1)}, f32[8,768]{1,0:T(8,128)}, bf16[4,4,384,384]{3,...) custom-call(s32[2]{0:T(128)} %pad_add_fusion.1.info, f32[1024,768]{1,0:T(8,128)} %get-tuple-element.162.res, ...), custom_call_target="tpu_custom_call" | custom-call | flops 28991029248 | bytes 29884416 | tf_op jit(solution)/shard_map/self_mlp/pallas_call | solution.py:207
  228.5 19.3 %self_attn_back.1 = (f32[1024,768]{1,0:T(8,128)}, f32[8,768]{1,0:T(8,128)}, bf16[8,128,768]{2,1,0:T(8,128)(2,1)}, bf16[8,128,768]{2,1,0:T(8,128)(2,1)}, bf16[8,1...) custom-call(s32[2]{0:T(128)} %pad_add_fusion.1.info, f32[1024,768]{1,0:T(8,128)} %get-tuple-element.178.total, ...), custom_call_target="tpu_custom_call" | custom-call | flops 6442450944 | bytes 29884416 | tf_op jit(solution)/shard_map/self_attn_back/pallas_call | solution.py:207
  252.0 20.6 %cross_mlp_back.1 = (f32[1024,768]{1,0:T(8,128)}, bf16[1024,768]{1,0:T(8,128)(2,1)}, f32[8,768]{1,0:T(8,128)}, bf16[1024,768]{1,0:T(8,128)(2,1)}, bf16[1024,3072]{1,0:T(8,128)(2,1)}, /*index=5*/bf16[1024,768]{1,0:T(8,128)(2,1)}) custom-call(s32[2]{0:T(128)} %pad_add_fusion.1.info, f32[1024,768]{1,0:T(8,128)} %get-tuple-element.188.up_grad, ...), custom_call_target="tpu_custom_call" | custom-call | flops 9663676416 | bytes 36175872 | tf_op jit(solution)/shard_map/cross_mlp_back/pallas_call | solution.py:207
  279.2 19.1 %cross_mlp_grads.1 = (bf16[4,4,432,384]{3,2,1,0:T(8,128)(2,1)}, bf16[4,4,432,384]{3,2,1,0:T(8,128)(2,1)}) custom-call(s32[2]{0:T(128)} %pad_add_fusion.1.info, bf16[1024,768]{1,0:T(8,128)(2,1)} %get-tuple-element.194.h, bf16[1024,3072]{1,0:T(8,128)(2,1)} %get-tuple-element.195.du, bf16[1024,3072]{1,0:T(8,128)(2,1)} %get-tuple-element.196.e, ...), custom_call_target="tpu_custom_call" | custom-call | flops 10871635968 | bytes 28311552 | tf_op jit(solution)/shard_map/cross_mlp_grads/pallas_call | solution.py:207
  300.9 10.1 %self_attn_grads.1 = (bf16[4,4,192,384]{3,2,1,0:T(8,128)(2,1)}, bf16[4,4,192,384]{3,2,1,0:T(8,128)(2,1)}) custom-call(s32[2]{0:T(128)} %pad_add_fusion.1.info, bf16[8,128,768]{2,1,0:T(8,128)(2,1)} %get-tuple-element.206.refs_0_, bf16[8,128,768]{2,1,0:T(8,128)(2,1)} %get-tuple-element.208.refs_1_, bf16[8,128,768]{2,1,0:T(8,128)(2,1)} %get-tuple-element.210.refs_2_, ...), custom_call_target="tpu_custom_call" | custom-call | flops 4831838208 | bytes 14155776 | tf_op jit(solution)/shard_map/self_attn_grads/pallas_call | solution.py:207
  322.2 22.1 %cross_attn_back_0.1 = (f32[8,768]{1,0:T(8,128)}, f32[1024,768]{1,0:T(8,128)}, f32[8,296,768]{2,1,0:T(8,128)}, bf16[8,128,768]{2,1,0:T(8,128)(2,1)}, bf16[8,128,...) custom-call(s32[2]{0:T(128)} %pad_add_fusion.1.info, ...), custom_call_target="tpu_custom_call" | custom-call | flops 5989466112 | bytes 31260672 | tf_op jit(solution)/shard_map/cross_attn_back_0/pallas_call | solution.py:207
  356.0 20.8 %cross_attn_back_1.1 = (f32[8,768]{1,0:T(8,128)}, f32[1024,768]{1,0:T(8,128)}, f32[8,296,768]{2,1,0:T(8,128)}, bf16[8,128,768]{2,1,0:T(8,128)(2,1)}, bf16[8,128,...) custom-call(s32[2]{0:T(128)} %pad_add_fusion.1.info, ...), custom_call_target="tpu_custom_call", output_to_operand_aliasing={{1}: (21, {}), {2}: (22, {}), {3}: (23, {}), {4}: (24, {}),... | custom-call | flops 5989466112 | bytes 31260672 | tf_op jit(solution)/shard_map/cross_attn_back_1/pallas_call | solution.py:207
  381.4 12.9 %cross_attn_grads.1 = (bf16[4,4,160,384]{3,2,1,0:T(8,128)(2,1)}, bf16[4,4,160,384]{3,2,1,0:T(8,128)(2,1)}) custom-call(s32[2]{0:T(128)} %pad_add_fusion.1.info, bf16[8,128,768]{2,1,0:T(8,128)(2,1)} %get-tuple-element.251.refs_0_, bf16[8,128,768]{2,1,0:T(8,128)(2,1)} %get-tuple-element.252.refs_1_, bf16[8,304,768]{2,1,0:T(8,128)(2,1)} %get-tuple-element.253.refs_2_, ...), custom_call_target="tpu_custom_call" | custom-call | flops 6945767424 | bytes 19070976 | tf_op jit(solution)/shard_map/cross_attn_grads/pallas_call | solution.py:207
  404.5 15.8 %collective-permute-done.63 = bf16[4,80,384]{2,1,0:T(8,128)(2,1)S(1)} collective-permute-done((bf16[4,80,384]{2,1,0:T(8,128)(2,1)S(1)}, bf16[4,80,384]{2,1,0:T(8,128)(2,1)S(1)}, u32[]{:S(2)}, u32[]{:S(2)}) %collective-permute-start.63) | collective-permute-done | bytes 245792 | tf_op jit(solution)/shard_map/ppermute | solution.py:951
  430.6 5.8 %collective-permute-done.73 = bf16[2,192,384]{2,1,0:T(8,128)(2,1)S(1)} collective-permute-done((bf16[2,192,384]{2,1,0:T(8,128)(2,1)S(1)}, bf16[2,192,384]{2,1,0:T(8,128)(2,1)S(1)}, u32[]{:S(2)}, u32[]{:S(2)}) %collective-permute-start.73) | collective-permute-done | bytes 294944 | tf_op jit(solution)/shard_map/ppermute | solution.py:1007
  439.4 4.2 collective-permute-start.74
  455.3 4.9 %collective-permute-done.68 = bf16[160,384]{1,0:T(8,128)(2,1)S(1)} collective-permute-done((bf16[160,384]{1,0:T(8,128)(2,1)S(1)}, bf16[160,384]{1,0:T(8,128)(2,1)S(1)}, u32[]{:S(2)}, u32[]{:S(2)}) %collective-permute-start.68) | collective-permute-done | bytes 122912 | tf_op jit(solution)/shard_map/ppermute | solution.py:1012
  (351 shorter events, 135.5 us)
Async XLA Ops:
  7.2 51.4 %all-gather.5.cloned.1.call-start = ((), (), s32[]{:S(2)}) async-start(), calls=%async_computation.4 | async-start | bytes 1474560 | tf_op jit(solution)/shard_map/all_gather | solution.py:960
  23.9 73.4 %all-gather.7.cloned.1.call-start = ((), (), s32[]{:S(2)}) async-start(), calls=%async_computation.5 | async-start | bytes 2211840 | tf_op jit(solution)/shard_map/all_gather | solution.py:960
  37.0 360.8 %reduce-scatter.5.cloned.1.call-start = ((), (), s32[]{:S(2)}) async-start(), calls=%async_computation.3 | async-start | bytes 1474560 | tf_op jit(solution)/shard_map/reduce_scatter | solution.py:995
  58.7 29.7 %collective-permute-start.14 = (bf16[4,384,384]{2,1,0:T(8,128)(2,1)}, bf16[4,384,384]{2,1,0:T(8,128)(2,1)}, u32[]{:S(2)}, u32[]{:S(2)}) collective-permute-start(bf16[4,384,384]{2,1,0:T(8,128)(2,1)} %bitcast.30.refs_0_), channel_id=1, source_target_pairs={{0,4},{1,5},{2,6},{3,7},{4,0},{5,1},{6,2},{7,3},{8,12},{9,13},{10,... | collective-permute-start | bytes 3538952 | tf_op jit(solution)/shard_map/ppermute | solution.py:951
  60.2 30.7 %collective-permute-start.13 = (bf16[4,384,384]{2,1,0:T(8,128)(2,1)}, bf16[4,384,384]{2,1,0:T(8,128)(2,1)}, u32[]{:S(2)}, u32[]{:S(2)}) collective-permute-start(bf16[4,384,384]{2,1,0:T(8,128)(2,1)} %bitcast.30.refs_0_), channel_id=1, source_target_pairs={{0,2},{1,3},{2,0},{3,1},{4,6},{5,7},{6,4},{7,5},{8,10},{9,11},{10,... | collective-permute-start | bytes 3538952 | tf_op jit(solution)/shard_map/ppermute | solution.py:948
  109.0 38.8 %collective-permute-start.28 = (bf16[4,192,384]{2,1,0:T(8,128)(2,1)S(1)}, bf16[4,192,384]{2,1,0:T(8,128)(2,1)S(1)}, u32[]{:S(2)}, u32[]{:S(2)}) collective-permute-start(bf16[4,192,384]{2,1,0:T(8,128)(2,1)S(1)} %get-tuple-element.153.refs_0_), channel_id=1, source_target_pairs={{0,1},{1,0},{2,3},{3,2},{4,5},{5,4},{6,7},{7,6},{8,9},{9,8},{10,11... | collective-permute-start | bytes 1769480 | tf_op jit(solution)/shard_map/ppermute | solution.py:945
  109.5 26.4 %collective-permute-start.23 = (bf16[4,192,384]{2,1,0:T(8,128)(2,1)S(1)}, bf16[4,192,384]{2,1,0:T(8,128)(2,1)S(1)}, u32[]{:S(2)}, u32[]{:S(2)}) collective-permute-start(bf16[4,192,384]{2,1,0:T(8,128)(2,1)S(1)} %get-tuple-element.153.refs_0_), channel_id=1, source_target_pairs={{0,4},{1,5},{2,6},{3,7},{4,0},{5,1},{6,2},{7,3},{8,12},{9,13},{10,... | collective-permute-start | bytes 1769480 | tf_op jit(solution)/shard_map/ppermute | solution.py:951
  110.2 25.5 %collective-permute-start.22 = (bf16[4,192,384]{2,1,0:T(8,128)(2,1)S(1)}, bf16[4,192,384]{2,1,0:T(8,128)(2,1)S(1)}, u32[]{:S(2)}, u32[]{:S(2)}) collective-permute-start(bf16[4,192,384]{2,1,0:T(8,128)(2,1)S(1)} %get-tuple-element.153.refs_0_), channel_id=1, source_target_pairs={{0,2},{1,3},{2,0},{3,1},{4,6},{5,7},{6,4},{7,5},{8,10},{9,11},{10,... | collective-permute-start | bytes 1769480 | tf_op jit(solution)/shard_map/ppermute | solution.py:948
  112.2 26.2 %collective-permute-start.24 = (bf16[4,192,384]{2,1,0:T(8,128)(2,1)S(1)}, bf16[4,192,384]{2,1,0:T(8,128)(2,1)}, u32[]{:S(2)}, u32[]{:S(2)}) collective-permute-start(bf16[4,192,384]{2,1,0:T(8,128)(2,1)S(1)} %get-tuple-element.164.refs_0_), channel_id=1, source_target_pairs={{0,4},{1,5},{2,6},{3,7},{4,0},{5,1},{6,2},{7,3},{8,12},{9,13},{10,... | collective-permute-start | bytes 1769480 | tf_op jit(solution)/shard_map/ppermute | solution.py:951
  113.0 25.4 %collective-permute-start.25 = (bf16[4,192,384]{2,1,0:T(8,128)(2,1)S(1)}, bf16[4,192,384]{2,1,0:T(8,128)(2,1)}, u32[]{:S(2)}, u32[]{:S(2)}) collective-permute-start(bf16[4,192,384]{2,1,0:T(8,128)(2,1)S(1)} %get-tuple-element.166.refs_1_), channel_id=1, source_target_pairs={{0,2},{1,3},{2,0},{3,1},{4,6},{5,7},{6,4},{7,5},{8,10},{9,11},{10,... | collective-permute-start | bytes 1769480 | tf_op jit(solution)/shard_map/ppermute | solution.py:948
  149.9 27.7 %collective-permute-start.33 = (bf16[4,192,384]{2,1,0:T(8,128)(2,1)S(1)}, bf16[4,192,384]{2,1,0:T(8,128)(2,1)}, u32[]{:S(2)}, u32[]{:S(2)}) collective-permute-start(bf16[4,192,384]{2,1,0:T(8,128)(2,1)S(1)} %get-tuple-element.164.refs_0_), channel_id=1, source_target_pairs={{0,2},{1,3},{2,0},{3,1},{4,6},{5,7},{6,4},{7,5},{8,10},{9,11},{10,... | collective-permute-start | bytes 1769480 | tf_op jit(solution)/shard_map/ppermute | solution.py:948
  152.1 24.4 %collective-permute-start.34 = (bf16[4,192,384]{2,1,0:T(8,128)(2,1)S(1)}, bf16[4,192,384]{2,1,0:T(8,128)(2,1)}, u32[]{:S(2)}, u32[]{:S(2)}) collective-permute-start(bf16[4,192,384]{2,1,0:T(8,128)(2,1)S(1)} %get-tuple-element.166.refs_1_), channel_id=1, source_target_pairs={{0,4},{1,5},{2,6},{3,7},{4,0},{5,1},{6,2},{7,3},{8,12},{9,13},{10,... | collective-permute-start | bytes 1769480 | tf_op jit(solution)/shard_map/ppermute | solution.py:951
  250.3 22.3 %collective-permute-start.46 = (bf16[4,192,384]{2,1,0:T(8,128)(2,1)}, bf16[4,192,384]{2,1,0:T(8,128)(2,1)S(1)}, u32[]{:S(2)}, u32[]{:S(2)}) collective-permute-start(bf16[4,192,384]{2,1,0:T(8,128)(2,1)} %get-tuple-element.279), channel_id=1, source_target_pairs={{0,4},{1,5},{2,6},{3,7},{4,0},{5,1},{6,2},{7,3},{8,12},{9,13},{10,... | collective-permute-start | bytes 1769480 | tf_op jit(solution)/shard_map/ppermute | solution.py:951
  315.8 35.4 %collective-permute-start.55 = (bf16[4,4,192,384]{3,2,1,0:T(8,128)(2,1)}, bf16[4,4,192,384]{3,2,1,0:T(8,128)(2,1)}, u32[]{:S(2)}, u32[]{:S(2)}) collective-permute-start(bf16[4,4,192,384]{3,2,1,0:T(8,128)(2,1)} %get-tuple-element.233), channel_id=1, source_target_pairs={{0,1},{1,0},{2,3},{3,2},{4,5},{5,4},{6,7},{7,6},{8,9},{9,8},{10,11... | collective-permute-start | bytes 7077896 | tf_op jit(solution)/shard_map/ppermute | solution.py:945
  315.9 28.4 %collective-permute-start.53 = (bf16[4,216,384]{2,1,0:T(8,128)(2,1)S(1)}, bf16[4,216,384]{2,1,0:T(8,128)(2,1)}, u32[]{:S(2)}, u32[]{:S(2)}) collective-permute-start(bf16[4,216,384]{2,1,0:T(8,128)(2,1)S(1)} %get-tuple-element.275), channel_id=1, source_target_pairs={{0,4},{1,5},{2,6},{3,7},{4,0},{5,1},{6,2},{7,3},{8,12},{9,13},{10,... | collective-permute-start | bytes 1990664 | tf_op jit(solution)/shard_map/ppermute | solution.py:951
  316.9 27.4 %collective-permute-start.54 = (bf16[4,216,384]{2,1,0:T(8,128)(2,1)}, bf16[4,216,384]{2,1,0:T(8,128)(2,1)}, u32[]{:S(2)}, u32[]{:S(2)}) collective-permute-start(bf16[4,216,384]{2,1,0:T(8,128)(2,1)} %get-tuple-element.276), channel_id=1, source_target_pairs={{0,2},{1,3},{2,0},{3,1},{4,6},{5,7},{6,4},{7,5},{8,10},{9,11},{10,... | collective-permute-start | bytes 1990664 | tf_op jit(solution)/shard_map/ppermute | solution.py:948
  322.2 114.3 %reduce-scatter.3.cloned.1.call-start = ((), (), s32[]{:S(2)}) async-start(), calls=%async_computation.2 | async-start | bytes 1658880 | tf_op jit(solution)/shard_map/reduce_scatter | solution.py:995
  348.5 28.2 %collective-permute-start.59 = (bf16[2,432,384]{2,1,0:T(8,128)(2,1)}, bf16[2,432,384]{2,1,0:T(8,128)(2,1)S(1)}, u32[]{:S(2)}, u32[]{:S(2)}) collective-permute-start(bf16[2,432,384]{2,1,0:T(8,128)(2,1)} %get-tuple-element.297), channel_id=1, source_target_pairs={{0,4},{1,5},{2,6},{3,7},{4,0},{5,1},{6,2},{7,3},{8,12},{9,13},{10,... | collective-permute-start | bytes 1990664 | tf_op jit(solution)/shard_map/ppermute | solution.py:951
  351.0 25.8 %collective-permute-start.58 = (bf16[2,432,384]{2,1,0:T(8,128)(2,1)}, bf16[2,432,384]{2,1,0:T(8,128)(2,1)}, u32[]{:S(2)}, u32[]{:S(2)}) collective-permute-start(bf16[2,432,384]{2,1,0:T(8,128)(2,1)} %get-tuple-element.299), channel_id=1, source_target_pairs={{0,2},{1,3},{2,0},{3,1},{4,6},{5,7},{6,4},{7,5},{8,10},{9,11},{10,... | collective-permute-start | bytes 1990664 | tf_op jit(solution)/shard_map/ppermute | solution.py:948
  353.3 24.9 %collective-permute-start.56 = (bf16[4,96,384]{2,1,0:T(8,128)(2,1)}, bf16[4,96,384]{2,1,0:T(8,128)(2,1)}, u32[]{:S(2)}, u32[]{:S(2)}) collective-permute-start(bf16[4,96,384]{2,1,0:T(8,128)(2,1)} %get-tuple-element.283), channel_id=1, source_target_pairs={{0,4},{1,5},{2,6},{3,7},{4,0},{5,1},{6,2},{7,3},{8,12},{9,13},{10,... | collective-permute-start | bytes 884744 | tf_op jit(solution)/shard_map/ppermute | solution.py:951
  354.2 24.0 %collective-permute-start.57 = (bf16[4,96,384]{2,1,0:T(8,128)(2,1)}, bf16[4,96,384]{2,1,0:T(8,128)(2,1)}, u32[]{:S(2)}, u32[]{:S(2)}) collective-permute-start(bf16[4,96,384]{2,1,0:T(8,128)(2,1)} %get-tuple-element.284), channel_id=1, source_target_pairs={{0,2},{1,3},{2,0},{3,1},{4,6},{5,7},{6,4},{7,5},{8,10},{9,11},{10,... | collective-permute-start | bytes 884744 | tf_op jit(solution)/shard_map/ppermute | solution.py:948
  399.0 27.1 %collective-permute-start.72 = (bf16[4,192,384]{2,1,0:T(8,128)(2,1)}, bf16[4,192,384]{2,1,0:T(8,128)(2,1)S(1)}, u32[]{:S(2)}, u32[]{:S(2)}) collective-permute-start(bf16[4,192,384]{2,1,0:T(8,128)(2,1)} %get-tuple-element.281), channel_id=1, source_target_pairs={{0,4},{1,5},{2,6},{3,7},{4,0},{5,1},{6,2},{7,3},{8,12},{9,13},{10,... | collective-permute-start | bytes 1769480 | tf_op jit(solution)/shard_map/ppermute | solution.py:951
  400.0 26.1 %collective-permute-start.71 = (bf16[4,192,384]{2,1,0:T(8,128)(2,1)S(1)}, bf16[4,192,384]{2,1,0:T(8,128)(2,1)S(1)}, u32[]{:S(2)}, u32[]{:S(2)}) collective-permute-start(bf16[4,192,384]{2,1,0:T(8,128)(2,1)S(1)} %copy-done.14), channel_id=1, source_target_pairs={{0,2},{1,3},{2,0},{3,1},{4,6},{5,7},{6,4},{7,5},{8,10},{9,11},{10,... | collective-permute-start | bytes 1769480 | tf_op jit(solution)/shard_map/ppermute | solution.py:948
  404.4 24.6 %collective-permute-start.76 = (f32[192,384]{1,0:T(8,128)S(1)}, f32[192,384]{1,0:T(8,128)S(1)}, u32[]{:S(2)}, u32[]{:S(2)}) collective-permute-start(f32[192,384]{1,0:T(8,128)S(1)} %fusion.13), channel_id=1, source_target_pairs={{0,1},{1,0},{2,3},{3,2},{4,5},{5,4},{6,7},{7,6},{8,9},{9,8},{10,11... | collective-permute-start | bytes 884744 | tf_op jit(solution)/shard_map/ppermute | solution.py:945
  (101 other events, 1108.2 us)
Sparse Core Ops, SparseCore 0:
  24.0 31.6 all-gather.4
  57.8 39.4 all-gather.6
  322.3 30.9 reduce-scatter.4
  397.9 33.8 reduce-scatter.2
